TPU v7x, 128 devices: a whole 4x4x4 slice. The times are simulated.
128 devices in a mesh: dp: 32 (over y, x, core), rep: 4 (over z).
Axes of the slice: x: 4, y: 4, z: 4, core: 2. Of those that a mesh axis runs over, the one named last changes fastest.
Arguments:
- residual: float32 [2, 32, 1024, 768], P(None, 'dp', 'rep'), may hold values from -6 to 6
- lengths: int32 [2, 32], P(None, 'dp'), may hold values from 256 to 1024, as said below
- norm_gain: bfloat16 [768], P('dp'), may hold values from 0.5 to 1.5
- expand: bfloat16 [768, 3352], P('dp'), may hold values from -0.21875 to 0.21875
- filters: bfloat16 [1792, 4], P('dp'), may hold values from -3 to 3
- offsets: bfloat16 [1792], P('dp'), may hold values from -3 to 3
- gate_gain: bfloat16 [1536], P('dp'), may hold values from 0.5 to 1.5
- contract: bfloat16 [1536, 768], P('dp'), may hold values from -0.15625 to 0.15625
- step_bias: float32 [24], replicated, may hold values from -3 to 0.5
- decay_log: float32 [24], replicated, may hold values from -7 to -1.5
- skip_gain: float32 [24], replicated, may hold values from 0.5 to 1.5
- cotangent: float32 [2, 32, 1024, 768], P(None, 'dp', 'rep'), may hold values from -6 to 6
Outputs:
- mixed: float32 [2, 32, 1024, 768], P(None, 'dp', 'rep')
- residual_grad: float32 [2, 32, 1024, 768], P(None, 'dp', 'rep')
- norm_grad: float32 [768], P('dp')
- expand_grad: float32 [768, 3352], P('dp')
- filters_grad: float32 [1792, 4], P('dp')
- offsets_grad: float32 [1792], P('dp')
- gain_grad: float32 [1536], P('dp')
- contract_grad: float32 [1536, 768], P('dp')
- bias_grad: float32 [24], replicated
- decay_grad: float32 [24], replicated
- skip_grad: float32 [24], replicated
Inputs may be any that keep to these rules, and one draw needn't show every extreme that they name: `lengths`: in each micro-batch one sequence has length 1024.
All inputs are finite; a program needn't handle non-finite values.
Results may differ from a plain program's by a relative error of at most 0.002.
The roundings to bfloat16 on the way count: a program that leaves them out, or rounds other values in their place, can miss the bound.
Values may be sent and summed in bfloat16 or wider, within the bound.
No kernel may reach another device: no remote copies, remote signals or barrier semaphores. Data moves between devices by JAX's collectives and lax.ppermute only.
A program may use at most 192 MiB of HBM per device.

v0:
```python
import jax
import jax.numpy as jnp
from jax import lax
from jax.sharding import PartitionSpec as P

epsilon = 1e-05
precise = lax.Precision.HIGHEST


def passed_along(block, axis, distance):
    devices = range(lax.axis_size(axis))
    route = [(i - distance, i) for i in devices if i - distance in devices]
    return lax.ppermute(block, axis, route)


def carried_in(part, axis, combine, identity, reverse):
    count = lax.axis_size(axis)
    place = lax.axis_index(axis)
    ahead = count - 1 - place if reverse else place
    gathered = jax.tree.map(lambda a: lax.all_gather(a, axis), part)
    state = jax.tree.map(lambda a, e: jnp.zeros_like(a) + jnp.asarray(e, a.dtype), part, identity)

    def one(hop, state):
        source = count - 1 - hop if reverse else hop
        return combine(
            state, jax.tree.map(lambda a: lax.dynamic_index_in_dim(a, source, 0, False), gathered)
        )

    return lax.fori_loop(0, ahead, one, state)


def chain_join(earlier, later):
    return (earlier[0] * later[0], later[0][..., None, None] * earlier[1] + later[1])


def body(
    residual,
    lengths,
    norm_gain,
    expand,
    filters,
    offsets,
    gate_gain,
    contract,
    step_bias,
    decay_log,
    skip_gain,
    cotangent,
):
    micro = residual.shape[0]
    slots = residual.shape[1]
    length = residual.shape[2]
    width = residual.shape[3]
    heads = step_bias.shape[0]
    inner_width = contract.shape[0] * lax.axis_size("dp")
    head_size = inner_width // heads
    state_size = (expand.shape[1] - 2 * inner_width - heads) // 2
    filter_width = inner_width + 2 * state_size
    kernel = filters.shape[1]
    rim = kernel - 1
    position = lax.axis_index("rep") * length + jnp.arange(length, dtype=jnp.int32)
    order = jnp.arange(length)
    causal = (order[:, None] >= order[None, :])[None, :, :, None]

    def prepare(padded, step_raw, filters_full, offsets_full, step_shift, decay_rate):
        filtered = offsets_full
        for tap in range(kernel):
            filtered = filtered + filters_full[:, tap] * padded[:, tap : tap + length]
        activated = jax.nn.silu(filtered)
        values = activated[..., :inner_width].reshape(slots, length, heads, head_size)
        writer = activated[..., inner_width : inner_width + state_size]
        reader = activated[..., inner_width + state_size :]
        step = jax.nn.softplus(step_raw + step_shift)
        cumulative = jnp.cumsum(-step * jnp.exp(decay_rate), axis=1)
        return (values, step, cumulative, writer, reader)

    def local_state(values, step, cumulative, writer):
        ends = jnp.exp(cumulative[:, -1][:, None, :] - cumulative) * step
        return jnp.einsum("ash,ashp,asn->ahpn", ends, values, writer, precision=precise)

    def mix_local(values, step, cumulative, writer, reader, state_in, skip_weight, gate):
        gaps = cumulative[:, :, None, :] - cumulative[:, None, :, :]
        decay = jnp.where(causal, jnp.exp(jnp.where(causal, gaps, 0.0)), 0.0)
        scores = jnp.einsum("atn,asn->ats", reader, writer, precision=precise)
        weights = scores[..., None] * decay * step[:, None, :, :]
        inner = jnp.einsum("atsh,ashp->athp", weights, values, precision=precise)
        carried = (
            jnp.einsum("atn,ahpn->athp", reader, state_in, precision=precise)
            * jnp.exp(cumulative)[..., None]
        )
        outputs = inner + carried + skip_weight[:, None] * values
        gated = outputs.reshape(slots, length, inner_width) * jax.nn.silu(gate)
        state_out = jnp.exp(cumulative[:, -1])[..., None, None] * state_in + local_state(
            values, step, cumulative, writer
        )
        return (gated, state_out)

    proj_width = expand.shape[1]
    sum_norm = jnp.zeros((width,), jnp.float32)
    sum_expand = jnp.zeros((width, proj_width), jnp.float32)
    sum_filters = jnp.zeros((filter_width, kernel), jnp.float32)
    sum_offsets = jnp.zeros((filter_width,), jnp.float32)
    sum_gain = jnp.zeros((inner_width,), jnp.float32)
    sum_contract = jnp.zeros((inner_width, width), jnp.float32)
    sum_bias = jnp.zeros((heads,), jnp.float32)
    sum_decay = jnp.zeros((heads,), jnp.float32)
    sum_skip = jnp.zeros((heads,), jnp.float32)
    mixed_list = []
    grad_list = []
    for index in range(micro):
        forward_set = (
            lax.all_gather(norm_gain, "dp", axis=0, tiled=True),
            lax.all_gather(expand, "dp", axis=0, tiled=True),
            lax.all_gather(filters, "dp", axis=0, tiled=True),
            lax.all_gather(offsets, "dp", axis=0, tiled=True),
            lax.all_gather(gate_gain, "dp", axis=0, tiled=True),
            lax.all_gather(contract, "dp", axis=0, tiled=True),
        )
        gain_one = forward_set[0].astype(jnp.float32)
        expand_full = forward_set[1]
        filters_full = forward_set[2].astype(jnp.float32)
        offsets_full = forward_set[3].astype(jnp.float32)
        gain_two = forward_set[4].astype(jnp.float32)
        contract_full = forward_set[5]
        source = residual[index]
        mask = (position[None, :] < lengths[index][:, None]).astype(jnp.float32)[..., None]
        scale_one = lax.rsqrt(jnp.mean(source * source, axis=-1, keepdims=True) + epsilon)
        unit_one = source * scale_one
        normed = (unit_one * gain_one).astype(jnp.bfloat16)
        projected = jnp.einsum(
            "ald,dp->alp", normed, expand_full, preferred_element_type=jnp.float32
        )
        gate = projected[..., :inner_width]
        signal = projected[..., inner_width : inner_width + filter_width]
        step_raw = projected[..., inner_width + filter_width :]
        before = passed_along(signal[:, length - rim :], "rep", 1)
        padded = jnp.concatenate([before, signal], axis=1)
        prepared, prepare_pull = jax.vjp(
            prepare, padded, step_raw, filters_full, offsets_full, step_bias, decay_log
        )
        values, step, cumulative, writer, reader = prepared
        own_state = local_state(values, step, cumulative, writer)
        decay_total = jnp.exp(cumulative[:, -1])
        identity = (jnp.ones_like(decay_total), jnp.zeros_like(own_state))
        _, state_in = carried_in((decay_total, own_state), "rep", chain_join, identity, False)
        mixture, mixture_pull = jax.vjp(
            mix_local, values, step, cumulative, writer, reader, state_in, skip_gain, gate
        )
        gated = mixture[0]
        scale_two = lax.rsqrt(jnp.mean(gated * gated, axis=-1, keepdims=True) + epsilon)
        unit_two = gated * scale_two
        normed_out = (unit_two * gain_two).astype(jnp.bfloat16)
        branch = jnp.einsum(
            "alk,kd->ald", normed_out, contract_full, preferred_element_type=jnp.float32
        )
        mixed_list.append(source + mask * branch)
        backward_set = (
            lax.all_gather(norm_gain, "dp", axis=0, tiled=True),
            lax.all_gather(expand, "dp", axis=0, tiled=True),
            lax.all_gather(filters, "dp", axis=0, tiled=True),
            lax.all_gather(offsets, "dp", axis=0, tiled=True),
            lax.all_gather(gate_gain, "dp", axis=0, tiled=True),
            lax.all_gather(contract, "dp", axis=0, tiled=True),
        )
        expand_back = backward_set[1]
        contract_back = backward_set[5]
        upstream = cotangent[index]
        branch_grad = (mask * upstream).astype(jnp.bfloat16)
        sum_contract = sum_contract + jnp.einsum(
            "alk,ald->kd", normed_out, branch_grad, preferred_element_type=jnp.float32
        )
        outcome_grad = jnp.einsum(
            "ald,kd->alk", branch_grad, contract_back, preferred_element_type=jnp.float32
        )
        sum_gain = sum_gain + jnp.sum(outcome_grad * unit_two, axis=(0, 1))
        scaled = outcome_grad * gain_two
        gated_grad = scale_two * (
            scaled - unit_two * jnp.mean(scaled * unit_two, axis=-1, keepdims=True)
        )
        heads_grad = (gated_grad * jax.nn.silu(gate)).reshape(slots, length, heads, head_size)
        state_local = jnp.einsum(
            "ath,athp,atn->ahpn", jnp.exp(cumulative), heads_grad, reader, precision=precise
        )
        _, state_after = carried_in((decay_total, state_local), "rep", chain_join, identity, True)
        (
            values_grad,
            step_grad,
            cumulative_grad,
            writer_grad,
            reader_grad,
            _,
            skip_part,
            gate_grad,
        ) = mixture_pull((gated_grad, state_after))
        padded_grad, raw_grad, filters_part, offsets_part, bias_part, decay_part = prepare_pull(
            (values_grad, step_grad, cumulative_grad, writer_grad, reader_grad)
        )
        returned = passed_along(padded_grad[:, :rim], "rep", -1)
        signal_grad = padded_grad[:, rim:] + jnp.concatenate(
            [jnp.zeros((slots, length - rim, filter_width), jnp.float32), returned], axis=1
        )
        projected_grad = jnp.concatenate([gate_grad, signal_grad, raw_grad], axis=-1).astype(
            jnp.bfloat16
        )
        sum_expand = sum_expand + jnp.einsum(
            "ald,alp->dp", normed, projected_grad, preferred_element_type=jnp.float32
        )
        normed_grad = jnp.einsum(
            "alp,dp->ald", projected_grad, expand_back, preferred_element_type=jnp.float32
        )
        sum_norm = sum_norm + jnp.sum(normed_grad * unit_one, axis=(0, 1))
        scaled_one = normed_grad * gain_one
        grad_list.append(
            upstream
            + scale_one
            * (scaled_one - unit_one * jnp.mean(scaled_one * unit_one, axis=-1, keepdims=True))
        )
        sum_filters = sum_filters + filters_part
        sum_offsets = sum_offsets + offsets_part
        sum_bias = sum_bias + bias_part
        sum_decay = sum_decay + decay_part
        sum_skip = sum_skip + skip_part
    norm_part, expand_part, filter_part, offset_part, gain_part, contract_part = (
        lax.psum_scatter(sum_norm, "dp", scatter_dimension=0, tiled=True),
        lax.psum_scatter(sum_expand, "dp", scatter_dimension=0, tiled=True),
        lax.psum_scatter(sum_filters, "dp", scatter_dimension=0, tiled=True),
        lax.psum_scatter(sum_offsets, "dp", scatter_dimension=0, tiled=True),
        lax.psum_scatter(sum_gain, "dp", scatter_dimension=0, tiled=True),
        lax.psum_scatter(sum_contract, "dp", scatter_dimension=0, tiled=True),
    )
    norm_grad, expand_grad, filters_grad, offsets_grad, gain_grad, contract_grad = lax.psum(
        (norm_part, expand_part, filter_part, offset_part, gain_part, contract_part), "rep"
    )
    bias_grad, decay_grad, skip_grad = lax.psum((sum_bias, sum_decay, sum_skip), ("dp", "rep"))
    mixed = jnp.stack(mixed_list)
    residual_grad = jnp.stack(grad_list)
    return (
        mixed,
        residual_grad,
        norm_grad,
        expand_grad,
        filters_grad,
        offsets_grad,
        gain_grad,
        contract_grad,
        bias_grad,
        decay_grad,
        skip_grad,
    )


def solution(mesh):
    in_specs = (
        P(None, "dp", "rep", None),
        P(None, "dp"),
        P("dp"),
        P("dp", None),
        P("dp", None),
        P("dp"),
        P("dp"),
        P("dp", None),
        P(),
        P(),
        P(),
        P(None, "dp", "rep", None),
    )
    out_specs = (
        P(None, "dp", "rep", None),
        P(None, "dp", "rep", None),
        P("dp"),
        P("dp", None),
        P("dp", None),
        P("dp"),
        P("dp"),
        P("dp", None),
        P(),
        P(),
        P(),
    )
    return jax.shard_map(body, mesh=mesh, in_specs=in_specs, out_specs=out_specs, check_vma=False)
```

profile of v0, /device:TPU:0, one launch (start us, length us, event | category | flops | bytes accessed | tf_op | source)
XLA Modules:
  0.0 786.4 jit_solution(16827388014846332858)
XLA Ops:
  8.7 24.5 %all-gather.4 = bf16[32,56,4]{1,2,0:T(4,128)(2,1)S(1)} all-gather(bf16[1,56,4]{1,2,0:T(4,128)(2,1)} %bitcast.663), channel_id=1, replica_groups=mesh['dp'=32,'rep'=4] {'dp'}, dimensions={0}, use_global_device_ids=true | all-gather | bytes 14784 | tf_op jit(solution)/shard_map/all_gather | solution.py:114
  40.5 126.9 %all-reduce.40 = (bf16[768]{0:T(1024)(128)(2,1)S(1)}, bf16[1792]{0:T(1024)(128)(2,1)S(1)}, bf16[1536]{0:T(1024)(128)(2,1)}) all-reduce(bf16[768]{0:T(1024)(128)(2,1)S(1)} %dynamic-update-slice.1, bf16[1792]{0:T(1024)(128)(2,1)S(1)} %dynamic-update-slice, bf16[1536]{0:T(1024)(128)(2,1)S(1)} %dynamic-update-slice.2), channel_id=1, replica_groups=mesh['dp'=32,'rep'=4] {'dp'}, use_global_device_ids=true, to_apply=%add.29 | all-reduce | flops 4096 | bytes 16384
  170.1 4.3 convolution_bitcast_fusion
  195.8 8.6 %fusion.47 = (f32[1,256,1792]{2,1,0:T(8,128)S(1)}, f32[1,256,1792]{2,1,0:T(8,128)}, f32[1,256,1792]{2,1,0:T(8,128)S(1)}, f32[1,256,1792]{2,1,0:T(8,128)}) fusion(f32[1,256,1792]{2,1,0:T(8,128)} %slice.190, f32[1792]{0:T(1024)S(1)} %copy-done.92, f32[1,3,1792]{2,1,0:T(4,128)S(1)} %copy.333, f32[1792]{0:T(1024)S(1)} %copy-done.94, f32[1792]{0:T(1024)S(1)} %copy-done.96, ...), kind=kLoop, calls=%fused_computation.96 | loop fusion | flops 13762560 | bytes 11088896 | tf_op jit(solution)/shard_map/jvp(jit(silu))/mul | solution.py:69
  233.0 8.5 %all_gather.73 = f32[4,1,24]{2,1,0:T(1,128)S(1)} all-gather(f32[1,1,24]{2,1,0:T(1,128)} %get-tuple-element.562), channel_id=1, replica_groups=mesh['dp'=32,'rep'=4] {'rep'}, dimensions={0}, use_global_device_ids=true | all-gather | bytes 480 | tf_op jit(solution)/shard_map/all_gather | solution.py:20
  241.5 7.7 all_gather.68
  255.4 8.6 %fusion.55 = f32[1,256,24,64]{1,3,2,0:T(8,128)} fusion(f32[1,256,24,64]{1,3,2,0:T(8,128)S(1)} %bitcast.618, f32[256,24,64]{0,2,1:T(8,128)S(1)} %fusion.120, f32[256,24,64]{0,2,1:T(8,128)S(1)} %bitcast.617, f32[256,24]{0,1:T(8,128)S(1)} %copy.339, f32[256,24]{0,1:T(8,128)S(1)} %copy.337, f32[256,256]{1,0:T(8,128)S(1)} %fusion.180, ...), kind=kOutput, calls=%fused_computation.113 | convolution fusion | flops 1217396736 | bytes 6692960 | tf_op jit(solution)/shard_map/jvp(atsh,ashp->athp)/dot_general | solution.py:86
  267.0 21.9 %all-gather.18.cloned.1.call-done = f32[96,64,128]{2,1,0:T(8,128)} async-done(((f32[24,64,128]{2,1,0:T(8,128)}), f32[96,64,128]{2,1,0:T(8,128)}) %all-gather.18.cloned.1.call-update) | async-done | bytes 3145744 | tf_op jit(solution)/shard_map/all_gather | solution.py:20
  291.5 8.6 %fusion.54 = f32[1,256,24,64]{1,3,2,0:T(8,128)} fusion(f32[1,256,24,64]{1,3,2,0:T(8,128)S(1)} %bitcast.610, f32[256,24,64]{0,2,1:T(8,128)S(1)} %fusion.117, f32[256,24,64]{0,2,1:T(8,128)S(1)} %bitcast.611, f32[256,24]{0,1:T(8,128)S(1)} %copy-done.126, f32[256,24]{0,1:T(8,128)S(1)} %copy-done.129, f32[256,256]{1,0:T(8,128)S(1)} %copy-done.76, ...), kind=kOutput, calls=%fused_computation.111 | convolution fusion | flops 1217396736 | bytes 6692960 | tf_op jit(solution)/shard_map/jvp(atsh,ashp->athp)/dot_general | solution.py:86
  311.9 5.6 multiply_reduce_fusion.10
  358.7 6.8 fusion.228
  365.5 13.6 %fusion.9 = (f32[256,24]{0,1:T(8,128)}, f32[256,24]{0,1:T(8,128)}, f32[256,24]{0,1:T(8,128)}, f32[256,256]{1,0:T(8,128)}, f32[256,256]{1,0:T(8,128)}, /*index=5*...) fusion(f32[256,256]{1,0:T(8,128)S(1)} %copy-done.80, f32[256,24]{0,1:T(8,128)S(1)} %copy-done.136, ...), kind=kOutput, calls=%fused_computation.33 | convolution fusion | flops 1254977536 | bytes 10797056 | tf_op jit(solution)/shard_map/transpose(jvp(atsh,ashp->athp))/dot_general | solution.py:86
  405.6 6.4 while.54
  416.9 6.0 while.55
  428.1 8.8 %bitcast_add_fusion.5 = f32[1,256,24,64]{1,3,2,0:T(8,128)} fusion(f32[24,64,256]{2,1,0:T(8,128)} %get-tuple-element.586, f32[256,24,64]{0,2,1:T(8,128)} %bitcast.629, f32[24,64,256]{2,1,0:T(8,128)} %bitcast.628, f32[256,24]{0,1:T(8,128)S(1)} %copy-done.134, f32[256,24]{0,1:T(8,128)S(1)} %copy-done.137, f32[256,256]{1,0:T(8,128)S(1)} %copy-done.81, ...), kind=kOutput, calls=%fused_computation.109 | convolution fusion | flops 1217396736 | bytes 6692960 | tf_op jit(solution)/shard_map/transpose(jvp(atsh,ashp->athp))/dot_general | solution.py:86
  440.3 9.2 %bitcast_add_fusion.4 = f32[1,256,24,64]{1,3,2,0:T(8,128)} fusion(f32[24,64,256]{2,1,0:T(8,128)} %get-tuple-element.588, f32[256,24,64]{0,2,1:T(8,128)} %bitcast.625, f32[24,64,256]{2,1,0:T(8,128)} %bitcast.624, f32[256,24]{0,1:T(8,128)S(1)} %copy-done.128, f32[256,24]{0,1:T(8,128)S(1)} %copy-done.131, f32[256,256]{1,0:T(8,128)S(1)} %copy-done.78, ...), kind=kOutput, calls=%fused_computation.108 | convolution fusion | flops 1217396736 | bytes 6692960 | tf_op jit(solution)/shard_map/transpose(jvp(atsh,ashp->athp))/dot_general | solution.py:86
  464.4 5.1 multiply_reduce_fusion.8
  490.3 5.2 pad_add_fusion
  506.0 5.8 convolution_add_fusion
  522.0 68.8 %all-reduce.36 = (f32[24]{0:T(128)}, f32[24]{0:T(128)}, f32[24]{0:T(128)}) all-reduce(f32[24]{0:T(128)} %add.372, f32[24]{0:T(128)} %add_multiply_fusion, f32[24]{0:T(128)} %add.374), channel_id=1, replica_groups=mesh['dp'=32,'rep'=4] {'dp','rep'}, use_global_device_ids=true, to_apply=%region_66.68 | all-reduce | flops 72 | bytes 576 | tf_op jit(solution)/shard_map/psum | solution.py:234
  594.2 4.6 fusion.132
  601.4 125.7 %all-reduce.37 = (f32[768]{0:T(1024)S(1)}, f32[1792,4]{0,1:T(4,128)S(1)}, f32[1792]{0:T(1024)S(1)}, f32[1536]{0:T(1024)S(1)}) all-reduce(f32[768]{0:T(1024)S(1)} %add.366, f32[1792,4]{0,1:T(4,128)} %add_add_fusion, f32[1792]{0:T(1024)} %add.369, f32[1536]{0:T(1024)} %add.370), channel_id=6, replica_groups=mesh['dp'=32,'rep'=4] {'dp'}, use_global_device_ids=true, to_apply=%region_40.42.clone | all-reduce | flops 11264 | bytes 90112
  727.4 9.9 %all-reduce.38 = (f32[24]{0:T(128)}, f32[56,4]{0,1:T(4,128)}, f32[56]{0:T(128)}, f32[48]{0:T(128)}) all-reduce(f32[24]{0:T(128)S(1)} %dynamic-slice.4, f32[56,4]{0,1:T(4,128)S(1)} %constant_dynamic-slice_fusion, f32[56]{0:T(128)S(1)} %dynamic-slice.10, f32[48]{0:T(128)S(1)} %dynamic-slice.12), channel_id=1, replica_groups=mesh['dp'=32,'rep'=4] {'rep'}, use_global_device_ids=true, to_apply=%region_41.43 | all-reduce | flops 352 | bytes 2816 | tf_op jit(solution)/shard_map/psum | solution.py:231
  742.0 34.1 %all-reduce.43.cloned.1.call-done = (f32[24,3352]{1,0:T(8,128)}, f32[48,768]{1,0:T(8,128)}) async-done(((f32[24,3352]{1,0:T(8,128)}, f32[48,768]{1,0:T(8,128)}), (f32[24,3352]{1,0:T(8,128)}, f32[48,768]{1,0:T(8,128)})) %all-reduce.43.cloned.1.call-update) | async-done | bytes 469264 | tf_op jit(solution)/shard_map/psum | solution.py:231
  (545 shorter events, 243.0 us)
Async XLA Ops:
  7.2 162.9 %copy-start.1 = (f32[2,1,256,768]{3,2,1,0:T(8,128)S(1)}, f32[2,1,256,768]{3,2,1,0:T(8,128)}, u32[]{:S(2)}) copy-start(f32[2,1,256,768]{3,2,1,0:T(8,128)} %param.21) | copy-start | bytes 4718596
  7.2 162.4 %all-gather.12.cloned.1.call-start = ((), (), s32[]{:S(2)}) async-start(), calls=%async_computation.2 | async-start | bytes 5474304 | tf_op jit(solution)/shard_map/all_gather | solution.py:113
  7.9 217.0 %all-gather.14.cloned.1.call-start = ((), (), s32[]{:S(2)}) async-start(), calls=%async_computation.3 | async-start | bytes 2433024 | tf_op jit(solution)/shard_map/all_gather | solution.py:117
  8.7 244.0 %all-gather.16.cloned.1.call-start = ((), (), s32[]{:S(2)}) async-start(), calls=%async_computation.5 | async-start | bytes 3932160 | tf_op jit(solution)/shard_map/all_gather | solution.py:20
  34.0 161.7 %copy-start.90 = (f32[1792]{0:T(1024)}, f32[1792]{0:T(1024)S(1)}, u32[]{:S(2)}) copy-start(f32[1792]{0:T(1024)S(1)} %get-tuple-element.453) | copy-start | bytes 21508
  38.0 146.1 %copy-start.145 = (f32[24]{0:T(128)}, f32[24]{0:T(128)S(1)}, u32[]{:S(2)}) copy-start(f32[24]{0:T(128)S(1)} %exp.110) | copy-start | bytes 292
  174.5 21.2 %collective-permute-start.1 = (f32[1,3,1792]{2,0,1:T(1,128)S(1)}, f32[1,3,1792]{2,0,1:T(1,128)S(1)}, u32[]{:S(2)}, u32[]{:S(2)}) collective-permute-start(f32[1,3,1792]{2,0,1:T(1,128)S(1)} %copy.346), channel_id=1, source_target_pairs={{0,1},{1,2},{2,3},{4,5},{5,6},{6,7},{8,9},{9,10},{10,11},{12,13},{... | collective-permute-start | bytes 64520 | tf_op jit(solution)/shard_map/ppermute | solution.py:13
  180.2 15.5 %collective-permute-start = (f32[1,3,1792]{2,0,1:T(1,128)S(1)}, f32[1,3,1792]{2,0,1:T(1,128)S(1)}, u32[]{:S(2)}, u32[]{:S(2)}) collective-permute-start(f32[1,3,1792]{2,0,1:T(1,128)S(1)} %copy.332), channel_id=1, source_target_pairs={{0,1},{1,2},{2,3},{4,5},{5,6},{6,7},{8,9},{9,10},{10,11},{12,13},{... | collective-permute-start | bytes 64520 | tf_op jit(solution)/shard_map/ppermute | solution.py:13
  212.3 76.6 %all-gather.18.cloned.1.call-start = ((), (), s32[]{:S(2)}) async-start(), calls=%async_computation.6 | async-start | bytes 3932160 | tf_op jit(solution)/shard_map/all_gather | solution.py:20
  217.3 141.3 %copy-start.3 = (f32[1,256,1536]{1,2,0:T(8,128)}, f32[1,256,1536]{1,2,0:T(8,128)S(1)}, u32[]{:S(2)}) copy-start(f32[1,256,1536]{1,2,0:T(8,128)S(1)} %copy.348) | copy-start | bytes 4718596
  220.9 184.6 %all-gather.20.cloned.1.call-start = ((), (), s32[]{:S(2)}) async-start(), calls=%async_computation.7 | async-start | bytes 3932160 | tf_op jit(solution)/shard_map/all_gather | solution.py:20
  324.2 92.6 %all-gather.22.cloned.1.call-start = ((), (), s32[]{:S(2)}) async-start(), calls=%async_computation.8 | async-start | bytes 3932160 | tf_op jit(solution)/shard_map/all_gather | solution.py:20
  331.0 407.6 %reduce-scatter.6.cloned.1.call-start = ((), (), s32[]{:S(2)}) async-start(), calls=%async_computation.4 | async-start | bytes 4866048 | tf_op jit(solution)/shard_map/reduce_scatter | solution.py:229
  405.4 333.3 %reduce-scatter.8.cloned.1.call-start = ((), (), s32[]{:S(2)}) async-start(), calls=%async_computation.9 | async-start | bytes 10948608
  481.6 18.0 %collective-permute-start.2 = (f32[1,3,1792]{2,0,1:T(1,128)}, f32[1,3,1792]{2,0,1:T(1,128)}, u32[]{:S(2)}, u32[]{:S(2)}) collective-permute-start(f32[1,3,1792]{2,0,1:T(1,128)} %copy.370), channel_id=1, source_target_pairs={{1,0},{2,1},{3,2},{5,4},{6,5},{7,6},{9,8},{10,9},{11,10},{13,12},{... | collective-permute-start | bytes 64520 | tf_op jit(solution)/shard_map/ppermute | solution.py:13
  482.9 17.5 %collective-permute-start.3 = (f32[1,3,1792]{2,0,1:T(1,128)}, f32[1,3,1792]{2,0,1:T(1,128)}, u32[]{:S(2)}, u32[]{:S(2)}) collective-permute-start(f32[1,3,1792]{2,0,1:T(1,128)} %copy.389), channel_id=1, source_target_pairs={{1,0},{2,1},{3,2},{5,4},{6,5},{7,6},{9,8},{10,9},{11,10},{13,12},{... | collective-permute-start | bytes 64520 | tf_op jit(solution)/shard_map/ppermute | solution.py:13
  511.8 264.3 %all-reduce.43.cloned.1.call-start = ((), (), s32[]{:S(2)}) async-start(), calls=%async_computation.10 | async-start | bytes 958464 | tf_op jit(solution)/shard_map/psum | solution.py:231
  518.0 80.8 %slice-start = ((s8[5308416]{0:T(1024)(128)(4,1)}), s8[1114112]{0:T(1024)(128)(4,1)S(1)}, s32[]{:S(2)}) async-start(s8[5308416]{0:T(1024)(128)(4,1)} %bitcast.607), calls=%async_computation.11 | async-start | bytes 2228224
  519.0 73.8 %copy-start.124 = (f32[1792]{0:T(1024)S(1)}, f32[1792]{0:T(1024)}, u32[]{:S(2)}) copy-start(f32[1792]{0:T(1024)} %get-tuple-element.444) | copy-start | bytes 21508
  519.0 73.8 %copy-start.122 = (f32[1792]{0:T(1024)S(1)}, f32[1792]{0:T(1024)}, u32[]{:S(2)}) copy-start(f32[1792]{0:T(1024)} %get-tuple-element.428) | copy-start | bytes 21508
  519.0 73.9 %copy-start.121 = (f32[1792]{0:T(1024)S(1)}, f32[1792]{0:T(1024)}, u32[]{:S(2)}) copy-start(f32[1792]{0:T(1024)} %get-tuple-element.429) | copy-start | bytes 21508
  519.0 73.9 %copy-start.120 = (f32[1792]{0:T(1024)S(1)}, f32[1792]{0:T(1024)}, u32[]{:S(2)}) copy-start(f32[1792]{0:T(1024)} %get-tuple-element.443) | copy-start | bytes 21508
  519.0 73.9 %copy-start.118 = (f32[1792]{0:T(1024)S(1)}, f32[1792]{0:T(1024)}, u32[]{:S(2)}) copy-start(f32[1792]{0:T(1024)} %get-tuple-element.442) | copy-start | bytes 21508
  519.0 73.9 %copy-start.119 = (f32[1792]{0:T(1024)S(1)}, f32[1792]{0:T(1024)}, u32[]{:S(2)}) copy-start(f32[1792]{0:T(1024)} %get-tuple-element.441) | copy-start | bytes 21508
  (147 other events, 722.8 us)
Sparse Core Ops, SparseCore 0:
  10.4 49.8 all-gather.11
  62.5 43.4 all-gather.13
  212.4 34.5 all-gather.15
  249.1 39.7 all-gather.17
  324.4 42.7 all-gather.19
  368.6 39.7 all-gather.21
  412.2 83.5 reduce-scatter.5
  511.9 101.4 reduce-scatter.7
  738.8 37.2 all-reduce.42
where the time goes:
time: 797 us; the launch traced here: 786 us
  blocking collectives  372 us (47%)
  matrix products  140 us (18%)
  local copies, waits for them, and re-layouts  97 us (12%)
  other arithmetic  87.6 us (11%)
  waiting for transfers between devices  57.6 us (7%)
  between operations  20.2 us (3%)
  starting transfers between devices  11.3 us (1%)
    unnamed x2, blocking collectives  253 us
    psum x1, blocking collectives, body(): lax.psum((sum_bias, sum_decay, sum_skip), ('dp', 'rep'))  68.8 us
    dot_general x6, matrix products, mix_local(): inner = jnp.einsum('atsh,ashp->athp', weights, values, precision=precise)  55.5 us
    psum x1, waiting for transfers between devices, body(): lax.psum((norm_part, expand_part, filter_part, offset_part, gain_part, co...  34.1 us
    all_gather x1, blocking collectives, body(): lax.all_gather(filters, 'dp', axis=0, tiled=True)  24.5 us
    dot_general x6, matrix products, local_state(): jnp.einsum('ash,ashp,asn->ahpn', ends, values, writer, precision=precise)  22.2 us
    all_gather x4, waiting for transfers between devices, carried_in(): gathered = jax.tree.map(lambda a: lax.all_gather(a, axis), part)  21.9 us
    unnamed x329, local copies, waits for them, and re-layouts  20 us
  transfers between devices with their start and end apart: 13, of which 2 were waited for; matrix products, arithmetic and copies ran while one was open for 35% of the time, Pallas kernels for 0%

commit v1 on v0

v1 whole, which is shorter than its diff:
```python
import functools

import jax
import jax.numpy as jnp
import numpy as np
from jax import lax
from jax.experimental import pallas as pl
from jax.experimental.pallas import tpu as pltpu
from jax.sharding import Mesh
from jax.sharding import PartitionSpec as P

EPS = 1e-05
DP = ("y", "x", "core")
F32 = jnp.float32
BF16 = jnp.bfloat16
HIGHEST = lax.Precision.HIGHEST
NN = (((1,), (0,)), ((), ()))
NT = (((1,), (1,)), ((), ()))
TN = (((0,), (0,)), ((), ()))
VMEM_LIMIT = 56 * 1024 * 1024


def shifted(x, axis, shift):
    n = lax.axis_size(axis)
    return lax.ppermute(x, axis, [(i, (i + shift) % n) for i in range(n)])


def in_order(rel, axis):
    n = lax.axis_size(axis)
    i = lax.axis_index(axis)
    twice = jnp.stack(rel + rel)
    return lax.dynamic_slice_in_dim(twice, (n - i) % n, n, 0)


def halves(x):
    h = x.shape[0] // 2
    return x[:h], x[h:]


def gather(x, axis, ring=False):
    n = lax.axis_size(axis)
    if n == 1:
        return x[None]
    if n == 4 and ring:
        left = shifted(x, axis, 1)
        right = shifted(x, axis, -1)
        far = jnp.concatenate(
            [shifted(halves(left)[0], axis, 1), shifted(halves(right)[1], axis, -1)], axis=0
        )
        return in_order([x, right, far, left], axis)
    return in_order([x] + [shifted(x, axis, -k) for k in range(1, n)], axis)


def block_at(x, index, dim):
    return lax.dynamic_index_in_dim(x, index, dim, keepdims=False)


def scatter_sum(x, axis, dim=0):
    n = lax.axis_size(axis)
    if n == 1:
        return block_at(x, 0, dim)
    i = lax.axis_index(axis)
    total = block_at(x, i, dim)
    for k in range(1, n):
        total = total + shifted(block_at(x, (i + k) % n, dim), axis, k)
    return total


def exchange(x, axis):
    n = lax.axis_size(axis)
    i = lax.axis_index(axis)
    rel = [block_at(x, i, 0)]
    for k in range(1, n):
        rel.append(shifted(block_at(x, (i - k) % n, 0), axis, -k))
    return in_order(rel, axis)


def sum_over(x, axis):
    total = x
    for k in range(1, lax.axis_size(axis)):
        total = total + shifted(x, axis, k)
    return total


def gather_dp(x):
    shape = x.shape
    for axis in ("x", "y", "core"):
        x = gather(x, axis)
    x = jnp.transpose(x, (1, 2, 0) + tuple(range(3, x.ndim)))
    return x.reshape((-1,) + shape)


def scatter_dp(x, shape):
    y, xs, core = (lax.axis_size(a) for a in DP)
    x = x.reshape((y, xs, core) + shape)
    x = scatter_sum(x, "core", 2)
    x = scatter_sum(x, "x", 1)
    return scatter_sum(x, "y", 0)


def dot(a, b, dims=NN):
    return lax.dot_general(a, b, dims, preferred_element_type=F32)


def exact(a, b, dims=NN):
    return lax.dot_general(a, b, dims, precision=HIGHEST, preferred_element_type=F32)


def split(a):
    hi = a.astype(BF16)
    return hi, (a - hi.astype(F32)).astype(BF16)


def dot3(a, b, dims=NN):
    ah, al = split(a)
    bh, bl = split(b)
    return dot(ah, bh, dims) + (dot(ah, bl, dims) + dot(al, bh, dims))


def sigmoid(v):
    return 1.0 / (1.0 + jnp.exp(-v))


def steps_of(sr, hp, heads):
    lane = lax.broadcasted_iota(jnp.int32, sr.shape, 1)
    shifted_raw = sr + hp[0:1]
    step = jnp.maximum(shifted_raw, 0.0) + jnp.log1p(jnp.exp(-jnp.abs(shifted_raw)))
    step = jnp.where(lane < heads, step, 0.0)
    return shifted_raw, step, -step * hp[1:2]


def triangle(q, lower):
    row = lax.broadcasted_iota(jnp.int32, (q, q), 0)
    col = lax.broadcasted_iota(jnp.int32, (q, q), 1)
    return (row >= col) if lower else (col >= row)


def forward_kernel(
    heads, nb, bg, w, co, fp, hp, cp, oh,
    gate_o, sig_o, pre_o, y_o, oc_o, sr_o, sin_o, sums_o,
    state, tail,
):
    q = nb.shape[0]
    ch = cp.shape[1]
    cw = fp.shape[1]
    ns = (cw - ch) // 2
    size = ch // heads

    @pl.when(pl.program_id(0) == 0)
    def _():
        state[...] = jnp.zeros_like(state)
        tail[...] = jnp.zeros_like(tail)

    proj = dot(nb[...], w[...])
    gate = proj[:, :ch]
    signal = proj[:, ch : ch + cw]
    lane = lax.broadcasted_iota(jnp.int32, (q, 128), 1)
    sr = jnp.where(lane < heads, proj[:, ch + cw : ch + cw + 128], 0.0)
    ext = jnp.concatenate([tail[...], signal], axis=0)
    pre = fp[4:5, :] + jnp.zeros_like(signal)
    for k in range(4):
        pre = pre + fp[k : k + 1, :] * ext[5 + k : 5 + k + q]
    tail[...] = signal[q - 8 :]
    act = pre * sigmoid(pre)
    values = act[:, :ch]
    writer = act[:, ch : ch + ns]
    reader = act[:, ch + ns :]
    _, step, ld = steps_of(sr, hp[...], heads)
    lower = triangle(q, True)
    cum = exact(jnp.where(lower, 1.0, 0.0), ld)
    cum_t = cum.T
    cum_e = exact(cum, oh[...])
    step_e = exact(step, oh[...])
    last_e = cum_e[q - 1 : q]
    xv = step_e * values
    scores = dot3(reader, writer, NT)
    parts = []
    for p in range(ch // 128):
        hi, lo = split(xv[:, 128 * p : 128 * p + 128])
        both = jnp.concatenate([hi, lo], axis=1)
        out = None
        for j in range(128 // size):
            h = p * (128 // size) + j
            decay = jnp.exp(cum[:, h : h + 1] - cum_t[h : h + 1, :])
            ph, plo = split(jnp.where(lower, scores * decay, 0.0))
            r = dot(ph, both)
            one = r[:, :128] + (r[:, 128:] + dot(plo, hi))
            out = one if out is None else jnp.where(lane < j * size, out, one)
        parts.append(out)
    inner = jnp.concatenate(parts, axis=1)
    old = state[...]
    sin_o[0] = old
    y = inner + jnp.exp(cum_e) * dot3(reader, old, NT) + cp[0:1, :] * values
    decay_last = jnp.exp(cum_t[:, q - 1 : q])
    decay_ch = exact(oh[...], decay_last * jnp.ones((1, ns), F32), TN)
    state[...] = decay_ch * old + dot3(jnp.exp(last_e - cum_e) * xv, writer, TN)
    gated = y * (gate * sigmoid(gate))
    outcome = dot(bg[...], co[...], NT)
    ones = jnp.ones((8, ch), F32)
    s1 = exact(ones, gated * gated, NT)
    s2 = exact(ones, outcome * cp[1:2, :] * gated, NT)
    row = lax.broadcasted_iota(jnp.int32, s1.shape, 0)
    sums_o[...] = jnp.where(row == 0, s1, jnp.where(row == 1, s2, 0.0))
    gate_o[...] = gate
    sig_o[...] = signal
    pre_o[...] = pre
    y_o[...] = y
    oc_o[...] = outcome
    sr_o[...] = sr


def gate_kernel(width, gate_r, y_r, oc_r, sums, bg, cp, nout_o, gg_o, dy_o, cg_o, acc_o):
    q, ch = gate_r.shape

    @pl.when(pl.program_id(0) == 0)
    def _():
        cg_o[...] = jnp.zeros_like(cg_o)
        acc_o[...] = jnp.zeros_like(acc_o)

    s = sums[...]
    scale_row = lax.rsqrt(s[0:1] * (1.0 / width) + EPS)
    mean_row = scale_row * s[1:2] * (1.0 / width)

    def column(v):
        c = jnp.broadcast_to(v, (128, q)).T
        return jnp.concatenate([c] * (ch // 128), axis=1)

    scale = column(scale_row)
    mean = column(mean_row)
    gate = gate_r[...]
    y = y_r[...]
    outcome = oc_r[...]
    gain = cp[1:2, :]
    sg = sigmoid(gate)
    sl = gate * sg
    unit = y * sl * scale
    nout = (unit * gain).astype(BF16)
    nout_o[...] = nout
    cg_o[...] += dot(nout, bg[...], TN)
    gated_grad = scale * (outcome * gain - unit * mean)
    dy_o[...] = gated_grad * sl
    gg_o[...] = (gated_grad * y * sg * (1.0 + gate * (1.0 - sg))).astype(BF16)
    gain_part = jnp.sum(outcome * unit, axis=0, keepdims=True)
    row = lax.broadcasted_iota(jnp.int32, acc_o.shape, 0)
    acc_o[...] += jnp.where(row == 0, gain_part, 0.0)


def backward_kernel(
    heads, sig_r, pre_r, y_r, dy_r, sr_r, sin_r, fp, hp, cp, oh,
    vg_o, wr_o, raw_o, acc_o, hacc_o,
    adj, head_rows,
):
    q, ch = y_r.shape
    cw = fp.shape[1]
    ns = (cw - ch) // 2
    size = ch // heads

    @pl.when(pl.program_id(0) == 0)
    def _():
        adj[...] = jnp.zeros_like(adj)
        head_rows[...] = jnp.zeros_like(head_rows)
        acc_o[...] = jnp.zeros_like(acc_o)
        hacc_o[...] = jnp.zeros_like(hacc_o)

    pre = pre_r[...]
    sgm = sigmoid(pre)
    act = pre * sgm
    values = act[:, :ch]
    writer = act[:, ch : ch + ns]
    reader = act[:, ch + ns :]
    shifted_raw, step, ld = steps_of(sr_r[...], hp[...], heads)
    lower = triangle(q, True)
    upper = triangle(q, False)
    cum = exact(jnp.where(lower, 1.0, 0.0), ld)
    cum_t = cum.T
    cum_e = exact(cum, oh[...])
    step_e = exact(step, oh[...])
    last_e = cum_e[q - 1 : q]
    skip = cp[0:1, :]
    dy = dy_r[...]
    y = y_r[...]
    xv = step_e * values
    lane = lax.broadcasted_iota(jnp.int32, (q, 128), 1)
    scores = dot3(writer, reader, NT)
    dscores = jnp.zeros((q, q), F32)
    parts = []
    for p in range(ch // 128):
        dpair = dy[:, 128 * p : 128 * p + 128]
        xpair = xv[:, 128 * p : 128 * p + 128]
        dh, dl = split(dpair)
        dboth = jnp.concatenate([dh, dl], axis=1)
        dtwice = jnp.concatenate([dh, dh], axis=1)
        out = None
        for j in range(128 // size):
            h = p * (128 // size) + j
            decay = jnp.where(upper, jnp.exp(cum_t[h : h + 1, :] - cum[:, h : h + 1]), 0.0)
            ph, plo = split(jnp.where(upper, scores * decay, 0.0))
            r = dot(ph, dboth)
            one = r[:, :128] + (r[:, 128:] + dot(plo, dh))
            out = one if out is None else jnp.where(lane < j * size, out, one)
            mine = (lane >= j * size) & (lane < (j + 1) * size)
            xh, xl = split(jnp.where(mine, xpair, 0.0))
            m = dot(jnp.concatenate([xh, xl], axis=1), dtwice, NT) + dot(xh, dl, NT)
            dscores = dscores + m * decay
        parts.append(out)
    inner = jnp.concatenate(parts, axis=1)
    old = adj[...]
    sin = sin_r[0]
    ends = jnp.exp(last_e - cum_e)
    from_state = ends * dot3(writer, old, NT)
    dxv = inner + from_state
    cdy = jnp.exp(cum_e) * dy
    dwriter = dot3(dscores, reader) + dot3(ends * xv, old)
    dreader = dot3(dscores, writer, TN) + dot3(cdy, sin)
    decay_last = jnp.exp(cum_t[:, q - 1 : q])
    decay_ch = exact(oh[...], decay_last * jnp.ones((1, ns), F32), TN)
    state_part = decay_ch * old * sin
    ones = jnp.ones((8, ns), F32)
    state_row = exact(ones, state_part, NT)[0:1]
    last_row = state_row + jnp.sum(xv * from_state, axis=0, keepdims=True)
    adj[...] = decay_ch * old + dot3(cdy, reader, TN)

    dstep = exact(values * dxv, oh[...], NT)
    row = lax.broadcasted_iota(jnp.int32, (q, ch), 0)
    dcum_ch = dy * (y - skip * values) - xv * dxv + jnp.where(row == q - 1, last_row, 0.0)
    dcum = exact(dcum_ch, oh[...], NT)
    dld = exact(jnp.where(upper, 1.0, 0.0), dcum)
    raw = (dstep - dld * hp[1:2]) * sigmoid(shifted_raw)
    raw = jnp.where(lane < heads, raw, 0.0)
    raw_o[...] = raw.astype(BF16)
    hrow = lax.broadcasted_iota(jnp.int32, hacc_o.shape, 0)
    hacc_o[...] += jnp.where(
        hrow == 0,
        jnp.sum(raw, axis=0, keepdims=True),
        jnp.where(hrow == 1, jnp.sum(dld * ld, axis=0, keepdims=True), 0.0),
    )

    wr_o[...] = jnp.concatenate([dwriter, dreader], axis=1)
    sv = sgm[:, :ch]
    dpre = (step_e * dxv + skip * dy) * (sv * (1.0 + pre[:, :ch] * (1.0 - sv)))
    ext = jnp.concatenate([dpre, head_rows[...]], axis=0)
    head_rows[...] = dpre[:8]
    signal = sig_r[:, :ch]
    total = jnp.zeros_like(dpre)
    rows = []
    for k in range(4):
        moved = ext[3 - k : 3 - k + q]
        total = total + fp[k : k + 1, :ch] * moved
        rows.append(jnp.sum(moved * signal, axis=0, keepdims=True))
    vg_o[...] = total.astype(BF16)
    rows.append(jnp.sum(dpre, axis=0, keepdims=True))
    rows.append(jnp.sum(values * dy, axis=0, keepdims=True))
    rows.append(jnp.zeros((2, ch), F32))
    acc_o[...] += jnp.concatenate(rows, axis=0)


def whole(shape):
    return pl.BlockSpec(shape, lambda b: (0,) * len(shape))


def rows_of(q, width, order=lambda b: b):
    return pl.BlockSpec((q, width), lambda b: (order(b), 0))


def params(flops, nbytes):
    return dict(
        compiler_params=pltpu.CompilerParams(
            dimension_semantics=("arbitrary",), vmem_limit_bytes=VMEM_LIMIT
        ),
        cost_estimate=pl.CostEstimate(flops=flops, bytes_accessed=nbytes, transcendentals=0),
    )


def body(
    residual, lengths, norm_gain, expand, filters, offsets, gate_gain, contract,
    step_bias, decay_log, skip_gain, cotangent,
):
    micro, _, q, width = residual.shape
    heads_all = step_bias.shape[0]
    reps = lax.axis_size("rep")
    heads = heads_all // reps
    dp = lax.axis_size("y") * lax.axis_size("x") * lax.axis_size("core")
    inner = contract.shape[0] * dp
    ch = inner // reps
    conv = filters.shape[0] * dp
    ns = (conv - inner) // 2
    cw = ch + 2 * ns
    size = inner // heads_all
    total = q * reps
    rep = lax.axis_index("rep")
    rows = expand.shape[0]
    wr = 2 * ns // reps
    residual = residual[:, 0]
    cotangent = cotangent[:, 0]

    small = jnp.concatenate([norm_gain, filters.reshape(-1), offsets, gate_gain])
    sizes = np.cumsum([0, norm_gain.shape[0], filters.size, offsets.shape[0], gate_gain.shape[0]])
    padded = -(-small.shape[0] // 128) * 128
    small = jnp.pad(small, (0, padded - small.shape[0])).reshape(-1, 128)
    position = rep * q + jnp.arange(q, dtype=jnp.int32)
    mask = (position[None, :] < lengths[:, :1]).astype(F32)[..., None]
    branch_grad = (mask * cotangent).astype(BF16)
    with jax.named_scope("gather_small"):
        small = gather_dp(small).reshape(dp, padded).astype(F32)
    gain_one = small[:, sizes[0] : sizes[1]].reshape(-1)
    filters_full = small[:, sizes[1] : sizes[2]].reshape(conv, 4).T
    offsets_full = small[:, sizes[2] : sizes[3]].reshape(1, conv)
    gain_two = small[:, sizes[3] : sizes[4]].reshape(1, inner)

    def own(a, start, count, dim=-1):
        return lax.dynamic_slice_in_dim(a, start + rep * count, count, a.ndim + dim)

    w_shard = jnp.concatenate(
        [
            own(expand, 0, ch),
            own(expand, inner, ch),
            expand[:, 2 * inner : 2 * inner + 2 * ns],
            jnp.pad(own(expand, 2 * inner + 2 * ns, heads), ((0, 0), (0, 128 - heads))),
        ],
        axis=1,
    )
    with jax.named_scope("gather_own_expand"):
        w_own = gather_dp(w_shard).reshape(width, ch + cw + 128)
    with jax.named_scope("gather_contract"):
        contract_full = lax.all_gather(contract, DP, axis=0, tiled=True)
    contract_own = lax.dynamic_slice_in_dim(contract_full, rep * ch, ch, 0)
    expand_cols = jnp.concatenate(
        [
            expand[:, :inner].reshape(rows, reps, ch),
            expand[:, inner : 2 * inner].reshape(rows, reps, ch),
            expand[:, 2 * inner : 2 * inner + 2 * ns].reshape(rows, reps, wr),
            expand[:, 2 * inner + 2 * ns :].reshape(rows, reps, heads),
            jnp.zeros((rows, reps, 128 - wr - heads), BF16),
        ],
        axis=2,
    ).reshape(rows, reps * (2 * ch + 128))
    with jax.named_scope("gather_expand"):
        expand_full = lax.all_gather(expand_cols, DP, axis=0, tiled=True)

    own_filters = jnp.concatenate(
        [own(filters_full[:, :inner], 0, ch), filters_full[:, inner:]], axis=1
    )
    own_offsets = jnp.concatenate(
        [own(offsets_full[:, :inner], 0, ch), offsets_full[:, inner:]], axis=1
    )
    fp = jnp.concatenate([own_filters, own_offsets, jnp.zeros((3, cw), F32)], axis=0)
    own_skip = own(skip_gain, 0, heads)
    cp = jnp.concatenate(
        [jnp.repeat(own_skip, size)[None], own(gain_two, 0, ch), jnp.zeros((6, ch), F32)], axis=0
    )
    rate = jnp.exp(own(decay_log, 0, heads))
    hp = jnp.pad(jnp.stack([own(step_bias, 0, heads), rate]), ((0, 6), (0, 128 - heads)))
    onehot = np.zeros((128, ch), np.float32)
    onehot[np.arange(ch) // size, np.arange(ch)] = 1.0
    onehot = jnp.asarray(onehot)

    scale_one = lax.rsqrt(jnp.mean(residual * residual, axis=-1, keepdims=True) + EPS)
    unit_one = residual * scale_one
    normed = (unit_one * gain_one).astype(BF16)

    full_bg, full_normed = [], []
    for m in range(micro):
        with jax.named_scope("gather_branch_grad"):
            full_bg.append(gather(branch_grad[m], "rep", ring=True).reshape(total, width))
        with jax.named_scope("gather_normed"):
            full_normed.append(gather(normed[m], "rep", ring=True).reshape(total, width))

    sds = jax.ShapeDtypeStruct
    forward = pl.pallas_call(
        functools.partial(forward_kernel, heads),
        grid=(reps,),
        in_specs=[
            rows_of(q, width), rows_of(q, width), whole((width, ch + cw + 128)), whole((ch, width)),
            whole((8, cw)), whole((8, 128)), whole((8, ch)), whole((128, ch)),
        ],
        out_specs=[
            rows_of(q, ch), rows_of(q, cw), rows_of(q, cw), rows_of(q, ch), rows_of(q, ch),
            rows_of(q, 128), pl.BlockSpec((1, ch, ns), lambda b: (b, 0, 0)),
            pl.BlockSpec((8, q), lambda b: (0, b)),
        ],
        out_shape=[
            sds((total, ch), F32), sds((total, cw), F32), sds((total, cw), F32),
            sds((total, ch), F32), sds((total, ch), F32), sds((total, 128), F32),
            sds((reps, ch, ns), F32), sds((8, total), F32),
        ],
        scratch_shapes=[pltpu.VMEM((ch, ns), F32), pltpu.VMEM((8, cw), F32)],
        name="scan_forward",
        **params(20_000_000_000, 20_000_000),
    )
    gating = pl.pallas_call(
        functools.partial(gate_kernel, inner),
        grid=(reps,),
        in_specs=[
            rows_of(q, ch), rows_of(q, ch), rows_of(q, ch),
            pl.BlockSpec((8, q), lambda b: (0, b)), rows_of(q, width), whole((8, ch)),
        ],
        out_specs=[
            rows_of(q, ch), rows_of(q, ch), rows_of(q, ch), whole((ch, width)), whole((8, ch)),
        ],
        out_shape=[
            sds((total, ch), BF16), sds((total, ch), BF16), sds((total, ch), F32),
            sds((ch, width), F32), sds((8, ch), F32),
        ],
        name="gate_backward",
        **params(4_000_000_000, 10_000_000),
    )
    back = lambda b: reps - 1 - b
    backward = pl.pallas_call(
        functools.partial(backward_kernel, heads),
        grid=(reps,),
        in_specs=[
            rows_of(q, cw, back), rows_of(q, cw, back), rows_of(q, ch, back), rows_of(q, ch, back),
            rows_of(q, 128, back), pl.BlockSpec((1, ch, ns), lambda b: (back(b), 0, 0)),
            whole((8, cw)), whole((8, 128)), whole((8, ch)), whole((128, ch)),
        ],
        out_specs=[
            rows_of(q, ch, back), rows_of(q, 2 * ns, back), rows_of(q, 128, back),
            whole((8, ch)), whole((8, 128)),
        ],
        out_shape=[
            sds((total, ch), BF16), sds((total, 2 * ns), F32), sds((total, 128), BF16),
            sds((8, ch), F32), sds((8, 128), F32),
        ],
        scratch_shapes=[pltpu.VMEM((ch, ns), F32), pltpu.VMEM((8, ch), F32)],
        name="scan_backward",
        **params(40_000_000_000, 20_000_000),
    )

    wr_filters = own(filters_full[:, inner:], 0, wr)
    sums = []
    kept = []
    for m in range(micro):
        out = forward(full_normed[m], full_bg[m], w_own, contract_own, fp, hp, cp, onehot)
        kept.append(out)
        with jax.named_scope("sum_norm_terms"):
            sums.append(sum_over(out[7], "rep"))
    mixed, gate_grads, dys, back_nout = [], [], [], []
    contract_part = 0.0
    gain_part = 0.0
    for m in range(micro):
        gate, _, _, y, outcome, _, _, _ = kept[m]
        nout, gg, dy, cg, acc = gating(gate, y, outcome, sums[m], full_bg[m], cp)
        gate_grads.append(gg)
        dys.append(dy)
        contract_part = contract_part + cg
        gain_part = gain_part + acc[0]
        back_nout.append(nout)
    own_pg = []
    for m in range(micro):
        with jax.named_scope("send_gate_parts"):
            both = jnp.concatenate([back_nout[m], gate_grads[m]], axis=1).reshape(reps, q, 2 * ch)
            got = exchange(both, "rep")
        nout_own = jnp.concatenate([got[s, :, :ch] for s in range(reps)], axis=1)
        branch = jnp.dot(nout_own, contract_full, preferred_element_type=F32)
        mixed.append(residual[m] + mask[m] * branch)
        own_pg.append(got[:, :, ch:])
    with jax.named_scope("sum_contract_grad"):
        cgs = contract_part.reshape(lax.axis_size("x"), lax.axis_size("core"), -1, width)
        cgs = scatter_sum(cgs, "core", 1)
        cgs = scatter_sum(cgs, "x", 0)
        ys = lax.axis_size("y")
        cgs = cgs.reshape(ys, -1, width)
        cgs = scatter_sum(cgs, "y", 0)
        cgs = lax.ppermute(
            cgs, ("y", "rep"), [(a * reps + b, b * reps + a) for a in range(ys) for b in range(reps)]
        )
        contract_grad = gather(cgs, "rep").reshape(-1, width)

    normed_all = jnp.concatenate(full_normed, axis=0)
    with jax.named_scope("sum_expand_grad_gate"):
        gate_all = jnp.concatenate(gate_grads, axis=0)
        eg_gate = lax.dot_general(normed_all, gate_all, TN, preferred_element_type=F32)
        eg_gate = scatter_dp(eg_gate, (rows, ch))

    value_grads, tails, channel_part, head_part, wr_part = [], [], 0.0, 0.0, 0.0
    grads = []
    for m in range(micro):
        _, signal, pre, y, _, sr, sin, _ = kept[m]
        vg, wrg, raw, acc, hacc = backward(signal, pre, y, dys[m], sr, sin, fp, hp, cp, onehot)
        value_grads.append(vg)
        channel_part = channel_part + acc
        head_part = head_part + hacc
        with jax.named_scope("sum_writer_reader_grad"):
            t = wrg.reshape(2, total // 2, reps, wr)
            t = jnp.transpose(t, (2, 1, 0, 3)).reshape(reps, total // 2, 2 * wr)
            t = scatter_sum(t, "rep", 0)
            t = jnp.transpose(t.reshape(total // 2, 2, wr), (1, 0, 2)).reshape(total, wr)
        pre_wr = own(pre[:, ch:], 0, wr)
        sig_wr = own(signal[:, ch:], 0, wr)
        s = jax.nn.sigmoid(pre_wr)
        dpre = t * (s * (1.0 + pre_wr * (1.0 - s)))
        ext = jnp.pad(dpre, ((0, 3), (0, 0)))
        wr_grad = jnp.zeros_like(dpre)
        parts = []
        for k in range(4):
            moved = ext[3 - k : 3 - k + total]
            wr_grad = wr_grad + wr_filters[k][None] * moved
            parts.append(jnp.sum(moved * sig_wr, axis=0))
        parts.append(jnp.sum(dpre, axis=0))
        wr_part = wr_part + jnp.stack(parts)
        tails.append(
            jnp.concatenate(
                [wr_grad.astype(BF16), raw[:, :heads], jnp.zeros((total, 128 - wr - heads), BF16)],
                axis=1,
            )
        )
    for m in range(micro):
        with jax.named_scope("send_value_grad"):
            vgs = exchange(value_grads[m].reshape(reps, q, ch), "rep")
        with jax.named_scope("send_tail_grad"):
            tls = exchange(tails[m].reshape(reps, q, 128), "rep")
        pg = jnp.concatenate([own_pg[m], vgs, tls], axis=2)
        pg = jnp.concatenate([pg[s] for s in range(reps)], axis=1)
        grads.append(lax.dot_general(pg, expand_full, NT, preferred_element_type=F32))
    with jax.named_scope("sum_expand_grad_values"):
        vg_all = jnp.concatenate(value_grads, axis=0)
        eg_values = lax.dot_general(normed_all, vg_all, TN, preferred_element_type=F32)
        eg_values = scatter_dp(eg_values, (rows, ch))
    with jax.named_scope("sum_expand_grad_tail"):
        tail_all = jnp.concatenate(tails, axis=0)
        eg_tail = lax.dot_general(normed_all, tail_all, TN, preferred_element_type=F32)
        eg_tail = scatter_dp(eg_tail, (rows, 128))
    with jax.named_scope("gather_expand_grad"):
        eg = gather(jnp.concatenate([eg_gate, eg_values, eg_tail], axis=1), "rep")
    expand_grad = jnp.concatenate(
        [eg[s, :, a:b] for a, b in ((0, ch), (ch, 2 * ch), (2 * ch, 2 * ch + wr), (2 * ch + wr, 2 * ch + wr + heads)) for s in range(reps)],
        axis=1,
    )

    normed_grad = jnp.stack(grads)
    norm_part = jnp.sum(normed_grad * unit_one, axis=(0, 1))
    scaled = normed_grad * gain_one
    residual_grad = cotangent + scale_one * (
        scaled - unit_one * jnp.mean(scaled * unit_one, axis=-1, keepdims=True)
    )

    def sum_dp(v):
        n = v.shape[0]
        v = jnp.pad(v, (0, -n % 1024)).reshape(-1, 128)
        for axis in ("core", "x", "y"):
            v = sum_over(v, axis)
        return v

    with jax.named_scope("sum_small"):
        flat = jnp.concatenate(
            [channel_part[:6].reshape(-1), gain_part, head_part[:2].reshape(-1), wr_part.reshape(-1)]
        )
        flat = gather(sum_dp(flat), "rep").reshape(reps, -1)
    cuts = np.cumsum([0, 6 * ch, ch, 256, 5 * wr])
    channels = flat[:, : cuts[1]].reshape(reps, 6, ch)
    gain_all = flat[:, cuts[1] : cuts[2]].reshape(-1)
    head_all = flat[:, cuts[2] : cuts[3]].reshape(reps, 2, 128)[:, :, :heads]
    wr_all = flat[:, cuts[3] : cuts[4]].reshape(reps, 5, wr)
    taps = jnp.concatenate(
        [
            jnp.transpose(channels[:, :5], (1, 0, 2)).reshape(5, inner),
            jnp.transpose(wr_all, (1, 0, 2)).reshape(5, 2 * ns),
        ],
        axis=1,
    )
    place = lax.axis_index(DP)
    mine = lambda a: lax.dynamic_slice_in_dim(a, place * (a.shape[-1] // dp), a.shape[-1] // dp, a.ndim - 1)
    own_taps = mine(taps)
    filters_grad = own_taps[:4].T
    offsets_grad = own_taps[4]
    gain_grad = mine(gain_all)
    skip_grad = jnp.sum(channels[:, 5].reshape(heads_all, size), axis=1)
    bias_grad = head_all[:, 0].reshape(-1)
    decay_grad = head_all[:, 1].reshape(-1)
    with jax.named_scope("sum_norm_grad"):
        norm_grad = mine(sum_over(sum_dp(norm_part), "rep").reshape(-1)[:width])

    return (
        jnp.stack(mixed)[:, None],
        residual_grad[:, None],
        norm_grad,
        expand_grad,
        filters_grad,
        offsets_grad,
        gain_grad,
        contract_grad,
        bias_grad,
        decay_grad,
        skip_grad,
    )


def solution(mesh):
    dp, rep = mesh.devices.shape
    core = 2 if dp % 8 == 0 else 1
    fine = Mesh(mesh.devices.reshape(rep, dp // (core * rep), core, rep), DP + ("rep",))
    rows = P(None, DP, "rep", None)
    in_specs = (
        rows, P(None, DP), P(DP), P(DP, None), P(DP, None), P(DP), P(DP), P(DP, None),
        P(), P(), P(), rows,
    )
    out_specs = (
        rows, rows, P(DP), P(DP, None), P(DP, None), P(DP), P(DP), P(DP, None), P(), P(), P(),
    )
    return jax.shard_map(body, mesh=fine, in_specs=in_specs, out_specs=out_specs, check_vma=False)
```

time: 797 us -> 601 us (0.75)
  blocking collectives: 372 us -> 0 us
  starting transfers between devices: 11.3 us -> 154 us
  matrix products: 140 us -> 17.7 us
  Pallas kernels: 0 us -> 104 us
  waiting for transfers between devices: 57.6 us -> 135 us
  other arithmetic: 87.6 us -> 37.6 us
  local copies, waits for them, and re-layouts: 97 us -> 123 us
    unnamed x2 -> x0, blocking collectives: 253 us -> none
    ppermute x4 -> x115, starting transfers between devices: 10.4 us -> 154 us  [the longest x114 154 us: shifted(): return lax.ppermute(x, axis, [(i, (i + shift) % n) for i in range(n)])]
    ppermute x4 -> x115, waiting for transfers between devices: 0.01 us -> 135 us  [the longest x114 135 us: shifted(): return lax.ppermute(x, axis, [(i, (i + shift) % n) for i in range(n)])]
    dot_general x36 -> x7, matrix products: 140 us -> 17.7 us  [the longest x2 6.34 us: body(): lax.dot_general(pg, expand_full, NT, preferred_element_type=F32)]
    pallas_call x0 -> x6, Pallas kernels: none -> 104 us  [the longest x2 52.4 us: body(): backward(signal, pre, y, dys[m], sr, sin, fp, hp, cp, onehot)]
    psum x2 -> x0, blocking collectives: 78.7 us -> none  [the longest x1 68.8 us: body(): lax.psum((sum_bias, sum_decay, sum_skip), ('dp', 'rep'))]
    all_gather x3 -> x0, blocking collectives: 40.7 us -> none  [the longest x1 24.5 us: body(): lax.all_gather(filters, 'dp', axis=0, tiled=True)]
    psum x1 -> x0, waiting for transfers between devices: 34.1 us -> none  [body(): lax.psum((norm_part, expand_part, filter_part, offset_part, gain_part, co...]
  transfers between devices with their start and end apart: 13 -> 117, of which waited for: 2 -> 47; matrix products, arithmetic and copies ran while one was open for 35% -> 28% of each run, Pallas kernels for 0% -> 18%
where the time goes in v1:
time: 601 us; the launch traced here: 589 us
  starting transfers between devices  154 us (26%)
  waiting for transfers between devices  135 us (22%)
  local copies, waits for them, and re-layouts  123 us (20%)
  Pallas kernels  104 us (17%)
  other arithmetic  37.6 us (6%)
  matrix products  17.7 us (3%)
  between operations  16.8 us (3%)
    ppermute x114, starting transfers between devices, shifted(): return lax.ppermute(x, axis, [(i, (i + shift) % n) for i in range(n)])  154 us
    ppermute x114, waiting for transfers between devices, shifted(): return lax.ppermute(x, axis, [(i, (i + shift) % n) for i in range(n)])  135 us
    pallas_call x2, Pallas kernels, body(): backward(signal, pre, y, dys[m], sr, sin, fp, hp, cp, onehot)  52.4 us
    pallas_call x2, Pallas kernels, body(): forward(full_normed[m], full_bg[m], w_own, contract_own, fp, hp, cp, onehot)  39.6 us
    unnamed x278, local copies, waits for them, and re-layouts  34.3 us
    pallas_call x2, Pallas kernels, body(): nout, gg, dy, cg, acc = gating(gate, y, outcome, sums[m], full_bg[m], cp)  12.4 us
  transfers between devices with their start and end apart: 117, of which 47 were waited for; matrix products, arithmetic and copies ran while one was open for 28% of the time, Pallas kernels for 18%

profile of v1, /device:TPU:0, one launch (start us, length us, event | category | flops | bytes accessed | tf_op | source)
XLA Modules:
  0.0 589.4 jit_solution(10310780862607768717)
XLA Ops:
  40.7 4.6 collective-permute-done.5
  61.1 4.5 collective-permute-done.18
  67.0 6.5 %collective-permute-done.19 = bf16[4,24,1152]{2,1,0:T(8,128)(2,1)S(1)} collective-permute-done((bf16[4,24,1152]{2,1,0:T(8,128)(2,1)S(1)}, bf16[4,24,1152]{2,1,0:T(8,128)(2,1)S(1)}, u32[]{:S(2)}, u32[]{:S(2)}) %collective-permute-start.19) | collective-permute-done | bytes 221216 | tf_op jit(solution)/shard_map/gather_own_expand/ppermute | solution.py:25
  73.7 7.9 %collective-permute-done.20 = bf16[4,24,1152]{2,1,0:T(8,128)(2,1)S(1)} collective-permute-done((bf16[4,24,1152]{2,1,0:T(8,128)(2,1)S(1)}, bf16[4,24,1152]{2,1,0:T(8,128)(2,1)S(1)}, u32[]{:S(2)}, u32[]{:S(2)}) %collective-permute-start.20) | collective-permute-done | bytes 221216 | tf_op jit(solution)/shard_map/gather_own_expand/ppermute | solution.py:25
  92.9 4.2 collective-permute-start.14
  123.0 19.8 %scan_forward.2 = (f32[1024,384]{1,0:T(8,128)}, f32[1024,640]{1,0:T(8,128)}, f32[1024,640]{1,0:T(8,128)}, f32[1024,384]{1,0:T(8,128)}, f32[1024,384]{1,0:T(8,128...) custom-call(bf16[1024,768]{1,0:T(8,128)(2,1)} %bitcast.601, bf16[1024,768]{1,0:T(8,128)(2,1)} %bitcast.607, ...), custom_call_target="tpu_custom_call" | custom-call | flops 20000000000 | bytes 20000000 | tf_op jit(solution)/shard_map/scan_forward/pallas_call | solution.py:533
  146.3 19.8 %scan_forward.3 = (f32[1024,384]{1,0:T(8,128)}, f32[1024,640]{1,0:T(8,128)}, f32[1024,640]{1,0:T(8,128)}, f32[1024,384]{1,0:T(8,128)}, f32[1024,384]{1,0:T(8,128...) custom-call(bf16[1024,768]{1,0:T(8,128)(2,1)} %bitcast.597, bf16[1024,768]{1,0:T(8,128)(2,1)} %bitcast.605, ...), custom_call_target="tpu_custom_call" | custom-call | flops 20000000000 | bytes 20000000 | tf_op jit(solution)/shard_map/scan_forward/pallas_call | solution.py:533
  180.5 6.2 %gate_backward.2 = (bf16[1024,384]{1,0:T(8,128)(2,1)}, bf16[1024,384]{1,0:T(8,128)(2,1)}, f32[1024,384]{1,0:T(8,128)}, f32[384,768]{1,0:T(8,128)}, f32[8,384]{1,0:T(8,128)}) custom-call(f32[1024,384]{1,0:T(8,128)} %get-tuple-element.47.gate_r, f32[1024,384]{1,0:T(8,128)} %get-tuple-element.48.y_r, f32[1024,384]{1,0:T(8,128)} %get-tuple-element.49.oc_r, ...), custom_call_target="tpu_custom_call" | custom-call | flops 4000000000 | bytes 10000000 | tf_op jit(solution)/shard_map/gate_backward/pallas_call | solution.py:542
  186.7 26.2 %scan_backward.2 = (bf16[1024,384]{1,0:T(8,128)(2,1)}, f32[1024,256]{1,0:T(8,128)}, bf16[1024,128]{1,0:T(8,128)(2,1)}, f32[8,384]{1,0:T(8,128)}, f32[8,128]{1,0:T(8,128)}) custom-call(f32[1024,640]{1,0:T(8,128)} %get-tuple-element.59.sig_r, f32[1024,640]{1,0:T(8,128)} %get-tuple-element.60.pre_r, f32[1024,384]{1,0:T(8,128)} %get-tuple-element.48.y_r, ...), custom_call_target="tpu_custom_call" | custom-call | flops 40000000000 | bytes 20000000 | tf_op jit(solution)/shard_map/scan_backward/pallas_call | solution.py:579
  228.0 6.2 %gate_backward.3 = (bf16[1024,384]{1,0:T(8,128)(2,1)}, bf16[1024,384]{1,0:T(8,128)(2,1)}, f32[1024,384]{1,0:T(8,128)}, f32[384,768]{1,0:T(8,128)}, f32[8,384]{1,0:T(8,128)}) custom-call(f32[1024,384]{1,0:T(8,128)} %get-tuple-element.53.gate_r, f32[1024,384]{1,0:T(8,128)} %get-tuple-element.54.y_r, f32[1024,384]{1,0:T(8,128)} %get-tuple-element.55.oc_r, ...), custom_call_target="tpu_custom_call" | custom-call | flops 4000000000 | bytes 10000000 | tf_op jit(solution)/shard_map/gate_backward/pallas_call | solution.py:542
  234.3 26.2 %scan_backward.3 = (bf16[1024,384]{1,0:T(8,128)(2,1)}, f32[1024,256]{1,0:T(8,128)}, bf16[1024,128]{1,0:T(8,128)(2,1)}, f32[8,384]{1,0:T(8,128)}, f32[8,128]{1,0:T(8,128)}) custom-call(f32[1024,640]{1,0:T(8,128)} %get-tuple-element.67.sig_r, f32[1024,640]{1,0:T(8,128)} %get-tuple-element.68.pre_r, f32[1024,384]{1,0:T(8,128)} %get-tuple-element.54.y_r, ...), custom_call_target="tpu_custom_call" | custom-call | flops 40000000000 | bytes 20000000 | tf_op jit(solution)/shard_map/scan_backward/pallas_call | solution.py:579
  266.1 4.3 fusion.27
  281.8 7.2 %collective-permute-done.43 = bf16[256,384]{1,0:T(8,128)(2,1)S(1)} collective-permute-done((bf16[256,384]{1,0:T(8,128)(2,1)S(1)}, bf16[256,384]{1,0:T(8,128)(2,1)S(1)}, u32[]{:S(2)}, u32[]{:S(2)}) %collective-permute-start.43) | collective-permute-done | bytes 196640 | tf_op jit(solution)/shard_map/send_value_grad/ppermute | solution.py:25
  297.8 5.9 %collective-permute-done.52 = bf16[256,384]{1,0:T(8,128)(2,1)S(1)} collective-permute-done((bf16[256,384]{1,0:T(8,128)(2,1)S(1)}, bf16[256,384]{1,0:T(8,128)(2,1)S(1)}, u32[]{:S(2)}, u32[]{:S(2)}) %collective-permute-start.52) | collective-permute-done | bytes 196640 | tf_op jit(solution)/shard_map/send_value_grad/ppermute | solution.py:25
  304.7 11.1 %collective-permute-done.53 = bf16[256,384]{1,0:T(8,128)(2,1)S(1)} collective-permute-done((bf16[256,384]{1,0:T(8,128)(2,1)S(1)}, bf16[256,384]{1,0:T(8,128)(2,1)S(1)}, u32[]{:S(2)}, u32[]{:S(2)}) %collective-permute-start.53) | collective-permute-done | bytes 196640 | tf_op jit(solution)/shard_map/send_value_grad/ppermute | solution.py:25
  321.9 4.1 collective-permute-start.26
  367.4 4.1 collective-permute-done.101
  376.9 4.8 collective-permute-done.103
  400.5 4.5 collective-permute-done.58
  406.0 4.6 collective-permute-done.59
  415.7 5.3 collective-permute-done.49
  448.5 10.7 %collective-permute-done.39 = bf16[256,768]{1,0:T(8,128)(2,1)S(1)} collective-permute-done((bf16[256,768]{1,0:T(8,128)(2,1)S(1)}, bf16[256,768]{1,0:T(8,128)(2,1)S(1)}, u32[]{:S(2)}, u32[]{:S(2)}) %collective-permute-start.39) | collective-permute-done | bytes 393248 | tf_op jit(solution)/shard_map/send_gate_parts/ppermute | solution.py:25
  527.9 8.2 %collective-permute-start.114 = (f32[12,768]{1,0:T(8,128)S(1)}, f32[12,768]{1,0:T(8,128)S(1)}, u32[]{:S(2)}, u32[]{:S(2)}) collective-permute-start(f32[12,768]{1,0:T(8,128)S(1)} %collective-permute-done.111), channel_id=1, source_target_pairs={{0,1},{1,2},{2,3},{3,0},{4,5},{5,6},{6,7},{7,4},{8,9},{9,10},{10,1... | collective-permute-start | bytes 110600 | tf_op jit(solution)/shard_map/sum_contract_grad/ppermute | solution.py:25
  549.1 4.7 fusion
  (723 shorter events, 360.8 us)
Async XLA Ops:
  7.2 113.9 %all-gather.3.cloned.1.call-start = ((), (), s32[]{:S(2)}) async-start(), calls=%async_computation | async-start | bytes 2433024 | tf_op jit(solution)/shard_map/gather_contract/all_gather | solution.py:425
  7.9 541.0 %all-gather.5.cloned.1.call-start = ((), (), s32[]{:S(2)}) async-start(), calls=%async_computation.1 | async-start | bytes 5677056 | tf_op jit(solution)/shard_map/gather_expand/all_gather | solution.py:438
  18.3 37.1 %collective-permute-start.16 = (bf16[24,1152]{1,0:T(8,128)(2,1)}, bf16[24,1152]{1,0:T(8,128)(2,1)S(1)}, u32[]{:S(2)}, u32[]{:S(2)}) collective-permute-start(bf16[24,1152]{1,0:T(8,128)(2,1)} %fusion.74), channel_id=1, source_target_pairs={{0,16},{8,24},{16,0},{24,8},{1,17},{9,25},{17,1},{25,9},{2,18},{10... | collective-permute-start | bytes 165896 | tf_op jit(solution)/shard_map/gather_own_expand/ppermute | solution.py:25
  18.8 36.6 %collective-permute-start.15 = (bf16[24,1152]{1,0:T(8,128)(2,1)}, bf16[24,1152]{1,0:T(8,128)(2,1)S(1)}, u32[]{:S(2)}, u32[]{:S(2)}) collective-permute-start(bf16[24,1152]{1,0:T(8,128)(2,1)} %fusion.74), channel_id=1, source_target_pairs={{0,24},{8,0},{16,8},{24,16},{1,25},{9,1},{17,9},{25,17},{2,26},{10... | collective-permute-start | bytes 165896 | tf_op jit(solution)/shard_map/gather_own_expand/ppermute | solution.py:25
  28.2 53.7 %collective-permute-start.12 = (bf16[256,768]{1,0:T(8,128)(2,1)}, bf16[256,768]{1,0:T(8,128)(2,1)}, u32[]{:S(2)}, u32[]{:S(2)}) collective-permute-start(bf16[256,768]{1,0:T(8,128)(2,1)} %get-tuple-element.176), channel_id=1, source_target_pairs={{0,1},{1,2},{2,3},{3,0},{4,5},{5,6},{6,7},{7,4},{8,9},{9,10},{10,1... | collective-permute-start | bytes 1179656 | tf_op jit(solution)/shard_map/gather_branch_grad/ppermute | solution.py:25
  46.6 39.6 %collective-permute-start.11 = (bf16[256,768]{1,0:T(8,128)(2,1)}, bf16[256,768]{1,0:T(8,128)(2,1)}, u32[]{:S(2)}, u32[]{:S(2)}) collective-permute-start(bf16[256,768]{1,0:T(8,128)(2,1)} %get-tuple-element.176), channel_id=1, source_target_pairs={{0,3},{1,0},{2,1},{3,2},{4,7},{5,4},{6,5},{7,6},{8,11},{9,8},{10,9... | collective-permute-start | bytes 1179656 | tf_op jit(solution)/shard_map/gather_branch_grad/ppermute | solution.py:25
  55.5 35.1 %collective-permute-start.32 = (bf16[256,768]{1,0:T(8,128)(2,1)S(1)}, bf16[256,768]{1,0:T(8,128)(2,1)S(1)}, u32[]{:S(2)}, u32[]{:S(2)}) collective-permute-start(bf16[256,768]{1,0:T(8,128)(2,1)S(1)} %copy-done.43), channel_id=1, source_target_pairs={{0,3},{1,0},{2,1},{3,2},{4,7},{5,4},{6,5},{7,6},{8,11},{9,8},{10,9... | collective-permute-start | bytes 1179656 | tf_op jit(solution)/shard_map/gather_branch_grad/ppermute | solution.py:25
  142.8 37.0 %collective-permute-start.24 = (f32[8,1024]{1,0:T(8,128)}, f32[8,1024]{1,0:T(8,128)S(1)}, u32[]{:S(2)}, u32[]{:S(2)}) collective-permute-start(f32[8,1024]{1,0:T(8,128)} %get-tuple-element.50), channel_id=1, source_target_pairs={{0,3},{1,0},{2,1},{3,2},{4,7},{5,4},{6,5},{7,6},{8,11},{9,8},{10,9... | collective-permute-start | bytes 98312 | tf_op jit(solution)/shard_map/sum_norm_terms/ppermute | solution.py:25
  145.1 34.7 %collective-permute-start.23 = (f32[8,1024]{1,0:T(8,128)}, f32[8,1024]{1,0:T(8,128)S(1)}, u32[]{:S(2)}, u32[]{:S(2)}) collective-permute-start(f32[8,1024]{1,0:T(8,128)} %get-tuple-element.50), channel_id=1, source_target_pairs={{0,2},{1,3},{2,0},{3,1},{4,6},{5,7},{6,4},{7,5},{8,10},{9,11},{10,... | collective-permute-start | bytes 98312 | tf_op jit(solution)/shard_map/sum_norm_terms/ppermute | solution.py:25
  145.1 34.7 %collective-permute-start.22 = (f32[8,1024]{1,0:T(8,128)}, f32[8,1024]{1,0:T(8,128)S(1)}, u32[]{:S(2)}, u32[]{:S(2)}) collective-permute-start(f32[8,1024]{1,0:T(8,128)} %get-tuple-element.50), channel_id=1, source_target_pairs={{0,1},{1,2},{2,3},{3,0},{4,5},{5,6},{6,7},{7,4},{8,9},{9,10},{10,1... | collective-permute-start | bytes 98312 | tf_op jit(solution)/shard_map/sum_norm_terms/ppermute | solution.py:25
  166.0 56.3 %collective-permute-start.38 = (f32[8,1024]{1,0:T(8,128)}, f32[8,1024]{1,0:T(8,128)S(1)}, u32[]{:S(2)}, u32[]{:S(2)}) collective-permute-start(f32[8,1024]{1,0:T(8,128)} %get-tuple-element.56), channel_id=1, source_target_pairs={{0,3},{1,0},{2,1},{3,2},{4,7},{5,4},{6,5},{7,6},{8,11},{9,8},{10,9... | collective-permute-start | bytes 98312 | tf_op jit(solution)/shard_map/sum_norm_terms/ppermute | solution.py:25
  168.4 55.4 %collective-permute-start.37 = (f32[8,1024]{1,0:T(8,128)}, f32[8,1024]{1,0:T(8,128)S(1)}, u32[]{:S(2)}, u32[]{:S(2)}) collective-permute-start(f32[8,1024]{1,0:T(8,128)} %get-tuple-element.56), channel_id=1, source_target_pairs={{0,2},{1,3},{2,0},{3,1},{4,6},{5,7},{6,4},{7,5},{8,10},{9,11},{10,... | collective-permute-start | bytes 98312 | tf_op jit(solution)/shard_map/sum_norm_terms/ppermute | solution.py:25
  179.8 45.4 %collective-permute-start.36 = (f32[8,1024]{1,0:T(8,128)S(1)}, f32[8,1024]{1,0:T(8,128)S(1)}, u32[]{:S(2)}, u32[]{:S(2)}) collective-permute-start(f32[8,1024]{1,0:T(8,128)S(1)} %copy-done.67), channel_id=1, source_target_pairs={{0,1},{1,2},{2,3},{3,0},{4,5},{5,6},{6,7},{7,4},{8,9},{9,10},{10,1... | collective-permute-start | bytes 98312 | tf_op jit(solution)/shard_map/sum_norm_terms/ppermute | solution.py:25
  216.5 102.5 %collective-permute-start.45 = (f32[512,128]{0,1:T(8,128)}, f32[512,128]{0,1:T(8,128)}, u32[]{:S(2)}, u32[]{:S(2)}) collective-permute-start(f32[512,128]{0,1:T(8,128)} %get-tuple-element.160), channel_id=1, source_target_pairs={{0,1},{1,2},{2,3},{3,0},{4,5},{5,6},{6,7},{7,4},{8,9},{9,10},{10,1... | collective-permute-start | bytes 786440 | tf_op jit(solution)/shard_map/sum_writer_reader_grad/ppermute | solution.py:25
  217.6 102.3 %collective-permute-start.47 = (f32[512,128]{0,1:T(8,128)}, f32[512,128]{0,1:T(8,128)}, u32[]{:S(2)}, u32[]{:S(2)}) collective-permute-start(f32[512,128]{0,1:T(8,128)} %get-tuple-element.161), channel_id=1, source_target_pairs={{0,3},{1,0},{2,1},{3,2},{4,7},{5,4},{6,5},{7,6},{8,11},{9,8},{10,9... | collective-permute-start | bytes 786440 | tf_op jit(solution)/shard_map/sum_writer_reader_grad/ppermute | solution.py:25
  222.3 99.6 %collective-permute-start.46 = (f32[512,128]{0,1:T(8,128)}, f32[512,128]{0,1:T(8,128)}, u32[]{:S(2)}, u32[]{:S(2)}) collective-permute-start(f32[512,128]{0,1:T(8,128)} %get-tuple-element.162), channel_id=1, source_target_pairs={{0,2},{1,3},{2,0},{3,1},{4,6},{5,7},{6,4},{7,5},{8,10},{9,11},{10,... | collective-permute-start | bytes 786440 | tf_op jit(solution)/shard_map/sum_writer_reader_grad/ppermute | solution.py:25
  223.8 65.2 %collective-permute-start.44 = (bf16[256,384]{1,0:T(8,128)(2,1)}, bf16[256,384]{1,0:T(8,128)(2,1)}, u32[]{:S(2)}, u32[]{:S(2)}) collective-permute-start(bf16[256,384]{1,0:T(8,128)(2,1)} %get-tuple-element.166), channel_id=1, source_target_pairs={{0,1},{1,2},{2,3},{3,0},{4,5},{5,6},{6,7},{7,4},{8,9},{9,10},{10,1... | collective-permute-start | bytes 589832 | tf_op jit(solution)/shard_map/send_value_grad/ppermute | solution.py:25
  225.2 54.8 %collective-permute-start.42 = (bf16[256,384]{1,0:T(8,128)(2,1)}, bf16[256,384]{1,0:T(8,128)(2,1)}, u32[]{:S(2)}, u32[]{:S(2)}) collective-permute-start(bf16[256,384]{1,0:T(8,128)(2,1)} %get-tuple-element.169), channel_id=1, source_target_pairs={{0,3},{1,0},{2,1},{3,2},{4,7},{5,4},{6,5},{7,6},{8,11},{9,8},{10,9... | collective-permute-start | bytes 589832 | tf_op jit(solution)/shard_map/send_value_grad/ppermute | solution.py:25
  289.0 41.0 %collective-permute-start.54 = (f32[512,128]{0,1:T(8,128)}, f32[512,128]{0,1:T(8,128)}, u32[]{:S(2)}, u32[]{:S(2)}) collective-permute-start(f32[512,128]{0,1:T(8,128)} %get-tuple-element.163), channel_id=1, source_target_pairs={{0,1},{1,2},{2,3},{3,0},{4,5},{5,6},{6,7},{7,4},{8,9},{9,10},{10,1... | collective-permute-start | bytes 786440 | tf_op jit(solution)/shard_map/sum_writer_reader_grad/ppermute | solution.py:25
  319.9 120.8 %collective-permute-start.27 = (bf16[256,768]{1,0:T(8,128)(2,1)}, bf16[256,768]{1,0:T(8,128)(2,1)S(1)}, u32[]{:S(2)}, u32[]{:S(2)}) collective-permute-start(bf16[256,768]{1,0:T(8,128)(2,1)} %get-tuple-element.152), channel_id=1, source_target_pairs={{0,1},{1,2},{2,3},{3,0},{4,5},{5,6},{6,7},{7,4},{8,9},{9,10},{10,1... | collective-permute-start | bytes 1179656 | tf_op jit(solution)/shard_map/send_gate_parts/ppermute | solution.py:25
  321.9 115.4 %collective-permute-start.26 = (bf16[256,768]{1,0:T(8,128)(2,1)}, bf16[256,768]{1,0:T(8,128)(2,1)}, u32[]{:S(2)}, u32[]{:S(2)}) collective-permute-start(bf16[256,768]{1,0:T(8,128)(2,1)} %get-tuple-element.154), channel_id=1, source_target_pairs={{0,2},{1,3},{2,0},{3,1},{4,6},{5,7},{6,4},{7,5},{8,10},{9,11},{10,... | collective-permute-start | bytes 1179656 | tf_op jit(solution)/shard_map/send_gate_parts/ppermute | solution.py:25
  361.5 74.0 %collective-permute-start.25 = (bf16[256,768]{1,0:T(8,128)(2,1)}, bf16[256,768]{1,0:T(8,128)(2,1)}, u32[]{:S(2)}, u32[]{:S(2)}) collective-permute-start(bf16[256,768]{1,0:T(8,128)(2,1)} %get-tuple-element.155), channel_id=1, source_target_pairs={{0,3},{1,0},{2,1},{3,2},{4,7},{5,4},{6,5},{7,6},{8,11},{9,8},{10,9... | collective-permute-start | bytes 1179656 | tf_op jit(solution)/shard_map/send_gate_parts/ppermute | solution.py:25
  365.1 119.4 %collective-permute-start.104 = (f32[4,48,768]{2,1,0:T(8,128)}, f32[4,48,768]{2,1,0:T(8,128)}, u32[]{:S(2)}, u32[]{:S(2)}) collective-permute-start(f32[4,48,768]{2,1,0:T(8,128)} %dynamic-slice_bitcast_fusion), channel_id=1, source_target_pairs={{0,4},{4,0},{1,5},{5,1},{2,6},{6,2},{3,7},{7,3},{8,12},{12,8},{9,1... | collective-permute-start | bytes 1769480 | tf_op jit(solution)/shard_map/sum_contract_grad/ppermute | solution.py:25
  426.8 62.3 %collective-permute-start.77 = (f32[4,4,24,384]{3,2,1,0:T(8,128)}, f32[4,4,24,384]{3,2,1,0:T(8,128)S(1)}, u32[]{:S(2)}, u32[]{:S(2)}) collective-permute-start(f32[4,4,24,384]{3,2,1,0:T(8,128)} %dynamic-slice_bitcast_fusion.1), channel_id=1, source_target_pairs={{0,4},{4,0},{1,5},{5,1},{2,6},{6,2},{3,7},{7,3},{8,12},{12,8},{9,1... | collective-permute-start | bytes 1769480 | tf_op jit(solution)/shard_map/sum_expand_grad_values/ppermute | solution.py:25
  (184 other events, 1581.5 us)
Sparse Core Ops, SparseCore 0:
  10.3 46.5 all-gather.2
  59.1 47.5 all-gather.4

commit v2 on v1

v2 whole, which is shorter than its diff:
```python
import functools

import jax
import jax.numpy as jnp
import numpy as np
from jax import lax
from jax.experimental import pallas as pl
from jax.experimental.pallas import tpu as pltpu
from jax.sharding import PartitionSpec as P

EPS = 1e-05
F32 = jnp.float32
BF16 = jnp.bfloat16
NN = (((1,), (0,)), ((), ()))
NT = (((1,), (1,)), ((), ()))
TN = (((0,), (0,)), ((), ()))
VMEM_LIMIT = 56 * 1024 * 1024


class Axes:
    def __init__(self, dims):
        self.size = dict(zip(("y", "x", "core"), dims))
        place = lax.axis_index("dp")
        y, x, core = dims
        self.place = {
            "y": place // (x * core),
            "x": (place // core) % x,
            "core": place % core,
            "rep": lax.axis_index("rep"),
        }
        self.size["rep"] = lax.axis_size("rep")

    def shift(self, v, axis, by):
        n = self.size[axis]
        if axis == "rep":
            return lax.ppermute(v, "rep", [(i, (i + by) % n) for i in range(n)])
        stride = {"core": 1, "x": self.size["core"], "y": self.size["core"] * self.size["x"]}[axis]
        route = []
        for i in range(lax.axis_size("dp")):
            at = (i // stride) % n
            route.append((i, i + ((at + by) % n - at) * stride))
        return lax.ppermute(v, "dp", route)

    def near_ring(self, v):
        return self.shift(v, "rep", 1), self.shift(v, "rep", -1)

    def far_ring(self, v, left, right):
        far = (self.shift(left[:1], "rep", 1), self.shift(right[1:], "rep", -1))
        return [v, right, left, far[0], far[1]]

    def exchange(self, v, axis="rep"):
        n = self.size[axis]
        if n == 1:
            return v
        if axis == "rep":
            return lax.all_to_all(v, "rep", 0, 0, tiled=True)
        stride = {"core": 1, "x": self.size["core"], "y": self.size["core"] * self.size["x"]}[axis]
        starts = [i for i in range(lax.axis_size("dp")) if (i // stride) % n == 0]
        groups = [[i + k * stride for k in range(n)] for i in starts]
        return lax.all_to_all(v, "dp", 0, 0, axis_index_groups=groups, tiled=True)

    def everywhere(self, v, axis="rep"):
        return self.exchange(jnp.broadcast_to(v[None], (self.size[axis],) + v.shape), axis)

    def block(self, v, axis, ahead, dim):
        index = (self.place[axis] + ahead) % self.size[axis]
        return lax.dynamic_index_in_dim(v, index, dim, keepdims=False)

    def scatter_sum(self, v, axis, dim):
        total = self.block(v, axis, 0, dim)
        for k in range(1, self.size[axis]):
            total = total + self.shift(self.block(v, axis, k, dim), axis, k)
        return total


def dot(a, b, dims=NN):
    return lax.dot_general(a, b, dims, preferred_element_type=F32)


def split(a):
    hi = a.astype(BF16)
    return hi, (a - hi.astype(F32)).astype(BF16)


def dot3(a, b, dims=NN):
    ah, al = split(a)
    bh, bl = split(b)
    return dot(ah, bh, dims) + (dot(ah, bl, dims) + dot(al, bh, dims))


def dot2(a, b, dims=NN):
    if a.dtype == BF16:
        bh, bl = split(b)
        return dot(a, bh, dims) + dot(a, bl, dims)
    ah, al = split(a)
    return dot(ah, b, dims) + dot(al, b, dims)


SLOT = 8


def three_pieces(v):
    hi = v.astype(BF16).astype(F32)
    rest = v - hi
    mid = rest.astype(BF16).astype(F32)
    low = (rest - mid).astype(BF16).astype(F32)
    return hi + pltpu.roll(mid, SLOT, 1) + pltpu.roll(low, 2 * SLOT, 1)


def triangle_sum(mask, v, heads):
    r = dot(jnp.where(mask, 1.0, 0.0).astype(BF16), three_pieces(v).astype(BF16))
    n = r.shape[1]
    r = r + (pltpu.roll(r, n - SLOT, 1) + pltpu.roll(r, n - 2 * SLOT, 1))
    lane = lax.broadcasted_iota(jnp.int32, r.shape, 1)
    return jnp.where(lane < heads, r, 0.0)


def by_channel(cum, step, spread):
    sh, sl = split(step)
    packed = three_pieces(cum) + (
        pltpu.roll(sh.astype(F32), 3 * SLOT, 1) + pltpu.roll(sl.astype(F32), 4 * SLOT, 1)
    )
    both = dot(packed.astype(BF16), spread)
    half = both.shape[1] // 2
    return both[:, :half], both[:, half:]


def sigmoid(v):
    return 1.0 / (1.0 + jnp.exp(-v))


def steps_of(sr, hp, heads):
    lane = lax.broadcasted_iota(jnp.int32, sr.shape, 1)
    moved = sr + hp[0:1]
    step = jnp.maximum(moved, 0.0) + jnp.log1p(jnp.exp(-jnp.abs(moved)))
    step = jnp.where(lane < heads, step, 0.0)
    return moved, step, -step * hp[1:2]


def triangle(q, lower):
    row = lax.broadcasted_iota(jnp.int32, (q, q), 0)
    col = lax.broadcasted_iota(jnp.int32, (q, q), 1)
    return (row >= col) if lower else (col >= row)


def contract_rows(front, rep, ch, width):
    start = rep * (ch // 2)
    if not isinstance(rep, int):
        start = pl.multiple_of(start, 16)
    pair = front[pl.ds(start, ch // 2), front.shape[1] - 2 * width :]
    return jnp.concatenate([pair[:, :width], pair[:, width:]], axis=0)


def beside(ref, parity, value, lead=None):
    half = value.shape[1]
    for odd in (0, 1):

        @pl.when(parity == odd)
        def _():
            if lead is None:
                ref[:, odd * half : odd * half + half] = value
            else:
                ref[lead, :, odd * half : odd * half + half] = value


def pick(out, source, m, near0, near1, near3, far0, far1):
    for index, ref in ((0, near0), (1, near1), (3, near3)):

        @pl.when(source == index)
        def _():
            out[...] = ref[0]

    for micro, ref in enumerate((far0, far1)):

        @pl.when((source == 2) & (m == micro))
        def _():
            out[...] = ref[0]


def forward_kernel(
    heads, reps, place, n0, n1, n3, n2a, n2b, b0, b1, b3, b2a, b2b, front, perm, fp, hp, cp, spread,
    nrm_o, bg_o, gate_o, sig_o, pre_o, y_o, oc_o, sr_o, sin_o, sums_o, pwr_o, swr_o,
    state, tail, co,
):
    q = nrm_o.shape[0]
    ch = cp.shape[1]
    cw = fp.shape[1]
    ns = (cw - ch) // 2
    wr = 2 * ns // reps
    size = ch // heads
    step_id = pl.program_id(0)
    block = step_id % reps
    rep = place[0]
    source = (block - rep + reps) % reps

    pick(nrm_o, source, step_id // reps, n0, n1, n3, n2a, n2b)
    pick(bg_o, source, step_id // reps, b0, b1, b3, b2a, b2b)

    @pl.when(step_id == 0)
    def _():
        co[...] = dot(perm[...], contract_rows(front, rep, ch, nrm_o.shape[1])).astype(BF16)

    @pl.when(block == 0)
    def _():
        state[...] = jnp.zeros_like(state)
        tail[...] = jnp.zeros_like(tail)

    proj = dot(nrm_o[...], front[:, : ch + cw + 128])
    gate = proj[:, :ch]
    signal = proj[:, ch : ch + cw]
    lane = lax.broadcasted_iota(jnp.int32, (q, 128), 1)
    sr = jnp.where(lane < heads, proj[:, ch + cw : ch + cw + 128], 0.0)
    ext = jnp.concatenate([tail[...], signal], axis=0)
    pre = fp[4:5, :] + jnp.zeros_like(signal)
    for k in range(4):
        pre = pre + fp[k : k + 1, :] * ext[5 + k : 5 + k + q]
    tail[...] = signal[q - 8 :]
    act = pre * sigmoid(pre)
    values = act[:, :ch]
    writer = act[:, ch : ch + ns]
    reader = act[:, ch + ns :]
    _, step, ld = steps_of(sr, hp[...], heads)
    lower = triangle(q, True)
    cum = triangle_sum(lower, ld, heads)
    cum_t = cum.T
    cum_e, step_e = by_channel(cum, step, spread[...])
    last_e = cum_e[q - 1 : q]
    xv = step_e * values
    scores = dot3(reader, writer, NT)
    parts = []
    for p in range(ch // 128):
        hi, lo = split(xv[:, 128 * p : 128 * p + 128])
        both = jnp.concatenate([hi, lo], axis=1)
        out = None
        for j in range(128 // size):
            h = p * (128 // size) + j
            decay = jnp.exp(cum[:, h : h + 1] - cum_t[h : h + 1, :])
            ph, plo = split(jnp.where(lower, scores * decay, 0.0))
            r = dot(ph, both)
            one = r[:, :128] + (r[:, 128:] + dot(plo, hi))
            out = one if out is None else jnp.where(lane < j * size, out, one)
        parts.append(out)
    inner = jnp.concatenate(parts, axis=1)
    old = state[...]
    sin_o[0] = old
    y = inner + jnp.exp(cum_e) * dot3(reader, old, NT) + cp[0:1, :] * values
    decay_ch = jnp.broadcast_to(jnp.exp(last_e), (ns, ch)).T
    state[...] = decay_ch * old + dot3(jnp.exp(last_e - cum_e) * xv, writer, TN)
    gated = y * (gate * sigmoid(gate))
    outcome = dot(bg_o[...], co[...], NT)
    ones = jnp.ones((8, ch), BF16)
    s1 = dot2(ones, gated * gated, NT)
    s2 = dot2(ones, outcome * cp[1:2, :] * gated, NT)
    row = lax.broadcasted_iota(jnp.int32, s1.shape, 0)
    both_sums = jnp.where(row == 0, s1, jnp.where(row == 1, s2, 0.0))
    for r in range(reps):
        sums_o[r] = both_sums
    gate_o[...] = gate
    sig_o[...] = signal[:, :ch]
    pre_o[...] = pre
    y_o[...] = y
    oc_o[...] = outcome
    sr_o[...] = sr
    for r in range(reps):

        @pl.when(rep == r)
        def _():
            beside(pwr_o, block % 2, pre[:, ch + r * wr : ch + r * wr + wr])
            beside(swr_o, block % 2, signal[:, ch + r * wr : ch + r * wr + wr])


def gate_kernel(
    width, ys, gate_r, y_r, oc_r, sums, bg, nrm, cp, send_o, early_o, dy_o, acc_o, cg
):
    q, ch = gate_r.shape
    dp = early_o.shape[0]
    rows = nrm.shape[1] // dp
    piece = (early_o.shape[1] - rows) // 2

    @pl.when(pl.program_id(0) == 0)
    def _():
        cg[...] = jnp.zeros_like(cg)
        early_o[...] = jnp.zeros_like(early_o)
        acc_o[...] = jnp.zeros_like(acc_o)

    s = jnp.sum(sums[...], axis=0)
    scale_row = lax.rsqrt(s[0:1] * (1.0 / width) + EPS)
    mean_row = scale_row * s[1:2] * (1.0 / width)

    def column(v):
        c = jnp.broadcast_to(v, (128, q)).T
        return jnp.concatenate([c] * (ch // 128), axis=1)

    scale = column(scale_row)
    mean = column(mean_row)
    gate = gate_r[...]
    y = y_r[...]
    outcome = oc_r[...]
    gain = cp[1:2, :]
    sg = sigmoid(gate)
    sl = gate * sg
    unit = y * sl * scale
    nout = (unit * gain).astype(BF16)
    cg[...] += dot(nout, bg[...], TN)
    gated_grad = scale * (outcome * gain - unit * mean)
    dy_o[...] = gated_grad * sl
    gg = (gated_grad * y * sg * (1.0 + gate * (1.0 - sg))).astype(BF16)
    early_o[:, :rows, :] += dot(nrm[...], gg, TN).reshape(dp, rows, ch)
    send_o[0, :, :ch] = nout
    send_o[0, :, ch:] = gg
    gain_part = jnp.sum(outcome * unit, axis=0, keepdims=True)
    row = lax.broadcasted_iota(jnp.int32, acc_o.shape, 0)
    acc_o[...] += jnp.where(row == 0, gain_part, 0.0)

    @pl.when(pl.program_id(0) == pl.num_programs(0) - 1)
    def _():
        half = bg.shape[1] // 2
        for d in range(dp):
            start = (d % (dp // ys)) * ys * piece + (d // (dp // ys)) * piece
            part = cg[start : start + piece, :]
            early_o[d, rows : rows + piece, :] = part[:, :half]
            early_o[d, rows + piece :, :] = part[:, half:]


def backward_kernel(
    heads, reps, sig_r, pre_r, y_r, dy_r, sr_r, sin_r, fp, hp, cp, spread, oh,
    vg_o, send_o, wr_o, raw_o, acc_o, hacc_o,
    adj, head_rows,
):
    q, ch = y_r.shape
    cw = fp.shape[1]
    ns = (cw - ch) // 2
    wr = 2 * ns // reps
    size = ch // heads
    block = reps - 1 - pl.program_id(0) % reps

    @pl.when(block == reps - 1)
    def _():
        adj[...] = jnp.zeros_like(adj)
        head_rows[...] = jnp.zeros_like(head_rows)

    @pl.when(pl.program_id(0) == 0)
    def _():
        acc_o[...] = jnp.zeros_like(acc_o)
        hacc_o[...] = jnp.zeros_like(hacc_o)

    pre = pre_r[...]
    sgm = sigmoid(pre)
    act = pre * sgm
    values = act[:, :ch]
    writer = act[:, ch : ch + ns]
    reader = act[:, ch + ns :]
    moved_raw, step, ld = steps_of(sr_r[...], hp[...], heads)
    lower = triangle(q, True)
    upper = triangle(q, False)
    cum = triangle_sum(lower, ld, heads)
    cum_t = cum.T
    cum_e, step_e = by_channel(cum, step, spread[...])
    last_e = cum_e[q - 1 : q]
    skip = cp[0:1, :]
    dy = dy_r[...]
    y = y_r[...]
    xv = step_e * values
    lane = lax.broadcasted_iota(jnp.int32, (q, 128), 1)
    scores = dot3(writer, reader, NT)
    dscores = jnp.zeros((q, q), F32)
    parts = []
    for p in range(ch // 128):
        dpair = dy[:, 128 * p : 128 * p + 128]
        xpair = xv[:, 128 * p : 128 * p + 128]
        dh, dl = split(dpair)
        dboth = jnp.concatenate([dh, dl], axis=1)
        dtwice = jnp.concatenate([dh, dh], axis=1)
        out = None
        for j in range(128 // size):
            h = p * (128 // size) + j
            decay = jnp.where(upper, jnp.exp(cum_t[h : h + 1, :] - cum[:, h : h + 1]), 0.0)
            ph, plo = split(scores * decay)
            r = dot(ph, dboth)
            one = r[:, :128] + (r[:, 128:] + dot(plo, dh))
            out = one if out is None else jnp.where(lane < j * size, out, one)
            mine = (lane >= j * size) & (lane < (j + 1) * size)
            xh, xl = split(jnp.where(mine, xpair, 0.0))
            m = dot(jnp.concatenate([xh, xl], axis=1), dtwice, NT) + dot(xh, dl, NT)
            dscores = dscores + m * decay
        parts.append(out)
    inner = jnp.concatenate(parts, axis=1)
    old = adj[...]
    sin = sin_r[0]
    ends = jnp.exp(last_e - cum_e)
    from_state = ends * dot3(writer, old, NT)
    dxv = inner + from_state
    cdy = jnp.exp(cum_e) * dy
    dwriter = dot3(dscores, reader) + dot3(ends * xv, old)
    dreader = dot3(dscores, writer, TN) + dot3(cdy, sin)
    decay_ch = jnp.broadcast_to(jnp.exp(last_e), (ns, ch)).T
    state_row = dot2(jnp.ones((8, ns), BF16), decay_ch * old * sin, NT)[0:1]
    last_row = state_row + jnp.sum(xv * from_state, axis=0, keepdims=True)
    adj[...] = decay_ch * old + dot3(cdy, reader, TN)

    dstep = dot2(values * dxv, oh[...], NT)
    row = lax.broadcasted_iota(jnp.int32, (q, ch), 0)
    dcum_ch = dy * (y - skip * values) - xv * dxv + jnp.where(row == q - 1, last_row, 0.0)
    dcum = dot2(dcum_ch, oh[...], NT)
    dld = triangle_sum(upper, dcum, heads)
    raw = (dstep - dld * hp[1:2]) * sigmoid(moved_raw)
    raw = jnp.where(lane < heads, raw, 0.0)
    raw_o[...] = jnp.concatenate([jnp.zeros((q, wr), F32), raw[:, : 128 - wr]], axis=1)
    hrow = lax.broadcasted_iota(jnp.int32, hacc_o.shape, 0)
    hacc_o[...] += jnp.where(
        hrow == 0,
        jnp.sum(raw, axis=0, keepdims=True),
        jnp.where(hrow == 1, jnp.sum(dld * ld, axis=0, keepdims=True), 0.0),
    )
    both = jnp.concatenate([dwriter, dreader], axis=1)
    for r in range(reps):
        beside(wr_o, block % 2, both[:, r * wr : r * wr + wr], r)

    sv = sgm[:, :ch]
    dpre = (step_e * dxv + skip * dy) * (sv * (1.0 + pre[:, :ch] * (1.0 - sv)))
    ext = jnp.concatenate([dpre, head_rows[...]], axis=0)
    head_rows[...] = dpre[:8]
    signal = sig_r[...]
    total = jnp.zeros_like(dpre)
    rows = []
    for k in range(4):
        moved = ext[3 - k : 3 - k + q]
        total = total + fp[k : k + 1, :ch] * moved
        rows.append(jnp.sum(moved * signal, axis=0, keepdims=True))
    vg = total.astype(BF16)
    vg_o[...] = vg
    send_o[0] = vg
    rows.append(jnp.sum(dpre, axis=0, keepdims=True))
    rows.append(jnp.sum(values * dy, axis=0, keepdims=True))
    rows.append(jnp.zeros((2, ch), F32))
    acc_o[...] += jnp.concatenate(rows, axis=0)


def tail_kernel(wr, got, pwr, swr, fw, raw, tail_o, send_o, acc_o):
    half = got.shape[1] // 2

    def line(v):
        return jnp.concatenate(
            [v[:half, :wr], v[:half, wr:], v[half:, :wr], v[half:, wr:]], axis=0
        )

    pre = pwr[...]
    s = sigmoid(pre)
    grads = jnp.sum(got[...], axis=0)
    dpre = line(grads * (s * (1.0 + pre * (1.0 - s))))
    signal = line(swr[...])
    total = jnp.zeros_like(dpre)
    ext = jnp.concatenate([dpre, jnp.zeros((8, wr), F32)], axis=0)
    rows = []
    n = dpre.shape[0]
    for k in range(4):
        moved = ext[3 - k : 3 - k + n]
        total = total + fw[k : k + 1, :] * moved
        rows.append(jnp.sum(moved * signal, axis=0, keepdims=True))
    rows.append(jnp.sum(dpre, axis=0, keepdims=True))
    rows.append(jnp.zeros((3, wr), F32))

    @pl.when(pl.program_id(0) == 0)
    def _():
        acc_o[...] = jnp.zeros_like(acc_o)

    acc_o[...] += jnp.concatenate(rows, axis=0)
    wide = jnp.concatenate([total, jnp.zeros((n, 128 - wr), F32)], axis=1)
    tail = (wide + raw[...]).astype(BF16)
    tail_o[...] = tail
    send_o[...] = tail.reshape(send_o.shape)


def mix_kernel(parts, front, perm, mask, residual, out):
    micro, q, width = residual.shape
    ch = perm.shape[0]
    totals = [0.0] * micro
    for k in range(parts.shape[0]):
        rows = contract_rows(front, k, ch, width)
        for m in range(micro):
            moved = dot(parts[k, :, 2 * m * ch : (2 * m + 1) * ch], perm[...]).astype(BF16)
            totals[m] = totals[m] + dot(moved, rows)
    for m in range(micro):
        out[m] = residual[m] + mask[m] * totals[m]


def first_kernel(parts, expand, out):
    micro = out.shape[0]
    reps = parts.shape[0]
    span = expand.shape[1] // reps
    ch = (span - 128) // 2
    totals = [0.0] * micro
    for k in range(reps):
        cols = expand[:, k * span : k * span + ch]
        for m in range(micro):
            totals[m] = totals[m] + dot(parts[k, :, (2 * m + 1) * ch : (2 * m + 2) * ch], cols, NT)
    for m in range(micro):
        out[m] = totals[m]


def last_kernel(part, parts, expand, residual, cotangent, gain, out, norm_o):
    micro, q, width = residual.shape
    reps = parts.shape[0]
    span = expand.shape[1] // reps
    ch = (span - 128) // 2
    totals = [part[m] for m in range(micro)]
    for k in range(reps):
        cols = expand[:, k * span + ch : (k + 1) * span]
        for m in range(micro):
            at = micro * ch + m * 128
            pg = jnp.concatenate([parts[k, :, m * ch : (m + 1) * ch], parts[k, :, at : at + 128]], axis=1)
            totals[m] = totals[m] + dot(pg, cols, NT)
    norm = jnp.zeros((1, width), F32)
    for m in range(micro):
        source = residual[m]
        scale = lax.rsqrt(jnp.mean(source * source, axis=-1, keepdims=True) + EPS)
        unit = source * scale
        norm = norm + jnp.sum(totals[m] * unit, axis=0, keepdims=True)
        scaled = totals[m] * gain[0:1]
        out[m] = cotangent[m] + scale * (
            scaled - unit * jnp.mean(scaled * unit, axis=-1, keepdims=True)
        )
    norm_o[...] = jnp.broadcast_to(norm, norm_o.shape)


def whole(shape):
    return pl.BlockSpec(shape, lambda *b: (0,) * len(shape))


def rows_of(q, width, order=lambda b: b):
    return pl.BlockSpec((q, width), lambda b: (order(b), 0))


SCALAR = pl.BlockSpec(memory_space=pltpu.SMEM)


def params(flops, nbytes, grid=True):
    kinds = dict(dimension_semantics=("arbitrary",)) if grid else {}
    return dict(
        compiler_params=pltpu.CompilerParams(vmem_limit_bytes=VMEM_LIMIT, **kinds),
        cost_estimate=pl.CostEstimate(flops=flops, bytes_accessed=nbytes, transcendentals=0),
    )


def body(
    dims,
    residual, lengths, norm_gain, expand, filters, offsets, gate_gain, contract,
    step_bias, decay_log, skip_gain, cotangent,
):
    ax = Axes(dims)
    micro, _, q, width = residual.shape
    heads_all = step_bias.shape[0]
    reps = lax.axis_size("rep")
    heads = heads_all // reps
    dp = lax.axis_size("dp")
    inner = contract.shape[0] * dp
    ch = inner // reps
    conv = filters.shape[0] * dp
    ns = (conv - inner) // 2
    cw = ch + 2 * ns
    size = inner // heads_all
    total = q * reps
    rep = lax.axis_index("rep")
    rows = expand.shape[0]
    wr = 2 * ns // reps
    sds = jax.ShapeDtypeStruct
    residual = residual[:, 0]
    cotangent = cotangent[:, 0]
    place = rep.astype(jnp.int32).reshape(1)

    def own(a, start, count, dim=-1):
        return lax.dynamic_slice_in_dim(a, start + rep * count, count, a.ndim + dim)

    position = rep * q + jnp.arange(q, dtype=jnp.int32)
    mask = (position[None, :] < lengths[:, :1]).astype(F32)[..., None]
    branch_grad = (mask * cotangent).astype(BF16)

    branch_grad, expand, contract = lax.optimization_barrier((branch_grad, expand, contract))

    half = contract.shape[0] // 2
    front = jnp.concatenate(
        [
            own(expand, 0, ch),
            own(expand, inner, ch),
            expand[:, 2 * inner : 2 * inner + 2 * ns],
            jnp.pad(own(expand, 2 * inner + 2 * ns, heads), ((0, 0), (0, 128 - heads))),
            contract[:half],
            contract[half:],
        ],
        axis=1,
    )
    w_width = ch + cw + 128
    with jax.named_scope("gather_own_expand"):
        front = lax.all_gather(front, "dp", axis=0, tiled=True)
    order = np.arange(ch).reshape(-1, 2, half).transpose(1, 0, 2).reshape(-1)
    perm = np.zeros((ch, ch), np.float32)
    perm[order, np.arange(ch)] = 1.0
    perm = jnp.asarray(perm, BF16)
    small = jnp.concatenate([norm_gain, filters.reshape(-1), offsets, gate_gain])
    sizes = np.cumsum([0, norm_gain.shape[0], filters.size, offsets.shape[0], gate_gain.shape[0]])
    padded = -(-small.shape[0] // 128) * 128
    small = jnp.pad(small, (0, padded - small.shape[0])).reshape(-1, 128)
    with jax.named_scope("gather_small"):
        small, branch_grad = lax.optimization_barrier((small, branch_grad))
        small = jnp.broadcast_to(small[None], (dp,) + small.shape)
        small = lax.all_to_all(small, "dp", 0, 0, tiled=True).reshape(dp, padded).astype(F32)
    with jax.named_scope("gather_branch_grad"):
        bg_near = ax.near_ring(branch_grad)
    gain_one = small[:, sizes[0] : sizes[1]].reshape(1, width)
    filters_full = small[:, sizes[1] : sizes[2]].reshape(conv, 4).T
    offsets_full = small[:, sizes[2] : sizes[3]].reshape(1, conv)
    gain_two = small[:, sizes[3] : sizes[4]].reshape(1, inner)

    scale_one = lax.rsqrt(jnp.mean(residual * residual, axis=-1, keepdims=True) + EPS)
    normed = (residual * scale_one * gain_one).astype(BF16)
    normed, expand, bg_near = lax.optimization_barrier((normed, expand, bg_near))
    with jax.named_scope("gather_normed"):
        nrm_ring = ax.far_ring(normed, *ax.near_ring(normed))
    with jax.named_scope("gather_branch_grad"):
        bg_ring = ax.far_ring(branch_grad, *bg_near)
    expand_cols = jnp.concatenate(
        [
            expand[:, :inner].reshape(rows, reps, ch),
            expand[:, inner : 2 * inner].reshape(rows, reps, ch),
            expand[:, 2 * inner : 2 * inner + 2 * ns].reshape(rows, reps, wr),
            expand[:, 2 * inner + 2 * ns :].reshape(rows, reps, heads),
            jnp.zeros((rows, reps, 128 - wr - heads), BF16),
        ],
        axis=2,
    ).reshape(rows, reps * (2 * ch + 128))
    with jax.named_scope("gather_expand"):
        expand_full = lax.all_gather(expand_cols, "dp", axis=0, tiled=True)

    own_filters = jnp.concatenate(
        [own(filters_full[:, :inner], 0, ch), filters_full[:, inner:]], axis=1
    )
    own_offsets = jnp.concatenate(
        [own(offsets_full[:, :inner], 0, ch), offsets_full[:, inner:]], axis=1
    )
    fp = jnp.concatenate([own_filters, own_offsets, jnp.zeros((3, cw), F32)], axis=0)
    own_skip = own(skip_gain, 0, heads)
    cp = jnp.concatenate(
        [jnp.repeat(own_skip, size)[None], own(gain_two, 0, ch), jnp.zeros((6, ch), F32)], axis=0
    )
    rate = jnp.exp(own(decay_log, 0, heads))
    hp = jnp.pad(jnp.stack([own(step_bias, 0, heads), rate]), ((0, 6), (0, 128 - heads)))
    onehot = np.zeros((128, ch), np.float32)
    onehot[np.arange(ch) // size, np.arange(ch)] = 1.0
    spread_of = np.zeros((128, 2 * ch), np.float32)
    for piece in range(5):
        spread_of[piece * SLOT : (piece + 1) * SLOT, (piece // 3) * ch : (piece // 3 + 1) * ch] = onehot[:SLOT]
    onehot = jnp.asarray(onehot, BF16)
    spread_of = jnp.asarray(spread_of, BF16)

    piece = pl.BlockSpec((1, q, width), lambda b: (b // reps, 0, 0))
    ring_specs = [piece, piece, piece, whole((1, q, width)), whole((1, q, width))]
    both = micro * total
    aside = pl.BlockSpec((q, 128), lambda b: (b // 2, 0))
    kept = pl.pallas_call(
        functools.partial(forward_kernel, heads, reps),
        grid=(micro * reps,),
        in_specs=[SCALAR] + ring_specs * 2 + [
            whole(front.shape), whole((ch, ch)),
            whole((8, cw)), whole((8, 128)), whole((8, ch)), whole((128, 2 * ch)),
        ],
        out_specs=[
            rows_of(q, width), rows_of(q, width),
            rows_of(q, ch), rows_of(q, ch), rows_of(q, cw), rows_of(q, ch), rows_of(q, ch),
            rows_of(q, 128), pl.BlockSpec((1, ch, ns), lambda b: (b, 0, 0)),
            pl.BlockSpec((reps, 8, q), lambda b: (0, 0, b)), aside, aside,
        ],
        out_shape=[
            sds((both, width), BF16), sds((both, width), BF16),
            sds((both, ch), F32), sds((both, ch), F32), sds((both, cw), F32),
            sds((both, ch), F32), sds((both, ch), F32), sds((both, 128), F32),
            sds((micro * reps, ch, ns), F32), sds((reps, 8, both), F32),
            sds((both // 2, 2 * wr), F32), sds((both // 2, 2 * wr), F32),
        ],
        scratch_shapes=[
            pltpu.VMEM((ch, ns), F32), pltpu.VMEM((8, cw), F32), pltpu.VMEM((ch, width), BF16),
        ],
        name="scan_forward",
        **params(40_000_000_000, 40_000_000),
    )(place, *nrm_ring, *bg_ring, front, perm, fp, hp, cp, spread_of)
    nrm, bg, gate, signal, pre, y, outcome, sr, sin, sums, pwr, swr = kept
    with jax.named_scope("sum_norm_terms"):
        sums, expand_full = lax.optimization_barrier((ax.exchange(sums), expand_full))

    strip = pl.BlockSpec((reps, 8, q), lambda b: (0, 0, b))
    ys = ax.size["y"]
    wide = width // 2
    early_rows = rows + 2 * (contract.shape[0] // ys)
    send, early, dy, gain_part = pl.pallas_call(
        functools.partial(gate_kernel, inner, ys),
        grid=(micro * reps,),
        in_specs=[rows_of(q, ch)] * 3 + [strip] + [rows_of(q, width)] * 2 + [whole((8, ch))],
        out_specs=[
            pl.BlockSpec((1, q, 2 * ch), lambda b: (b % reps, 0, b // reps)),
            whole((dp, early_rows, ch)), rows_of(q, ch), whole((8, ch)),
        ],
        out_shape=[
            sds((reps, q, micro * 2 * ch), BF16), sds((dp, early_rows, ch), F32),
            sds((both, ch), F32), sds((8, ch), F32),
        ],
        scratch_shapes=[pltpu.VMEM((ch, width), F32)],
        name="gate_backward",
        **params(8_000_000_000, 20_000_000),
    )(gate, y, outcome, sums, bg, nrm, cp)
    with jax.named_scope("early_sums"):
        early = lax.psum_scatter(early, "dp", scatter_dimension=0)

    with jax.named_scope("send_gate_parts"):
        a_parts = ax.exchange(send)
    def back(b):
        return b // reps * reps + reps - 1 - b % reps

    value_grads, v_send, wrg, raws, channel_part, head_part = pl.pallas_call(
        functools.partial(backward_kernel, heads, reps),
        grid=(micro * reps,),
        in_specs=[
            rows_of(q, ch, back), rows_of(q, cw, back), rows_of(q, ch, back), rows_of(q, ch, back),
            rows_of(q, 128, back), pl.BlockSpec((1, ch, ns), lambda b: (back(b), 0, 0)),
            whole((8, cw)), whole((8, 128)), whole((8, ch)), whole((128, 2 * ch)), whole((128, ch)),
        ],
        out_specs=[
            rows_of(q, ch, back),
            pl.BlockSpec((1, q, ch), lambda b: (back(b) % reps, 0, b // reps)),
            pl.BlockSpec((reps, q, 2 * wr), lambda b: (0, back(b) // 2, 0)),
            rows_of(q, 128, back), whole((8, ch)), whole((8, 128)),
        ],
        out_shape=[
            sds((both, ch), BF16), sds((reps, q, micro * ch), BF16),
            sds((reps, both // 2, 2 * wr), F32),
            sds((both, 128), F32), sds((8, ch), F32), sds((8, 128), F32),
        ],
        scratch_shapes=[pltpu.VMEM((ch, ns), F32), pltpu.VMEM((8, ch), F32)],
        name="scan_backward",
        **params(80_000_000_000, 40_000_000),
    )(signal, pre, y, dy, sr, sin, fp, hp, cp, spread_of, onehot)
    with jax.named_scope("sum_writer_reader_grad"):
        a_parts, wrg = lax.optimization_barrier((a_parts, wrg))
        wr_got = ax.exchange(wrg)
    vmem = pl.BlockSpec(memory_space=pltpu.VMEM)
    mixed = pl.pallas_call(
        mix_kernel,
        in_specs=[vmem] * 5,
        out_specs=vmem,
        out_shape=sds(residual.shape, F32),
        name="mixed",
        **params(1_200_000_000, 8_000_000, False),
    )(a_parts, front, perm, mask, residual)
    first = pl.pallas_call(
        first_kernel,
        in_specs=[vmem] * 2,
        out_specs=vmem,
        out_shape=sds(residual.shape, F32),
        name="normed_grad_gate",
        **params(1_200_000_000, 8_000_000, False),
    )(a_parts, expand_full)
    with jax.named_scope("late_sums"):
        eg_values = lax.dot_general(nrm, value_grads, TN, preferred_element_type=F32)
    first, mixed, eg_values, wr_got = lax.optimization_barrier((first, mixed, eg_values, wr_got))
    fw = jnp.pad(own(filters_full[:, inner:], 0, wr), ((0, 4), (0, 0)))
    strip = pl.BlockSpec((total // 2, 2 * wr), lambda m: (m, 0))
    tails, t_send, wr_part = pl.pallas_call(
        functools.partial(tail_kernel, wr),
        grid=(micro,),
        in_specs=[
            pl.BlockSpec((reps, total // 2, 2 * wr), lambda m: (0, m, 0)), strip, strip,
            whole((8, wr)), rows_of(total, 128),
        ],
        out_specs=[
            rows_of(total, 128), pl.BlockSpec((reps, q, 128), lambda m: (0, 0, m)), whole((8, wr)),
        ],
        out_shape=[
            sds((both, 128), BF16), sds((reps, q, micro * 128), BF16), sds((8, wr), F32),
        ],
        name="writer_reader_grad",
        **params(100_000_000, 6_000_000),
    )(wr_got, pwr, swr, fw, raws)
    with jax.named_scope("send_values"):
        v_parts = ax.exchange(jnp.concatenate([v_send, t_send], axis=2))

    def spread(a, whole_width):
        blank = jnp.zeros((a.shape[0], whole_width), F32)
        return lax.dynamic_update_slice_in_dim(blank, a, rep * a.shape[1], 1)

    with jax.named_scope("late_sums"):
        taps = jnp.concatenate([spread(channel_part[:5], inner), spread(wr_part[:5], 2 * ns)], axis=1)
        own_heads = jnp.stack(
            [
                head_part[0, :heads],
                head_part[1, :heads],
                jnp.sum(channel_part[5].reshape(heads, size), axis=1),
            ]
        )
        heads_part = jnp.broadcast_to(spread(own_heads, heads_all).reshape(1, -1), (dp, 3 * heads_all))
        per = conv // dp
        flat = jnp.concatenate(
            [
                jnp.transpose(taps.reshape(5, dp, per), (1, 0, 2)).reshape(dp, 5 * per),
                spread(gain_part[:1], inner).reshape(dp, -1),
                heads_part,
            ],
            axis=1,
        )
        cuts = np.cumsum([0, 5 * per, inner // dp, 3 * heads_all])
        block = ch + 128
        spare = 56
        flat = jnp.pad(flat, ((0, 0), (0, rows * spare - flat.shape[1]))).reshape(dp, rows, spare)
        flat = jnp.pad(flat, ((0, 0), (0, 0), (128 - spare, 0)))
        eg_tail = lax.dot_general(nrm, tails, TN, preferred_element_type=F32)
        early, eg_tail = lax.optimization_barrier((early, eg_tail))
        late = jnp.concatenate(
            [eg_values.reshape(dp, rows, ch), eg_tail.reshape(dp, rows, 128) + flat], axis=2
        )
        late = late.reshape(dims + late.shape[1:])
        late = ax.scatter_sum(late, "core", 2)
        late = ax.scatter_sum(late, "x", 1)
        late = ax.scatter_sum(late, "y", 0)
    with jax.named_scope("last_gather"):
        late, v_parts = lax.optimization_barrier((late, v_parts))
        eg_gate = early[:rows]
        cgs = early[rows:]
        if ys == reps:
            turn = [(a * (dp // ys) + e) * reps + b for a in range(ys) for e in range(dp // ys) for b in range(reps)]
            to = [(b * (dp // ys) + e) * reps + a for a in range(ys) for e in range(dp // ys) for b in range(reps)]
            cgs = lax.ppermute(cgs, ("dp", "rep"), list(zip(turn, to)))
        packed = jnp.concatenate([eg_gate.reshape(-1, 128), cgs.reshape(-1, 128), late.reshape(-1, 128)], axis=0)
    residual_grad, norm_part = pl.pallas_call(
        last_kernel,
        in_specs=[vmem] * 6,
        out_specs=[vmem] * 2,
        out_shape=[sds(residual.shape, F32), sds((8, width), F32)],
        name="residual_grad",
        **params(2_000_000_000, 15_000_000, False),
    )(first, v_parts, expand_full, residual, cotangent, gain_one)
    with jax.named_scope("sum_norm_grad"):
        spread_norm = norm_part[:1].reshape(dp, 1, -1)
        spread_norm = jnp.pad(spread_norm, ((0, 0), (0, 0), (0, -spread_norm.shape[2] % 128)))
        norm_sum = jnp.sum(lax.all_to_all(spread_norm, "dp", 0, 0, tiled=True), axis=0)
        norm_sum = jnp.pad(norm_sum.reshape(-1, 128), ((0, -norm_sum.size // 128 % 8), (0, 0)))
    with jax.named_scope("last_gather"):
        got = ax.everywhere(jnp.concatenate([packed, norm_sum], axis=0))
    mark = rows * ch // 128
    eg_gate = got[:, :mark].reshape(reps, rows, ch)
    cgs = got[:, mark : 2 * mark].reshape(reps, 2, -1, wide)
    late = got[:, 2 * mark : packed.shape[0]].reshape(reps, rows, block)
    norm_grad = jnp.sum(got[:, packed.shape[0] :], axis=0).reshape(-1)[: width // dp]
    contract_grad = jnp.concatenate([cgs[:, 0], cgs[:, 1]], axis=2).reshape(-1, width)
    expand_grad = jnp.concatenate(
        [eg_gate[s] for s in range(reps)]
        + [late[s, :rows, :ch] for s in range(reps)]
        + [late[s, :rows, ch : ch + wr] for s in range(reps)]
        + [late[s, :rows, ch + wr : ch + wr + heads] for s in range(reps)],
        axis=1,
    )
    flat = jnp.sum(late[:, :, block - spare :], axis=0).reshape(-1)
    own_taps = flat[: cuts[1]].reshape(5, per)
    gain_grad = flat[cuts[1] : cuts[2]]
    by_head = flat[cuts[2] : cuts[3]].reshape(3, heads_all)
    return (
        mixed[:, None],
        residual_grad[:, None],
        norm_grad,
        expand_grad,
        own_taps[:4].T,
        own_taps[4],
        gain_grad,
        contract_grad,
        by_head[0],
        by_head[1],
        by_head[2],
    )


def solution(mesh):
    dp, rep = mesh.devices.shape
    core = 2 if dp % 8 == 0 else 1
    dims = (rep, dp // (core * rep), core)
    rows = P(None, "dp", "rep", None)
    in_specs = (
        rows, P(None, "dp"), P("dp"), P("dp", None), P("dp", None), P("dp"), P("dp"), P("dp", None),
        P(), P(), P(), rows,
    )
    out_specs = (
        rows, rows, P("dp"), P("dp", None), P("dp", None), P("dp"), P("dp"), P("dp", None),
        P(), P(), P(),
    )
    return jax.shard_map(
        functools.partial(body, dims), mesh=mesh, in_specs=in_specs, out_specs=out_specs, check_vma=False
    )
```

time: 601 us -> 305 us (0.51); the launches traced: 589 us -> 303 us
  starting transfers between devices: 154 us -> 51 us
  local copies, waits for them, and re-layouts: 123 us -> 24.8 us
  waiting for transfers between devices: 135 us -> 52.1 us
  other arithmetic: 37.6 us -> 13 us
  blocking collectives: 0 us -> 22.8 us
  Pallas kernels: 104 us -> 117 us
  matrix products: 17.7 us -> 7.99 us
    ppermute x115 -> x16, starting transfers between devices: 154 us -> 25.1 us  [the longest x8 14.1 us: shift(): return lax.ppermute(v, 'rep', [(i, (i + by) % n) for i in range(n)])]
    ppermute x115 -> x16, waiting for transfers between devices: 135 us -> 30.6 us  [the longest x8 21.4 us: shift(): return lax.ppermute(v, 'rep', [(i, (i + by) % n) for i in range(n)])]
    unnamed x278 -> x70, local copies, waits for them, and re-layouts: 34.3 us -> 7.82 us
    all_to_all x0 -> x5, starting transfers between devices: none -> 25.6 us  [the longest x3 12.8 us: exchange(): return lax.all_to_all(v, 'rep', 0, 0, tiled=True)]
    all_to_all x0 -> x2, blocking collectives: none -> 22.8 us  [exchange(): return lax.all_to_all(v, 'rep', 0, 0, tiled=True)]
    all_to_all x0 -> x5, waiting for transfers between devices: none -> 18.1 us  [the longest x1 7.23 us: body(): lax.all_to_all(spread_norm, 'dp', 0, 0, tiled=True)]
    squeeze x30 -> x11, local copies, waits for them, and re-layouts: 18.5 us -> 0.8 us  [the longest x1 0.51 us: body(): own_taps[4]]
    add x28 -> x4, other arithmetic: 17.1 us -> 3.71 us  [the longest x3 2.28 us: scatter_sum(): total = total + self.shift(self.block(v, axis, k, dim), axis, k)]
  transfers between devices with their start and end apart: 117 -> 24, of which waited for: 47 -> 14; matrix products, arithmetic and copies ran while one was open for 28% -> 10% of each run, Pallas kernels for 18% -> 34%
where the time goes in v2:
time: 305 us; the launch traced here: 303 us
  Pallas kernels  117 us (38%)
  waiting for transfers between devices  52.1 us (17%)
  starting transfers between devices  51 us (17%)
  local copies, waits for them, and re-layouts  24.8 us (8%)
  blocking collectives  22.8 us (7%)
  between operations  14.6 us (5%)
  other arithmetic  13 us (4%)
  matrix products  7.99 us (3%)
    pallas_call x1, Pallas kernels, body(): pl.pallas_call(functools.partial(backward_kernel, heads, reps), grid=(mic...  41.8 us
    pallas_call x1, Pallas kernels, body(): pl.pallas_call(functools.partial(forward_kernel, heads, reps), grid=(micr...  34.9 us
    all_to_all x2, blocking collectives, exchange(): return lax.all_to_all(v, 'rep', 0, 0, tiled=True)  22.8 us
    ppermute x8, waiting for transfers between devices, shift(): return lax.ppermute(v, 'rep', [(i, (i + by) % n) for i in range(n)])  21.4 us
    ppermute x8, starting transfers between devices, shift(): return lax.ppermute(v, 'rep', [(i, (i + by) % n) for i in range(n)])  14.1 us
    pallas_call x1, Pallas kernels, body(): pl.pallas_call(functools.partial(gate_kernel, inner, ys), grid=(micro * r...  13.5 us
    all_to_all x3, starting transfers between devices, exchange(): return lax.all_to_all(v, 'rep', 0, 0, tiled=True)  12.8 us
    ppermute x7, starting transfers between devices, shift(): return lax.ppermute(v, 'dp', route)  10.1 us
  transfers between devices with their start and end apart: 24, of which 14 were waited for; matrix products, arithmetic and copies ran while one was open for 10% of the time, Pallas kernels for 34%

profile of v2, /device:TPU:0, one launch (start us, length us, event | category | flops | bytes accessed | tf_op | source)
XLA Modules:
  0.0 303.4 jit_solution(5670156828799313260)
XLA Ops:
  16.0 7.3 %all-to-all-start = ((bf16[32,3,128]{2,1,0:T(4,128)(2,1)}), bf16[32,3,128]{2,1,0:T(4,128)(2,1)S(1)}, u32[]{:S(2)}, u32[]{:S(2)}) async-start(bf16[32,3,128]{2,1,0:T(4,128)(2,1)} %broadcast_in_dim.52), calls=%async_computation | async-start | bytes 65536 | tf_op jit(solution)/shard_map/gather_small/all_to_all | solution.py:606
  23.6 7.2 %all-to-all-done = bf16[32,3,128]{2,1,0:T(4,128)(2,1)S(1)} async-done(((bf16[32,3,128]{2,1,0:T(4,128)(2,1)}), bf16[32,3,128]{2,1,0:T(4,128)(2,1)S(1)}, u32[]{:S(2)}, u32[]{:S(2)}) %all-to-all-start) | async-done | bytes 24608 | tf_op jit(solution)/shard_map/gather_small/all_to_all | solution.py:606
  41.8 3.3 %collective-permute-start.7 = (bf16[1,256,768]{2,1,0:T(8,128)(2,1)S(1)}, bf16[1,256,768]{2,1,0:T(8,128)(2,1)S(1)}, u32[]{:S(2)}, u32[]{:S(2)}) collective-permute-start(bf16[1,256,768]{2,1,0:T(8,128)(2,1)S(1)} %slice.196), channel_id=1, source_target_pairs={{0,3},{1,0},{2,1},{3,2},{4,7},{5,4},{6,5},{7,6},{8,11},{9,8},{10,9... | collective-permute-start | bytes 1179656 | tf_op jit(solution)/shard_map/gather_branch_grad/ppermute | solution.py:36
  45.1 10.8 %collective-permute-done.3.n3 = bf16[2,256,768]{2,1,0:T(8,128)(2,1)S(1)} collective-permute-done((bf16[2,256,768]{2,1,0:T(8,128)(2,1)S(1)}, bf16[2,256,768]{2,1,0:T(8,128)(2,1)S(1)}, u32[]{:S(2)}, u32[]{:S(2)}) %collective-permute-start.3) | collective-permute-done | bytes 786464 | tf_op jit(solution)/shard_map/gather_normed/ppermute | solution.py:36
  57.2 3.1 %collective-permute-start.5 = (bf16[1,256,768]{2,1,0:T(8,128)(2,1)S(1)}, bf16[1,256,768]{2,1,0:T(8,128)(2,1)S(1)}, u32[]{:S(2)}, u32[]{:S(2)}) collective-permute-start(bf16[1,256,768]{2,1,0:T(8,128)(2,1)S(1)} %slice.250), channel_id=1, source_target_pairs={{0,3},{1,0},{2,1},{3,2},{4,7},{5,4},{6,5},{7,6},{8,11},{9,8},{10,9... | collective-permute-start | bytes 1179656 | tf_op jit(solution)/shard_map/gather_normed/ppermute | solution.py:36
  64.4 6.6 %collective-permute-done.4.n2a = bf16[1,256,768]{2,1,0:T(8,128)(2,1)S(1)} collective-permute-done((bf16[1,256,768]{2,1,0:T(8,128)(2,1)S(1)}, bf16[1,256,768]{2,1,0:T(8,128)(2,1)S(1)}, u32[]{:S(2)}, u32[]{:S(2)}) %collective-permute-start.4) | collective-permute-done | bytes 393248 | tf_op jit(solution)/shard_map/gather_normed/ppermute | solution.py:36
  71.9 34.9 %scan_forward.1 = (bf16[2048,768]{1,0:T(8,128)(2,1)}, bf16[2048,768]{1,0:T(8,128)(2,1)}, f32[2048,384]{1,0:T(8,128)}, f32[2048,384]{1,0:T(8,128)}, f32[2048,640]...) custom-call(s32[1]{0:T(128)} %bitcast.place, ...), custom_call_target="tpu_custom_call" | custom-call | flops 40000000000 | bytes 40000000 | tf_op jit(solution)/shard_map/scan_forward/pallas_call | solution.py:659
  106.8 10.8 %all_to_all.35.sums = f32[4,8,2048]{2,1,0:T(8,128)} all-to-all(f32[4,8,2048]{2,1,0:T(8,128)} %get-tuple-element.70), channel_id=1, replica_groups=mesh['dp'=32,'rep'=4] {'rep'}, dimensions={0} | all-to-all | bytes 524288 | tf_op jit(solution)/shard_map/sum_norm_terms/all_to_all | solution.py:56
  117.6 13.5 %gate_backward.1 = (bf16[4,256,1536]{2,1,0:T(8,128)(2,1)}, f32[32,48,384]{2,1,0:T(8,128)}, f32[2048,384]{1,0:T(8,128)}, f32[8,384]{1,0:T(8,128)}) custom-call(f32[2048,384]{1,0:T(8,128)} %get-tuple-element.67.gate_r, f32[2048,384]{1,0:T(8,128)} %get-tuple-element.68.y_r, f32[2048,384]{1,0:T(8,128)} %get-tuple-element.69.oc_r, ...), custom_call_target="tpu_custom_call" | custom-call | flops 8000000000 | bytes 20000000 | tf_op jit(solution)/shard_map/gate_backward/pallas_call | solution.py:693
  131.1 3.7 %all-to-all-start.2 = ((bf16[4,256,1536]{2,1,0:T(8,128)(2,1)}), bf16[4,256,1536]{2,1,0:T(8,128)(2,1)S(1)}, u32[]{:S(2)}, u32[]{:S(2)}) async-start(bf16[4,256,1536]{2,1,0:T(8,128)(2,1)} %get-tuple-element.75), calls=%async_computation.2 | async-start | bytes 6291456 | tf_op jit(solution)/shard_map/send_gate_parts/all_to_all | solution.py:56
  135.6 41.8 %scan_backward.1 = (bf16[2048,384]{1,0:T(8,128)(2,1)}, bf16[4,256,768]{2,1,0:T(8,128)(2,1)}, f32[4,1024,128]{2,1,0:T(8,128)}, f32[2048,128]{1,0:T(8,128)}, f32[8,384]{1,0:T(8,128)}, /*index=5*/f32[8,128]{1,0:T(8,128)}) custom-call(f32[2048,384]{1,0:T(8,128)} %get-tuple-element.76.sig_r, f32[2048,640]{1,0:T(8,128)} %get-tuple-element.77.pre_r, ...), custom_call_target="tpu_custom_call" | custom-call | flops 80000000000 | bytes 40000000 | tf_op jit(solution)/shard_map/scan_backward/pallas_call | solution.py:717
  179.1 4.7 %all-to-all-start.3 = ((f32[4,1024,128]{2,1,0:T(8,128)}), f32[4,1024,128]{2,1,0:T(8,128)}, u32[]{:S(2)}, u32[]{:S(2)}) async-start(f32[4,1024,128]{2,1,0:T(8,128)} %get-tuple-element.85), calls=%async_computation.3 | async-start | bytes 4194304 | tf_op jit(solution)/shard_map/sum_writer_reader_grad/all_to_all | solution.py:56
  187.4 5.2 %fusion.22 = f32[768,384]{1,0:T(8,128)} fusion(bf16[2048,768]{1,0:T(8,128)(2,1)} %get-tuple-element.74.nrm, bf16[2048,384]{1,0:T(8,128)(2,1)} %get-tuple-element.84), kind=kOutput, calls=%fused_computation.89 | convolution fusion | flops 1207959552 | bytes 5898240 | tf_op jit(solution)/shard_map/late_sums/dot_general | solution.py:761
  192.6 6.5 %normed_grad_gate.1.part = f32[2,256,768]{2,1,0:T(8,128)} custom-call(bf16[4,256,1536]{2,1,0:T(8,128)(2,1)} %copy-done, bf16[768,3584]{1,0:T(8,128)(2,1)} %all-gather.5.cloned.1.call-done.expand), custom_call_target="tpu_custom_call" | custom-call | flops 1200000000 | bytes 8000000 | tf_op jit(solution)/shard_map/normed_grad_gate/pallas_call | solution.py:752
  199.1 7.8 %mixed.1 = f32[2,256,768]{2,1,0:T(8,128)} custom-call(bf16[4,256,1536]{2,1,0:T(8,128)(2,1)} %copy-done, bf16[768,2688]{1,0:T(8,128)(2,1)} %all-gather.3.cloned.1.call-done.front, bf16[384,384]{1,0:T(8,128)(2,1)} %constant.165.clone.perm, f32[2,256,1]{2,1,0:T(8,128)} %compare_convert_fusion.mask, f32[2,256,768]{2,1,0:T(8,128)} %bitcast.99), custom_call_target="tpu_custom_call" | custom-call | flops 1200000000 | bytes 8000000 | tf_op jit(solution)/shard_map/mixed/pallas_call | solution.py:744
  207.7 4.8 %writer_reader_grad.1 = (bf16[2048,128]{1,0:T(8,128)(2,1)}, bf16[4,256,256]{2,1,0:T(8,128)(2,1)}, f32[8,64]{1,0:T(8,128)}) custom-call(f32[4,1024,128]{2,1,0:T(8,128)} %all-to-all-done.3.got, f32[1024,128]{1,0:T(8,128)} %get-tuple-element.91.pwr, f32[1024,128]{1,0:T(8,128)} %get-tuple-element.92.swr, f32[8,64]{1,0:T(8,128)} %pad.35.fw, ...), custom_call_target="tpu_custom_call" | custom-call | flops 100000000 | bytes 6000000 | tf_op jit(solution)/shard_map/writer_reader_grad/pallas_call | solution.py:765
  225.1 4.4 %all-to-all-start.4 = ((bf16[4,256,1024]{2,1,0:T(8,128)(2,1)}), bf16[4,256,1024]{2,1,0:T(8,128)(2,1)S(1)}, u32[]{:S(2)}, u32[]{:S(2)}) async-start(bf16[4,256,1024]{2,1,0:T(8,128)(2,1)} %pad_maximum_fusion), calls=%async_computation.5 | async-start | bytes 4194304 | tf_op jit(solution)/shard_map/send_values/all_to_all | solution.py:56
  237.2 3.9 %collective-permute-done.10 = f32[4,24,512]{2,1,0:T(8,128)S(1)} collective-permute-done((f32[4,24,512]{2,1,0:T(8,128)S(1)}, f32[4,24,512]{2,1,0:T(8,128)S(1)}, u32[]{:S(2)}, u32[]{:S(2)}) %collective-permute-start.10) | collective-permute-done | bytes 196640 | tf_op jit(solution)/shard_map/late_sums/ppermute | solution.py:42
  241.1 3.3 %collective-permute-done.11 = f32[4,24,512]{2,1,0:T(8,128)S(1)} collective-permute-done((f32[4,24,512]{2,1,0:T(8,128)S(1)}, f32[4,24,512]{2,1,0:T(8,128)S(1)}, u32[]{:S(2)}, u32[]{:S(2)}) %collective-permute-start.11) | collective-permute-done | bytes 196640 | tf_op jit(solution)/shard_map/late_sums/ppermute | solution.py:42
  253.7 2.9 all-to-all-done.4.parts
  257.9 7.9 %residual_grad.1 = (f32[2,256,768]{2,1,0:T(8,128)}, f32[8,768]{1,0:T(8,128)}) custom-call(f32[2,256,768]{2,1,0:T(8,128)} %normed_grad_gate.1.part, bf16[4,256,1024]{2,1,0:T(8,128)(2,1)} %copy-done.4, bf16[768,3584]{1,0:T(8,128)(2,1)} %all-gather.5.cloned.1.call-done.expand, f32[2,256,768]{2,1,0:T(8,128)} %bitcast.100, f32[2,256,768]{2,1,0:T(8,128)} %bitcast.103, ...), custom_call_target="tpu_custom_call" | custom-call | flops 2000000000 | bytes 15000000 | tf_op jit(solution)/shard_map/residual_grad/pallas_call | solution.py:830
  267.2 5.4 %all-to-all-start.5 = ((f32[32,1,128]{2,1,0:T(1,128)}), f32[32,1,128]{2,1,0:T(1,128)S(1)}, u32[]{:S(2)}, u32[]{:S(2)}) async-start(f32[32,1,128]{2,1,0:T(1,128)} %bitcast.28), calls=%async_computation.6 | async-start | bytes 32768 | tf_op jit(solution)/shard_map/sum_norm_grad/all_to_all | solution.py:841
  272.7 7.2 %all-to-all-done.5 = f32[32,1,128]{2,1,0:T(1,128)S(1)} async-done(((f32[32,1,128]{2,1,0:T(1,128)}), f32[32,1,128]{2,1,0:T(1,128)S(1)}, u32[]{:S(2)}, u32[]{:S(2)}) %all-to-all-start.5) | async-done | bytes 16416 | tf_op jit(solution)/shard_map/sum_norm_grad/all_to_all | solution.py:841
  280.1 12.0 %all_to_all.36 = f32[4,248,128]{2,1,0:T(8,128)S(1)} all-to-all(f32[4,248,128]{2,1,0:T(8,128)S(1)} %broadcast_in_dim.65), channel_id=1, replica_groups=mesh['dp'=32,'rep'=4] {'rep'}, dimensions={0} | all-to-all | bytes 1015808 | tf_op jit(solution)/shard_map/last_gather/all_to_all | solution.py:56
  (232 shorter events, 69.7 us)
Async XLA Ops:
  7.3 63.8 %all-gather.3.cloned.1.call-start = ((), (), s32[]{:S(2)}) async-start(), calls=%async_computation.8 | async-start | bytes 4257792 | tf_op jit(solution)/shard_map/gather_own_expand/all_gather | solution.py:594
  11.1 21.8 %collective-permute-start = (bf16[2,256,768]{2,1,0:T(8,128)(2,1)S(1)}, bf16[2,256,768]{2,1,0:T(8,128)(2,1)}, u32[]{:S(2)}, u32[]{:S(2)}) collective-permute-start(bf16[2,256,768]{2,1,0:T(8,128)(2,1)S(1)} %multiply_convert_fusion.1.b0), channel_id=1, source_target_pairs={{0,1},{1,2},{2,3},{3,0},{4,5},{5,6},{6,7},{7,4},{8,9},{9,10},{10,1... | collective-permute-start | bytes 2359304 | tf_op jit(solution)/shard_map/gather_branch_grad/ppermute | solution.py:36
  13.1 19.8 %collective-permute-start.1 = (bf16[2,256,768]{2,1,0:T(8,128)(2,1)S(1)}, bf16[2,256,768]{2,1,0:T(8,128)(2,1)}, u32[]{:S(2)}, u32[]{:S(2)}) collective-permute-start(bf16[2,256,768]{2,1,0:T(8,128)(2,1)S(1)} %multiply_convert_fusion.1.b0), channel_id=1, source_target_pairs={{0,3},{1,0},{2,1},{3,2},{4,7},{5,4},{6,5},{7,6},{8,11},{9,8},{10,9... | collective-permute-start | bytes 2359304 | tf_op jit(solution)/shard_map/gather_branch_grad/ppermute | solution.py:36
  16.0 14.7 %all-to-all-start = ((bf16[32,3,128]{2,1,0:T(4,128)(2,1)}), bf16[32,3,128]{2,1,0:T(4,128)(2,1)S(1)}, u32[]{:S(2)}, u32[]{:S(2)}) async-start(bf16[32,3,128]{2,1,0:T(4,128)(2,1)} %broadcast_in_dim.52), calls=%async_computation | async-start | bytes 65536 | tf_op jit(solution)/shard_map/gather_small/all_to_all | solution.py:606
  23.3 94.3 %all-gather.5.cloned.1.call-start = ((), (), s32[]{:S(2)}) async-start(), calls=%async_computation.9 | async-start | bytes 5677056 | tf_op jit(solution)/shard_map/gather_expand/all_gather | solution.py:632
  34.1 21.8 %collective-permute-start.3 = (bf16[2,256,768]{2,1,0:T(8,128)(2,1)S(1)}, bf16[2,256,768]{2,1,0:T(8,128)(2,1)S(1)}, u32[]{:S(2)}, u32[]{:S(2)}) collective-permute-start(bf16[2,256,768]{2,1,0:T(8,128)(2,1)S(1)} %multiply_convert_fusion.n0), channel_id=1, source_target_pairs={{0,1},{1,2},{2,3},{3,0},{4,5},{5,6},{6,7},{7,4},{8,9},{9,10},{10,1... | collective-permute-start | bytes 2359304 | tf_op jit(solution)/shard_map/gather_normed/ppermute | solution.py:36
  35.5 20.6 %collective-permute-start.2 = (bf16[2,256,768]{2,1,0:T(8,128)(2,1)S(1)}, bf16[2,256,768]{2,1,0:T(8,128)(2,1)}, u32[]{:S(2)}, u32[]{:S(2)}) collective-permute-start(bf16[2,256,768]{2,1,0:T(8,128)(2,1)S(1)} %multiply_convert_fusion.n0), channel_id=1, source_target_pairs={{0,3},{1,0},{2,1},{3,2},{4,7},{5,4},{6,5},{7,6},{8,11},{9,8},{10,9... | collective-permute-start | bytes 2359304 | tf_op jit(solution)/shard_map/gather_normed/ppermute | solution.py:36
  40.7 23.7 %collective-permute-start.6 = (bf16[1,256,768]{2,1,0:T(8,128)(2,1)S(1)}, bf16[1,256,768]{2,1,0:T(8,128)(2,1)S(1)}, u32[]{:S(2)}, u32[]{:S(2)}) collective-permute-start(bf16[1,256,768]{2,1,0:T(8,128)(2,1)S(1)} %slice.195), channel_id=1, source_target_pairs={{0,1},{1,2},{2,3},{3,0},{4,5},{5,6},{6,7},{7,4},{8,9},{9,10},{10,1... | collective-permute-start | bytes 1179656 | tf_op jit(solution)/shard_map/gather_branch_grad/ppermute | solution.py:36
  41.8 22.6 %collective-permute-start.7 = (bf16[1,256,768]{2,1,0:T(8,128)(2,1)S(1)}, bf16[1,256,768]{2,1,0:T(8,128)(2,1)S(1)}, u32[]{:S(2)}, u32[]{:S(2)}) collective-permute-start(bf16[1,256,768]{2,1,0:T(8,128)(2,1)S(1)} %slice.196), channel_id=1, source_target_pairs={{0,3},{1,0},{2,1},{3,2},{4,7},{5,4},{6,5},{7,6},{8,11},{9,8},{10,9... | collective-permute-start | bytes 1179656 | tf_op jit(solution)/shard_map/gather_branch_grad/ppermute | solution.py:36
  55.9 15.1 %collective-permute-start.4 = (bf16[1,256,768]{2,1,0:T(8,128)(2,1)S(1)}, bf16[1,256,768]{2,1,0:T(8,128)(2,1)S(1)}, u32[]{:S(2)}, u32[]{:S(2)}) collective-permute-start(bf16[1,256,768]{2,1,0:T(8,128)(2,1)S(1)} %slice.249), channel_id=1, source_target_pairs={{0,1},{1,2},{2,3},{3,0},{4,5},{5,6},{6,7},{7,4},{8,9},{9,10},{10,1... | collective-permute-start | bytes 1179656 | tf_op jit(solution)/shard_map/gather_normed/ppermute | solution.py:36
  57.2 13.8 %collective-permute-start.5 = (bf16[1,256,768]{2,1,0:T(8,128)(2,1)S(1)}, bf16[1,256,768]{2,1,0:T(8,128)(2,1)S(1)}, u32[]{:S(2)}, u32[]{:S(2)}) collective-permute-start(bf16[1,256,768]{2,1,0:T(8,128)(2,1)S(1)} %slice.250), channel_id=1, source_target_pairs={{0,3},{1,0},{2,1},{3,2},{4,7},{5,4},{6,5},{7,6},{8,11},{9,8},{10,9... | collective-permute-start | bytes 1179656 | tf_op jit(solution)/shard_map/gather_normed/ppermute | solution.py:36
  131.1 46.2 %all-to-all-start.2 = ((bf16[4,256,1536]{2,1,0:T(8,128)(2,1)}), bf16[4,256,1536]{2,1,0:T(8,128)(2,1)S(1)}, u32[]{:S(2)}, u32[]{:S(2)}) async-start(bf16[4,256,1536]{2,1,0:T(8,128)(2,1)} %get-tuple-element.75), calls=%async_computation.2 | async-start | bytes 6291456 | tf_op jit(solution)/shard_map/send_gate_parts/all_to_all | solution.py:56
  134.9 85.5 %reduce-scatter.2.cloned.1.call-start = ((), (), s32[]{:S(2)}) async-start(), calls=%async_computation.10 | async-start | bytes 2433024 | tf_op jit(solution)/shard_map/early_sums/reduce_scatter | solution.py:710
  179.1 28.6 %all-to-all-start.3 = ((f32[4,1024,128]{2,1,0:T(8,128)}), f32[4,1024,128]{2,1,0:T(8,128)}, u32[]{:S(2)}, u32[]{:S(2)}) async-start(f32[4,1024,128]{2,1,0:T(8,128)} %get-tuple-element.85), calls=%async_computation.3 | async-start | bytes 4194304 | tf_op jit(solution)/shard_map/sum_writer_reader_grad/all_to_all | solution.py:56
  223.5 6.1 %collective-permute-start.8 = (f32[4,4,24,512]{3,2,1,0:T(8,128)}, f32[4,4,24,512]{3,2,1,0:T(8,128)}, u32[]{:S(2)}, u32[]{:S(2)}) collective-permute-start(f32[4,4,24,512]{3,2,1,0:T(8,128)} %fusion.1), channel_id=1, source_target_pairs={{0,4},{4,0},{8,12},{12,8},{16,20},{20,16},{24,28},{28,24},{32,36},... | collective-permute-start | bytes 2359304 | tf_op jit(solution)/shard_map/late_sums/ppermute | solution.py:42
  225.1 31.4 %all-to-all-start.4 = ((bf16[4,256,1024]{2,1,0:T(8,128)(2,1)}), bf16[4,256,1024]{2,1,0:T(8,128)(2,1)S(1)}, u32[]{:S(2)}, u32[]{:S(2)}) async-start(bf16[4,256,1024]{2,1,0:T(8,128)(2,1)} %pad_maximum_fusion), calls=%async_computation.5 | async-start | bytes 4194304 | tf_op jit(solution)/shard_map/send_values/all_to_all | solution.py:56
  231.8 9.3 %collective-permute-start.10 = (f32[4,24,512]{2,1,0:T(8,128)S(1)}, f32[4,24,512]{2,1,0:T(8,128)S(1)}, u32[]{:S(2)}, u32[]{:S(2)}) collective-permute-start(f32[4,24,512]{2,1,0:T(8,128)S(1)} %get-tuple-element.164), channel_id=1, source_target_pairs={{0,16},{4,20},{8,24},{12,28},{16,0},{20,4},{24,8},{28,12},{32,48},... | collective-permute-start | bytes 589832 | tf_op jit(solution)/shard_map/late_sums/ppermute | solution.py:42
  234.5 9.9 %collective-permute-start.11 = (f32[4,24,512]{2,1,0:T(8,128)S(1)}, f32[4,24,512]{2,1,0:T(8,128)S(1)}, u32[]{:S(2)}, u32[]{:S(2)}) collective-permute-start(f32[4,24,512]{2,1,0:T(8,128)S(1)} %get-tuple-element.163), channel_id=1, source_target_pairs={{0,24},{4,28},{8,0},{12,4},{16,8},{20,12},{24,16},{28,20},{32,56},... | collective-permute-start | bytes 589832 | tf_op jit(solution)/shard_map/late_sums/ppermute | solution.py:42
  235.7 8.9 %collective-permute-start.9 = (f32[4,24,512]{2,1,0:T(8,128)S(1)}, f32[4,24,512]{2,1,0:T(8,128)S(1)}, u32[]{:S(2)}, u32[]{:S(2)}) collective-permute-start(f32[4,24,512]{2,1,0:T(8,128)S(1)} %get-tuple-element.162), channel_id=1, source_target_pairs={{0,8},{4,12},{8,16},{12,20},{16,24},{20,28},{24,0},{28,4},{32,40},... | collective-permute-start | bytes 589832 | tf_op jit(solution)/shard_map/late_sums/ppermute | solution.py:42
  245.6 6.2 %collective-permute-start.12 = (f32[24,512]{1,0:T(8,128)S(1)}, f32[24,512]{1,0:T(8,128)S(1)}, u32[]{:S(2)}, u32[]{:S(2)}) collective-permute-start(f32[24,512]{1,0:T(8,128)S(1)} %get-tuple-element.183), channel_id=1, source_target_pairs={{0,32},{4,36},{8,40},{12,44},{16,48},{20,52},{24,56},{28,60},{32,6... | collective-permute-start | bytes 147464 | tf_op jit(solution)/shard_map/late_sums/ppermute | solution.py:42
  246.9 5.6 %collective-permute-start.13 = (f32[24,512]{1,0:T(8,128)S(1)}, f32[24,512]{1,0:T(8,128)S(1)}, u32[]{:S(2)}, u32[]{:S(2)}) collective-permute-start(f32[24,512]{1,0:T(8,128)S(1)} %get-tuple-element.185), channel_id=1, source_target_pairs={{0,64},{4,68},{8,72},{12,76},{16,80},{20,84},{24,88},{28,92},{32,9... | collective-permute-start | bytes 147464 | tf_op jit(solution)/shard_map/late_sums/ppermute | solution.py:42
  249.6 4.1 %collective-permute-start.14 = (f32[24,512]{1,0:T(8,128)S(1)}, f32[24,512]{1,0:T(8,128)S(1)}, u32[]{:S(2)}, u32[]{:S(2)}) collective-permute-start(f32[24,512]{1,0:T(8,128)S(1)} %get-tuple-element.184), channel_id=1, source_target_pairs={{0,96},{4,100},{8,104},{12,108},{16,112},{20,116},{24,120},{28,124... | collective-permute-start | bytes 147464 | tf_op jit(solution)/shard_map/late_sums/ppermute | solution.py:42
  251.0 21.7 %collective-permute-start.15 = (f32[24,384]{1,0:T(8,128)S(1)}, f32[24,384]{1,0:T(8,128)S(1)}, u32[]{:S(2)}, u32[]{:S(2)}) collective-permute-start(f32[24,384]{1,0:T(8,128)S(1)} %get-tuple-element.189), channel_id=1, source_target_pairs={{0,0},{1,32},{2,64},{3,96},{4,4},{5,36},{6,68},{7,100},{8,8},{9,40... | collective-permute-start | bytes 110600 | tf_op jit(solution)/shard_map/last_gather/ppermute | solution.py:828
  267.2 12.7 %all-to-all-start.5 = ((f32[32,1,128]{2,1,0:T(1,128)}), f32[32,1,128]{2,1,0:T(1,128)S(1)}, u32[]{:S(2)}, u32[]{:S(2)}) async-start(f32[32,1,128]{2,1,0:T(1,128)} %bitcast.28), calls=%async_computation.6 | async-start | bytes 32768 | tf_op jit(solution)/shard_map/sum_norm_grad/all_to_all | solution.py:841
  (33 other events, 191.8 us)
Sparse Core Ops, SparseCore 0:
  10.9 48.3 all-gather.2
  61.5 47.1 all-gather.4
  139.3 81.0 reduce-scatter.1

commit v3 on v2

--- a/solution.py
+++ b/solution.py
@@ -151,30 +151,31 @@
     return jnp.concatenate([pair[:, :width], pair[:, width:]], axis=0)
 
 
-def beside(ref, parity, value, lead=None):
+def beside(ref, parity, value, *lead):
     half = value.shape[1]
     for odd in (0, 1):
 
         @pl.when(parity == odd)
         def _():
-            if lead is None:
-                ref[:, odd * half : odd * half + half] = value
-            else:
-                ref[lead, :, odd * half : odd * half + half] = value
-
-
-def pick(out, source, m, near0, near1, near3, far0, far1):
+            ref[(*lead, slice(None), slice(odd * half, odd * half + half))] = value
+
+
+def pick(out, source, near0, near1, near3, far0, far1):
     for index, ref in ((0, near0), (1, near1), (3, near3)):
 
         @pl.when(source == index)
         def _():
-            out[...] = ref[0]
-
-    for micro, ref in enumerate((far0, far1)):
-
-        @pl.when((source == 2) & (m == micro))
-        def _():
-            out[...] = ref[0]
+            out[...] = ref[...]
+
+    @pl.when(source == 2)
+    def _():
+        out[0] = far0[0]
+        out[1] = far1[0]
+
+
+def side_by_side(works):
+    for _ in zip(*works):
+        pass
 
 
 def forward_kernel(
@@ -182,91 +183,100 @@
     nrm_o, bg_o, gate_o, sig_o, pre_o, y_o, oc_o, sr_o, sin_o, sums_o, pwr_o, swr_o,
     state, tail, co,
 ):
-    q = nrm_o.shape[0]
+    micro, q = nrm_o.shape[:2]
     ch = cp.shape[1]
     cw = fp.shape[1]
     ns = (cw - ch) // 2
     wr = 2 * ns // reps
     size = ch // heads
-    step_id = pl.program_id(0)
-    block = step_id % reps
+    block = pl.program_id(0)
     rep = place[0]
     source = (block - rep + reps) % reps
 
-    pick(nrm_o, source, step_id // reps, n0, n1, n3, n2a, n2b)
-    pick(bg_o, source, step_id // reps, b0, b1, b3, b2a, b2b)
-
-    @pl.when(step_id == 0)
-    def _():
-        co[...] = dot(perm[...], contract_rows(front, rep, ch, nrm_o.shape[1])).astype(BF16)
+    pick(nrm_o, source, n0, n1, n3, n2a, n2b)
+    pick(bg_o, source, b0, b1, b3, b2a, b2b)
 
     @pl.when(block == 0)
     def _():
+        co[...] = dot(perm[...], contract_rows(front, rep, ch, nrm_o.shape[2])).astype(BF16)
         state[...] = jnp.zeros_like(state)
         tail[...] = jnp.zeros_like(tail)
 
-    proj = dot(nrm_o[...], front[:, : ch + cw + 128])
-    gate = proj[:, :ch]
-    signal = proj[:, ch : ch + cw]
+    aside = [None] * micro
     lane = lax.broadcasted_iota(jnp.int32, (q, 128), 1)
-    sr = jnp.where(lane < heads, proj[:, ch + cw : ch + cw + 128], 0.0)
-    ext = jnp.concatenate([tail[...], signal], axis=0)
-    pre = fp[4:5, :] + jnp.zeros_like(signal)
-    for k in range(4):
-        pre = pre + fp[k : k + 1, :] * ext[5 + k : 5 + k + q]
-    tail[...] = signal[q - 8 :]
-    act = pre * sigmoid(pre)
-    values = act[:, :ch]
-    writer = act[:, ch : ch + ns]
-    reader = act[:, ch + ns :]
-    _, step, ld = steps_of(sr, hp[...], heads)
     lower = triangle(q, True)
-    cum = triangle_sum(lower, ld, heads)
-    cum_t = cum.T
-    cum_e, step_e = by_channel(cum, step, spread[...])
-    last_e = cum_e[q - 1 : q]
-    xv = step_e * values
-    scores = dot3(reader, writer, NT)
-    parts = []
-    for p in range(ch // 128):
-        hi, lo = split(xv[:, 128 * p : 128 * p + 128])
-        both = jnp.concatenate([hi, lo], axis=1)
-        out = None
-        for j in range(128 // size):
-            h = p * (128 // size) + j
-            decay = jnp.exp(cum[:, h : h + 1] - cum_t[h : h + 1, :])
-            ph, plo = split(jnp.where(lower, scores * decay, 0.0))
-            r = dot(ph, both)
-            one = r[:, :128] + (r[:, 128:] + dot(plo, hi))
-            out = one if out is None else jnp.where(lane < j * size, out, one)
-        parts.append(out)
-    inner = jnp.concatenate(parts, axis=1)
-    old = state[...]
-    sin_o[0] = old
-    y = inner + jnp.exp(cum_e) * dot3(reader, old, NT) + cp[0:1, :] * values
-    decay_ch = jnp.broadcast_to(jnp.exp(last_e), (ns, ch)).T
-    state[...] = decay_ch * old + dot3(jnp.exp(last_e - cum_e) * xv, writer, TN)
-    gated = y * (gate * sigmoid(gate))
-    outcome = dot(bg_o[...], co[...], NT)
-    ones = jnp.ones((8, ch), BF16)
-    s1 = dot2(ones, gated * gated, NT)
-    s2 = dot2(ones, outcome * cp[1:2, :] * gated, NT)
-    row = lax.broadcasted_iota(jnp.int32, s1.shape, 0)
-    both_sums = jnp.where(row == 0, s1, jnp.where(row == 1, s2, 0.0))
-    for r in range(reps):
-        sums_o[r] = both_sums
-    gate_o[...] = gate
-    sig_o[...] = signal[:, :ch]
-    pre_o[...] = pre
-    y_o[...] = y
-    oc_o[...] = outcome
-    sr_o[...] = sr
+
+    def work(m):
+        proj = dot(nrm_o[m], front[:, : ch + cw + 128])
+        gate = proj[:, :ch]
+        signal = proj[:, ch : ch + cw]
+        sr = jnp.where(lane < heads, proj[:, ch + cw : ch + cw + 128], 0.0)
+        ext = jnp.concatenate([tail[m], signal], axis=0)
+        pre = fp[4:5, :] + jnp.zeros_like(signal)
+        for k in range(4):
+            pre = pre + fp[k : k + 1, :] * ext[5 + k : 5 + k + q]
+        tail[m] = signal[q - 8 :]
+        yield
+        act = pre * sigmoid(pre)
+        values = act[:, :ch]
+        writer = act[:, ch : ch + ns]
+        reader = act[:, ch + ns :]
+        _, step, ld = steps_of(sr, hp[...], heads)
+        cum = triangle_sum(lower, ld, heads)
+        cum_t = cum.T
+        cum_e, step_e = by_channel(cum, step, spread[...])
+        last_e = cum_e[q - 1 : q]
+        xv = step_e * values
+        yield
+        scores = dot3(reader, writer, NT)
+        yield
+        parts = []
+        for p in range(ch // 128):
+            hi, lo = split(xv[:, 128 * p : 128 * p + 128])
+            both = jnp.concatenate([hi, lo], axis=1)
+            out = None
+            for j in range(128 // size):
+                h = p * (128 // size) + j
+                decay = jnp.exp(cum[:, h : h + 1] - cum_t[h : h + 1, :])
+                ph, plo = split(jnp.where(lower, scores * decay, 0.0))
+                r = dot(ph, both)
+                one = r[:, :128] + (r[:, 128:] + dot(plo, hi))
+                out = one if out is None else jnp.where(lane < j * size, out, one)
+                yield
+            parts.append(out)
+        inner = jnp.concatenate(parts, axis=1)
+        old = state[m]
+        sin_o[m, 0] = old
+        y = inner + jnp.exp(cum_e) * dot3(reader, old, NT) + cp[0:1, :] * values
+        decay_ch = jnp.broadcast_to(jnp.exp(last_e), (ns, ch)).T
+        state[m] = decay_ch * old + dot3(jnp.exp(last_e - cum_e) * xv, writer, TN)
+        yield
+        gated = y * (gate * sigmoid(gate))
+        outcome = dot(bg_o[m], co[...], NT)
+        ones = jnp.ones((8, ch), BF16)
+        s1 = dot2(ones, gated * gated, NT)
+        s2 = dot2(ones, outcome * cp[1:2, :] * gated, NT)
+        row = lax.broadcasted_iota(jnp.int32, s1.shape, 0)
+        both_sums = jnp.where(row == 0, s1, jnp.where(row == 1, s2, 0.0))
+        for r in range(reps):
+            sums_o[r, m] = both_sums
+        gate_o[m] = gate
+        sig_o[m] = signal[:, :ch]
+        pre_o[m] = pre
+        y_o[m] = y
+        oc_o[m] = outcome
+        sr_o[m] = sr
+        aside[m] = (pre[:, ch:], signal[:, ch:])
+        yield
+
+    side_by_side([work(m) for m in range(micro)])
     for r in range(reps):
 
         @pl.when(rep == r)
         def _():
-            beside(pwr_o, block % 2, pre[:, ch + r * wr : ch + r * wr + wr])
-            beside(swr_o, block % 2, signal[:, ch + r * wr : ch + r * wr + wr])
+            for m in range(micro):
+                for out, value in zip((pwr_o, swr_o), aside[m]):
+                    beside(out, block % 2, value[:, r * wr : r * wr + wr], m)
 
 
 def gate_kernel(
@@ -283,7 +293,7 @@
         early_o[...] = jnp.zeros_like(early_o)
         acc_o[...] = jnp.zeros_like(acc_o)
 
-    s = jnp.sum(sums[...], axis=0)
+    s = jnp.sum(sums[:, 0], axis=0)
     scale_row = lax.rsqrt(s[0:1] * (1.0 / width) + EPS)
     mean_row = scale_row * s[1:2] * (1.0 / width)
 
@@ -327,113 +337,122 @@
     vg_o, send_o, wr_o, raw_o, acc_o, hacc_o,
     adj, head_rows,
 ):
-    q, ch = y_r.shape
+    micro, q, ch = y_r.shape
     cw = fp.shape[1]
     ns = (cw - ch) // 2
     wr = 2 * ns // reps
     size = ch // heads
-    block = reps - 1 - pl.program_id(0) % reps
-
-    @pl.when(block == reps - 1)
+    block = reps - 1 - pl.program_id(0)
+
+    @pl.when(pl.program_id(0) == 0)
     def _():
         adj[...] = jnp.zeros_like(adj)
         head_rows[...] = jnp.zeros_like(head_rows)
-
-    @pl.when(pl.program_id(0) == 0)
-    def _():
         acc_o[...] = jnp.zeros_like(acc_o)
         hacc_o[...] = jnp.zeros_like(hacc_o)
 
-    pre = pre_r[...]
-    sgm = sigmoid(pre)
-    act = pre * sgm
-    values = act[:, :ch]
-    writer = act[:, ch : ch + ns]
-    reader = act[:, ch + ns :]
-    moved_raw, step, ld = steps_of(sr_r[...], hp[...], heads)
+    lane = lax.broadcasted_iota(jnp.int32, (q, 128), 1)
     lower = triangle(q, True)
     upper = triangle(q, False)
-    cum = triangle_sum(lower, ld, heads)
-    cum_t = cum.T
-    cum_e, step_e = by_channel(cum, step, spread[...])
-    last_e = cum_e[q - 1 : q]
-    skip = cp[0:1, :]
-    dy = dy_r[...]
-    y = y_r[...]
-    xv = step_e * values
-    lane = lax.broadcasted_iota(jnp.int32, (q, 128), 1)
-    scores = dot3(writer, reader, NT)
-    dscores = jnp.zeros((q, q), F32)
-    parts = []
-    for p in range(ch // 128):
-        dpair = dy[:, 128 * p : 128 * p + 128]
-        xpair = xv[:, 128 * p : 128 * p + 128]
-        dh, dl = split(dpair)
-        dboth = jnp.concatenate([dh, dl], axis=1)
-        dtwice = jnp.concatenate([dh, dh], axis=1)
-        out = None
-        for j in range(128 // size):
-            h = p * (128 // size) + j
-            decay = jnp.where(upper, jnp.exp(cum_t[h : h + 1, :] - cum[:, h : h + 1]), 0.0)
-            ph, plo = split(scores * decay)
-            r = dot(ph, dboth)
-            one = r[:, :128] + (r[:, 128:] + dot(plo, dh))
-            out = one if out is None else jnp.where(lane < j * size, out, one)
-            mine = (lane >= j * size) & (lane < (j + 1) * size)
-            xh, xl = split(jnp.where(mine, xpair, 0.0))
-            m = dot(jnp.concatenate([xh, xl], axis=1), dtwice, NT) + dot(xh, dl, NT)
-            dscores = dscores + m * decay
-        parts.append(out)
-    inner = jnp.concatenate(parts, axis=1)
-    old = adj[...]
-    sin = sin_r[0]
-    ends = jnp.exp(last_e - cum_e)
-    from_state = ends * dot3(writer, old, NT)
-    dxv = inner + from_state
-    cdy = jnp.exp(cum_e) * dy
-    dwriter = dot3(dscores, reader) + dot3(ends * xv, old)
-    dreader = dot3(dscores, writer, TN) + dot3(cdy, sin)
-    decay_ch = jnp.broadcast_to(jnp.exp(last_e), (ns, ch)).T
-    state_row = dot2(jnp.ones((8, ns), BF16), decay_ch * old * sin, NT)[0:1]
-    last_row = state_row + jnp.sum(xv * from_state, axis=0, keepdims=True)
-    adj[...] = decay_ch * old + dot3(cdy, reader, TN)
-
-    dstep = dot2(values * dxv, oh[...], NT)
-    row = lax.broadcasted_iota(jnp.int32, (q, ch), 0)
-    dcum_ch = dy * (y - skip * values) - xv * dxv + jnp.where(row == q - 1, last_row, 0.0)
-    dcum = dot2(dcum_ch, oh[...], NT)
-    dld = triangle_sum(upper, dcum, heads)
-    raw = (dstep - dld * hp[1:2]) * sigmoid(moved_raw)
-    raw = jnp.where(lane < heads, raw, 0.0)
-    raw_o[...] = jnp.concatenate([jnp.zeros((q, wr), F32), raw[:, : 128 - wr]], axis=1)
-    hrow = lax.broadcasted_iota(jnp.int32, hacc_o.shape, 0)
-    hacc_o[...] += jnp.where(
-        hrow == 0,
-        jnp.sum(raw, axis=0, keepdims=True),
-        jnp.where(hrow == 1, jnp.sum(dld * ld, axis=0, keepdims=True), 0.0),
-    )
-    both = jnp.concatenate([dwriter, dreader], axis=1)
-    for r in range(reps):
-        beside(wr_o, block % 2, both[:, r * wr : r * wr + wr], r)
-
-    sv = sgm[:, :ch]
-    dpre = (step_e * dxv + skip * dy) * (sv * (1.0 + pre[:, :ch] * (1.0 - sv)))
-    ext = jnp.concatenate([dpre, head_rows[...]], axis=0)
-    head_rows[...] = dpre[:8]
-    signal = sig_r[...]
-    total = jnp.zeros_like(dpre)
-    rows = []
-    for k in range(4):
-        moved = ext[3 - k : 3 - k + q]
-        total = total + fp[k : k + 1, :ch] * moved
-        rows.append(jnp.sum(moved * signal, axis=0, keepdims=True))
-    vg = total.astype(BF16)
-    vg_o[...] = vg
-    send_o[0] = vg
-    rows.append(jnp.sum(dpre, axis=0, keepdims=True))
-    rows.append(jnp.sum(values * dy, axis=0, keepdims=True))
-    rows.append(jnp.zeros((2, ch), F32))
-    acc_o[...] += jnp.concatenate(rows, axis=0)
+    found = [None] * micro
+
+    def work(m):
+        pre = pre_r[m]
+        sgm = sigmoid(pre)
+        act = pre * sgm
+        values = act[:, :ch]
+        writer = act[:, ch : ch + ns]
+        reader = act[:, ch + ns :]
+        moved_raw, step, ld = steps_of(sr_r[m], hp[...], heads)
+        cum = triangle_sum(lower, ld, heads)
+        cum_t = cum.T
+        cum_e, step_e = by_channel(cum, step, spread[...])
+        last_e = cum_e[q - 1 : q]
+        skip = cp[0:1, :]
+        dy = dy_r[m]
+        y = y_r[m]
+        xv = step_e * values
+        yield
+        scores = dot3(writer, reader, NT)
+        yield
+        dscores = jnp.zeros((q, q), F32)
+        parts = []
+        for p in range(ch // 128):
+            dpair = dy[:, 128 * p : 128 * p + 128]
+            xpair = xv[:, 128 * p : 128 * p + 128]
+            dh, dl = split(dpair)
+            dboth = jnp.concatenate([dh, dl], axis=1)
+            dtwice = jnp.concatenate([dh, dh], axis=1)
+            out = None
+            for j in range(128 // size):
+                h = p * (128 // size) + j
+                decay = jnp.where(upper, jnp.exp(cum_t[h : h + 1, :] - cum[:, h : h + 1]), 0.0)
+                ph, plo = split(scores * decay)
+                r = dot(ph, dboth)
+                one = r[:, :128] + (r[:, 128:] + dot(plo, dh))
+                out = one if out is None else jnp.where(lane < j * size, out, one)
+                mine = (lane >= j * size) & (lane < (j + 1) * size)
+                xh, xl = split(jnp.where(mine, xpair, 0.0))
+                got = dot(jnp.concatenate([xh, xl], axis=1), dtwice, NT) + dot(xh, dl, NT)
+                dscores = dscores + got * decay
+                yield
+            parts.append(out)
+        inner = jnp.concatenate(parts, axis=1)
+        old = adj[m]
+        sin = sin_r[m, 0]
+        ends = jnp.exp(last_e - cum_e)
+        from_state = ends * dot3(writer, old, NT)
+        dxv = inner + from_state
+        cdy = jnp.exp(cum_e) * dy
+        dwriter = dot3(dscores, reader) + dot3(ends * xv, old)
+        dreader = dot3(dscores, writer, TN) + dot3(cdy, sin)
+        decay_ch = jnp.broadcast_to(jnp.exp(last_e), (ns, ch)).T
+        state_row = dot2(jnp.ones((8, ns), BF16), decay_ch * old * sin, NT)[0:1]
+        last_row = state_row + jnp.sum(xv * from_state, axis=0, keepdims=True)
+        adj[m] = decay_ch * old + dot3(cdy, reader, TN)
+
+        yield
+        dstep = dot2(values * dxv, oh[...], NT)
+        row = lax.broadcasted_iota(jnp.int32, (q, ch), 0)
+        dcum_ch = dy * (y - skip * values) - xv * dxv + jnp.where(row == q - 1, last_row, 0.0)
+        dcum = dot2(dcum_ch, oh[...], NT)
+        dld = triangle_sum(upper, dcum, heads)
+        raw = (dstep - dld * hp[1:2]) * sigmoid(moved_raw)
+        raw = jnp.where(lane < heads, raw, 0.0)
+        raw_o[m] = jnp.concatenate([jnp.zeros((q, wr), F32), raw[:, : 128 - wr]], axis=1)
+        hrow = lax.broadcasted_iota(jnp.int32, hacc_o.shape, 0)
+        hacc_o[...] += jnp.where(
+            hrow == 0,
+            jnp.sum(raw, axis=0, keepdims=True),
+            jnp.where(hrow == 1, jnp.sum(dld * ld, axis=0, keepdims=True), 0.0),
+        )
+        found[m] = jnp.concatenate([dwriter, dreader], axis=1)
+        yield
+
+        sv = sgm[:, :ch]
+        dpre = (step_e * dxv + skip * dy) * (sv * (1.0 + pre[:, :ch] * (1.0 - sv)))
+        ext = jnp.concatenate([dpre, head_rows[m]], axis=0)
+        head_rows[m] = dpre[:8]
+        signal = sig_r[m]
+        total = jnp.zeros_like(dpre)
+        rows = []
+        for k in range(4):
+            moved = ext[3 - k : 3 - k + q]
+            total = total + fp[k : k + 1, :ch] * moved
+            rows.append(jnp.sum(moved * signal, axis=0, keepdims=True))
+        vg = total.astype(BF16)
+        vg_o[m] = vg
+        send_o[0, :, m * ch : (m + 1) * ch] = vg
+        rows.append(jnp.sum(dpre, axis=0, keepdims=True))
+        rows.append(jnp.sum(values * dy, axis=0, keepdims=True))
+        rows.append(jnp.zeros((2, ch), F32))
+        acc_o[...] += jnp.concatenate(rows, axis=0)
+        yield
+
+    side_by_side([work(m) for m in range(micro)])
+    for m in range(micro):
+        for r in range(reps):
+            beside(wr_o, block % 2, found[m][:, r * wr : r * wr + wr], r, m)
 
 
 def tail_kernel(wr, got, pwr, swr, fw, raw, tail_o, send_o, acc_o):
@@ -652,41 +671,50 @@
     onehot = jnp.asarray(onehot, BF16)
     spread_of = jnp.asarray(spread_of, BF16)
 
-    piece = pl.BlockSpec((1, q, width), lambda b: (b // reps, 0, 0))
-    ring_specs = [piece, piece, piece, whole((1, q, width)), whole((1, q, width))]
+    pieces = whole((micro, q, width))
+    ring_specs = [pieces, pieces, pieces, whole((1, q, width)), whole((1, q, width))]
     both = micro * total
-    aside = pl.BlockSpec((q, 128), lambda b: (b // 2, 0))
+
+    def pairs_of(w, order=lambda b: b):
+        return pl.BlockSpec((micro, q, w), lambda b: (0, order(b), 0))
+
+    def pairs(w, dtype=F32):
+        return sds((micro, total, w), dtype)
+
+    aside = pl.BlockSpec((micro, q, 2 * wr), lambda b: (0, b // 2, 0))
     kept = pl.pallas_call(
         functools.partial(forward_kernel, heads, reps),
-        grid=(micro * reps,),
+        grid=(reps,),
         in_specs=[SCALAR] + ring_specs * 2 + [
             whole(front.shape), whole((ch, ch)),
             whole((8, cw)), whole((8, 128)), whole((8, ch)), whole((128, 2 * ch)),
         ],
         out_specs=[
-            rows_of(q, width), rows_of(q, width),
-            rows_of(q, ch), rows_of(q, ch), rows_of(q, cw), rows_of(q, ch), rows_of(q, ch),
-            rows_of(q, 128), pl.BlockSpec((1, ch, ns), lambda b: (b, 0, 0)),
-            pl.BlockSpec((reps, 8, q), lambda b: (0, 0, b)), aside, aside,
+            pairs_of(width), pairs_of(width),
+            pairs_of(ch), pairs_of(ch), pairs_of(cw), pairs_of(ch), pairs_of(ch), pairs_of(128),
+            pl.BlockSpec((micro, 1, ch, ns), lambda b: (0, b, 0, 0)),
+            pl.BlockSpec((reps, micro, 8, q), lambda b: (0, 0, 0, b)), aside, aside,
         ],
         out_shape=[
-            sds((both, width), BF16), sds((both, width), BF16),
-            sds((both, ch), F32), sds((both, ch), F32), sds((both, cw), F32),
-            sds((both, ch), F32), sds((both, ch), F32), sds((both, 128), F32),
-            sds((micro * reps, ch, ns), F32), sds((reps, 8, both), F32),
-            sds((both // 2, 2 * wr), F32), sds((both // 2, 2 * wr), F32),
+            pairs(width, BF16), pairs(width, BF16),
+            pairs(ch), pairs(ch), pairs(cw), pairs(ch), pairs(ch), pairs(128),
+            sds((micro, reps, ch, ns), F32), sds((reps, micro, 8, total), F32),
+            sds((micro, total // 2, 2 * wr), F32), sds((micro, total // 2, 2 * wr), F32),
         ],
         scratch_shapes=[
-            pltpu.VMEM((ch, ns), F32), pltpu.VMEM((8, cw), F32), pltpu.VMEM((ch, width), BF16),
+            pltpu.VMEM((micro, ch, ns), F32), pltpu.VMEM((micro, 8, cw), F32),
+            pltpu.VMEM((ch, width), BF16),
         ],
         name="scan_forward",
         **params(40_000_000_000, 40_000_000),
     )(place, *nrm_ring, *bg_ring, front, perm, fp, hp, cp, spread_of)
     nrm, bg, gate, signal, pre, y, outcome, sr, sin, sums, pwr, swr = kept
+    nrm, bg, gate, outcome = (v.reshape(both, -1) for v in (nrm, bg, gate, outcome))
+    pwr, swr = (v.reshape(both // 2, -1) for v in (pwr, swr))
     with jax.named_scope("sum_norm_terms"):
         sums, expand_full = lax.optimization_barrier((ax.exchange(sums), expand_full))
 
-    strip = pl.BlockSpec((reps, 8, q), lambda b: (0, 0, b))
+    strip = pl.BlockSpec((reps, 1, 8, q), lambda b: (0, b // reps, 0, b % reps))
     ys = ax.size["y"]
     wide = width // 2
     early_rows = rows + 2 * (contract.shape[0] // ys)
@@ -705,38 +733,40 @@
         scratch_shapes=[pltpu.VMEM((ch, width), F32)],
         name="gate_backward",
         **params(8_000_000_000, 20_000_000),
-    )(gate, y, outcome, sums, bg, nrm, cp)
+    )(gate, y.reshape(both, ch), outcome, sums, bg, nrm, cp)
     with jax.named_scope("early_sums"):
         early = lax.psum_scatter(early, "dp", scatter_dimension=0)
 
     with jax.named_scope("send_gate_parts"):
         a_parts = ax.exchange(send)
     def back(b):
-        return b // reps * reps + reps - 1 - b % reps
+        return reps - 1 - b
 
     value_grads, v_send, wrg, raws, channel_part, head_part = pl.pallas_call(
         functools.partial(backward_kernel, heads, reps),
-        grid=(micro * reps,),
+        grid=(reps,),
         in_specs=[
-            rows_of(q, ch, back), rows_of(q, cw, back), rows_of(q, ch, back), rows_of(q, ch, back),
-            rows_of(q, 128, back), pl.BlockSpec((1, ch, ns), lambda b: (back(b), 0, 0)),
+            pairs_of(ch, back), pairs_of(cw, back), pairs_of(ch, back), pairs_of(ch, back),
+            pairs_of(128, back), pl.BlockSpec((micro, 1, ch, ns), lambda b: (0, back(b), 0, 0)),
             whole((8, cw)), whole((8, 128)), whole((8, ch)), whole((128, 2 * ch)), whole((128, ch)),
         ],
         out_specs=[
-            rows_of(q, ch, back),
-            pl.BlockSpec((1, q, ch), lambda b: (back(b) % reps, 0, b // reps)),
-            pl.BlockSpec((reps, q, 2 * wr), lambda b: (0, back(b) // 2, 0)),
-            rows_of(q, 128, back), whole((8, ch)), whole((8, 128)),
+            pairs_of(ch, back),
+            pl.BlockSpec((1, q, micro * ch), lambda b: (back(b), 0, 0)),
+            pl.BlockSpec((reps, micro, q, 2 * wr), lambda b: (0, 0, back(b) // 2, 0)),
+            pairs_of(128, back), whole((8, ch)), whole((8, 128)),
         ],
         out_shape=[
-            sds((both, ch), BF16), sds((reps, q, micro * ch), BF16),
-            sds((reps, both // 2, 2 * wr), F32),
-            sds((both, 128), F32), sds((8, ch), F32), sds((8, 128), F32),
-        ],
-        scratch_shapes=[pltpu.VMEM((ch, ns), F32), pltpu.VMEM((8, ch), F32)],
+            pairs(ch, BF16), sds((reps, q, micro * ch), BF16),
+            sds((reps, micro, total // 2, 2 * wr), F32),
+            pairs(128), sds((8, ch), F32), sds((8, 128), F32),
+        ],
+        scratch_shapes=[pltpu.VMEM((micro, ch, ns), F32), pltpu.VMEM((micro, 8, ch), F32)],
         name="scan_backward",
         **params(80_000_000_000, 40_000_000),
-    )(signal, pre, y, dy, sr, sin, fp, hp, cp, spread_of, onehot)
+    )(signal, pre, y, dy.reshape(micro, total, ch), sr, sin, fp, hp, cp, spread_of, onehot)
+    value_grads, raws = value_grads.reshape(both, ch), raws.reshape(both, 128)
+    wrg = wrg.reshape(reps, both // 2, 2 * wr)
     with jax.named_scope("sum_writer_reader_grad"):
         a_parts, wrg = lax.optimization_barrier((a_parts, wrg))
         wr_got = ax.exchange(wrg)

time: 305 us -> 307 us (level); the launches traced: 303 us -> 302 us
  Pallas kernels: 117 us -> 112 us
    pallas_call x2, Pallas kernels: 76.7 us -> 71.1 us  [the longest x1 38.1 us: body(): pl.pallas_call(functools.partial(backward_kernel, heads, reps), grid=(rep...]
    reduce_scatter x1, waiting for transfers between devices: 2.84 us -> 6.25 us  [body(): early = lax.psum_scatter(early, 'dp', scatter_dimension=0)]
  transfers between devices with their start and end apart: 24 -> 24, of which waited for: 14 -> 14; matrix products, arithmetic and copies ran while one was open for 10% -> 10% of each run, Pallas kernels for 34% -> 33%
where the time goes in v3:
time: 307 us; the launch traced here: 302 us
  Pallas kernels  112 us (36%)
  waiting for transfers between devices  54.9 us (18%)
  starting transfers between devices  51.9 us (17%)
  local copies, waits for them, and re-layouts  24.8 us (8%)
  blocking collectives  22.8 us (7%)
  between operations  14.9 us (5%)
  other arithmetic  13 us (4%)
  matrix products  7.99 us (3%)
    pallas_call x1, Pallas kernels, body(): pl.pallas_call(functools.partial(backward_kernel, heads, reps), grid=(rep...  38.1 us
    pallas_call x1, Pallas kernels, body(): pl.pallas_call(functools.partial(forward_kernel, heads, reps), grid=(reps...  33 us
    all_to_all x2, blocking collectives, exchange(): return lax.all_to_all(v, 'rep', 0, 0, tiled=True)  22.8 us
    ppermute x8, waiting for transfers between devices, shift(): return lax.ppermute(v, 'rep', [(i, (i + by) % n) for i in range(n)])  20.9 us
    ppermute x8, starting transfers between devices, shift(): return lax.ppermute(v, 'rep', [(i, (i + by) % n) for i in range(n)])  14.6 us
    pallas_call x1, Pallas kernels, body(): pl.pallas_call(functools.partial(gate_kernel, inner, ys), grid=(micro * r...  13.5 us
    all_to_all x3, starting transfers between devices, exchange(): return lax.all_to_all(v, 'rep', 0, 0, tiled=True)  13.1 us
    ppermute x7, starting transfers between devices, shift(): return lax.ppermute(v, 'dp', route)  10.1 us
  transfers between devices with their start and end apart: 24, of which 14 were waited for; matrix products, arithmetic and copies ran while one was open for 10% of the time, Pallas kernels for 33%

profile of v3, /device:TPU:0, one launch (start us, length us, event | category | flops | bytes accessed | tf_op | source)
XLA Modules:
  0.0 301.8 jit_solution(1256693233623277967)
XLA Ops:
  16.0 7.3 %all-to-all-start = ((bf16[32,3,128]{2,1,0:T(4,128)(2,1)}), bf16[32,3,128]{2,1,0:T(4,128)(2,1)S(1)}, u32[]{:S(2)}, u32[]{:S(2)}) async-start(bf16[32,3,128]{2,1,0:T(4,128)(2,1)} %broadcast_in_dim.52), calls=%async_computation | async-start | bytes 65536 | tf_op jit(solution)/shard_map/gather_small/all_to_all | solution.py:625
  23.6 7.2 %all-to-all-done = bf16[32,3,128]{2,1,0:T(4,128)(2,1)S(1)} async-done(((bf16[32,3,128]{2,1,0:T(4,128)(2,1)}), bf16[32,3,128]{2,1,0:T(4,128)(2,1)S(1)}, u32[]{:S(2)}, u32[]{:S(2)}) %all-to-all-start) | async-done | bytes 24608 | tf_op jit(solution)/shard_map/gather_small/all_to_all | solution.py:625
  41.8 3.3 %collective-permute-start.7 = (bf16[1,256,768]{2,1,0:T(8,128)(2,1)S(1)}, bf16[1,256,768]{2,1,0:T(8,128)(2,1)S(1)}, u32[]{:S(2)}, u32[]{:S(2)}) collective-permute-start(bf16[1,256,768]{2,1,0:T(8,128)(2,1)S(1)} %slice.196), channel_id=1, source_target_pairs={{0,3},{1,0},{2,1},{3,2},{4,7},{5,4},{6,5},{7,6},{8,11},{9,8},{10,9... | collective-permute-start | bytes 1179656 | tf_op jit(solution)/shard_map/gather_branch_grad/ppermute | solution.py:36
  45.1 10.8 %collective-permute-done.3.n3 = bf16[2,256,768]{2,1,0:T(8,128)(2,1)S(1)} collective-permute-done((bf16[2,256,768]{2,1,0:T(8,128)(2,1)S(1)}, bf16[2,256,768]{2,1,0:T(8,128)(2,1)S(1)}, u32[]{:S(2)}, u32[]{:S(2)}) %collective-permute-start.3) | collective-permute-done | bytes 786464 | tf_op jit(solution)/shard_map/gather_normed/ppermute | solution.py:36
  57.2 3.6 %collective-permute-start.5 = (bf16[1,256,768]{2,1,0:T(8,128)(2,1)S(1)}, bf16[1,256,768]{2,1,0:T(8,128)(2,1)S(1)}, u32[]{:S(2)}, u32[]{:S(2)}) collective-permute-start(bf16[1,256,768]{2,1,0:T(8,128)(2,1)S(1)} %slice.250), channel_id=1, source_target_pairs={{0,3},{1,0},{2,1},{3,2},{4,7},{5,4},{6,5},{7,6},{8,11},{9,8},{10,9... | collective-permute-start | bytes 1179656 | tf_op jit(solution)/shard_map/gather_normed/ppermute | solution.py:36
  64.4 6.6 %collective-permute-done.4.n2a = bf16[1,256,768]{2,1,0:T(8,128)(2,1)S(1)} collective-permute-done((bf16[1,256,768]{2,1,0:T(8,128)(2,1)S(1)}, bf16[1,256,768]{2,1,0:T(8,128)(2,1)S(1)}, u32[]{:S(2)}, u32[]{:S(2)}) %collective-permute-start.4) | collective-permute-done | bytes 393248 | tf_op jit(solution)/shard_map/gather_normed/ppermute | solution.py:36
  71.9 33.0 %scan_forward.1 = (bf16[2,1024,768]{2,1,0:T(8,128)(2,1)}, bf16[2,1024,768]{2,1,0:T(8,128)(2,1)}, f32[2,1024,384]{2,1,0:T(8,128)}, f32[2,1024,384]{2,1,0:T(8,128)...) custom-call(s32[1]{0:T(128)} %bitcast.place, ...), custom_call_target="tpu_custom_call" | custom-call | flops 40000000000 | bytes 40000000 | tf_op jit(solution)/shard_map/scan_forward/pallas_call | solution.py:685
  104.9 10.8 %all_to_all.35.sums = f32[4,2,8,1024]{3,2,1,0:T(8,128)} all-to-all(f32[4,2,8,1024]{3,2,1,0:T(8,128)} %get-tuple-element.70), channel_id=1, replica_groups=mesh['dp'=32,'rep'=4] {'rep'}, dimensions={0} | all-to-all | bytes 524288 | tf_op jit(solution)/shard_map/sum_norm_terms/all_to_all | solution.py:56
  115.7 13.5 %gate_backward.1 = (bf16[4,256,1536]{2,1,0:T(8,128)(2,1)}, f32[32,48,384]{2,1,0:T(8,128)}, f32[2048,384]{1,0:T(8,128)}, f32[8,384]{1,0:T(8,128)}) custom-call(f32[2048,384]{1,0:T(8,128)} %bitcast.147, f32[2048,384]{1,0:T(8,128)} %bitcast.144, f32[2048,384]{1,0:T(8,128)} %bitcast.148, f32[4,2,8,1024]{3,2,1,0:T(8,128)} %all_to_all.35.sums, ...), custom_call_target="tpu_custom_call" | custom-call | flops 8000000000 | bytes 20000000 | tf_op jit(solution)/shard_map/gate_backward/pallas_call | solution.py:721
  129.2 3.7 %all-to-all-start.2 = ((bf16[4,256,1536]{2,1,0:T(8,128)(2,1)}), bf16[4,256,1536]{2,1,0:T(8,128)(2,1)S(1)}, u32[]{:S(2)}, u32[]{:S(2)}) async-start(bf16[4,256,1536]{2,1,0:T(8,128)(2,1)} %get-tuple-element.75), calls=%async_computation.2 | async-start | bytes 6291456 | tf_op jit(solution)/shard_map/send_gate_parts/all_to_all | solution.py:56
  133.6 38.1 %scan_backward.1 = (bf16[2,1024,384]{2,1,0:T(8,128)(2,1)}, bf16[4,256,768]{2,1,0:T(8,128)(2,1)}, f32[4,2,512,128]{3,2,1,0:T(8,128)}, f32[2,1024,128]{2,1,0:T(8,1...) custom-call(f32[2,1024,384]{2,1,0:T(8,128)} %get-tuple-element.76.sig_r, f32[2,1024,640]{2,1,0:T(8,128)} %get-tuple-element.77.pre_r, ...), custom_call_target="tpu_custom_call" | custom-call | flops 80000000000 | bytes 40000000 | tf_op jit(solution)/shard_map/scan_backward/pallas_call | solution.py:745
  173.5 4.9 %all-to-all-start.3 = ((f32[4,1024,128]{2,1,0:T(8,128)}), f32[4,1024,128]{2,1,0:T(8,128)}, u32[]{:S(2)}, u32[]{:S(2)}) async-start(f32[4,1024,128]{2,1,0:T(8,128)} %bitcast.120), calls=%async_computation.3 | async-start | bytes 4194304 | tf_op jit(solution)/shard_map/sum_writer_reader_grad/all_to_all | solution.py:56
  182.0 5.2 %convolution_bitcast_fusion = f32[768,384]{1,0:T(8,128)} fusion(bf16[2,1024,768]{2,1,0:T(8,128)(2,1)} %get-tuple-element.74, bf16[2,1024,384]{2,1,0:T(8,128)(2,1)} %get-tuple-element.84), kind=kOutput, calls=%fused_computation.8 | convolution fusion | flops 1207959552 | bytes 5898240 | tf_op jit(solution)/shard_map/late_sums/dot_general | solution.py:791
  187.2 6.5 %normed_grad_gate.1.part = f32[2,256,768]{2,1,0:T(8,128)} custom-call(bf16[4,256,1536]{2,1,0:T(8,128)(2,1)} %copy-done, bf16[768,3584]{1,0:T(8,128)(2,1)} %all-gather.5.cloned.1.call-done.expand), custom_call_target="tpu_custom_call" | custom-call | flops 1200000000 | bytes 8000000 | tf_op jit(solution)/shard_map/normed_grad_gate/pallas_call | solution.py:782
  193.7 7.8 %mixed.1 = f32[2,256,768]{2,1,0:T(8,128)} custom-call(bf16[4,256,1536]{2,1,0:T(8,128)(2,1)} %copy-done, bf16[768,2688]{1,0:T(8,128)(2,1)} %all-gather.3.cloned.1.call-done.front, bf16[384,384]{1,0:T(8,128)(2,1)} %constant.165.clone.perm, f32[2,256,1]{2,1,0:T(8,128)} %compare_convert_fusion.mask, f32[2,256,768]{2,1,0:T(8,128)} %bitcast.111), custom_call_target="tpu_custom_call" | custom-call | flops 1200000000 | bytes 8000000 | tf_op jit(solution)/shard_map/mixed/pallas_call | solution.py:774
  202.3 4.8 %writer_reader_grad.1 = (bf16[2048,128]{1,0:T(8,128)(2,1)}, bf16[4,256,256]{2,1,0:T(8,128)(2,1)}, f32[8,64]{1,0:T(8,128)}) custom-call(f32[4,1024,128]{2,1,0:T(8,128)} %all-to-all-done.3.got, f32[1024,128]{1,0:T(8,128)} %bitcast.126, f32[1024,128]{1,0:T(8,128)} %bitcast.127, f32[8,64]{1,0:T(8,128)} %pad.35.fw, f32[2048,128]{1,0:T(8,128)} %bitcast.123), custom_call_target="tpu_custom_call" | custom-call | flops 100000000 | bytes 6000000 | tf_op jit(solution)/shard_map/writer_reader_grad/pallas_call | solution.py:795
  212.1 6.3 %reduce-scatter.2.cloned.1.call-done = f32[1,48,384]{2,1,0:T(8,128)} async-done(((f32[32,48,384]{2,1,0:T(8,128)}), f32[1,48,384]{2,1,0:T(8,128)}) %reduce-scatter.2.cloned.1.call-update) | async-done | bytes 73744 | tf_op jit(solution)/shard_map/early_sums/reduce_scatter | solution.py:738
  223.1 4.4 %all-to-all-start.4 = ((bf16[4,256,1024]{2,1,0:T(8,128)(2,1)}), bf16[4,256,1024]{2,1,0:T(8,128)(2,1)S(1)}, u32[]{:S(2)}, u32[]{:S(2)}) async-start(bf16[4,256,1024]{2,1,0:T(8,128)(2,1)} %pad_maximum_fusion), calls=%async_computation.5 | async-start | bytes 4194304 | tf_op jit(solution)/shard_map/send_values/all_to_all | solution.py:56
  235.2 3.9 %collective-permute-done.10 = f32[4,24,512]{2,1,0:T(8,128)S(1)} collective-permute-done((f32[4,24,512]{2,1,0:T(8,128)S(1)}, f32[4,24,512]{2,1,0:T(8,128)S(1)}, u32[]{:S(2)}, u32[]{:S(2)}) %collective-permute-start.10) | collective-permute-done | bytes 196640 | tf_op jit(solution)/shard_map/late_sums/ppermute | solution.py:42
  239.1 3.3 %collective-permute-done.11 = f32[4,24,512]{2,1,0:T(8,128)S(1)} collective-permute-done((f32[4,24,512]{2,1,0:T(8,128)S(1)}, f32[4,24,512]{2,1,0:T(8,128)S(1)}, u32[]{:S(2)}, u32[]{:S(2)}) %collective-permute-start.11) | collective-permute-done | bytes 196640 | tf_op jit(solution)/shard_map/late_sums/ppermute | solution.py:42
  255.9 7.9 %residual_grad.1 = (f32[2,256,768]{2,1,0:T(8,128)}, f32[8,768]{1,0:T(8,128)}) custom-call(f32[2,256,768]{2,1,0:T(8,128)} %normed_grad_gate.1.part, bf16[4,256,1024]{2,1,0:T(8,128)(2,1)} %copy-done.4, bf16[768,3584]{1,0:T(8,128)(2,1)} %all-gather.5.cloned.1.call-done.expand, f32[2,256,768]{2,1,0:T(8,128)} %bitcast.112, f32[2,256,768]{2,1,0:T(8,128)} %bitcast.117, ...), custom_call_target="tpu_custom_call" | custom-call | flops 2000000000 | bytes 15000000 | tf_op jit(solution)/shard_map/residual_grad/pallas_call | solution.py:860
  265.2 5.5 %all-to-all-start.5 = ((f32[32,1,128]{2,1,0:T(1,128)}), f32[32,1,128]{2,1,0:T(1,128)S(1)}, u32[]{:S(2)}, u32[]{:S(2)}) async-start(f32[32,1,128]{2,1,0:T(1,128)} %bitcast.39), calls=%async_computation.6 | async-start | bytes 32768 | tf_op jit(solution)/shard_map/sum_norm_grad/all_to_all | solution.py:871
  270.8 7.2 %all-to-all-done.5 = f32[32,1,128]{2,1,0:T(1,128)S(1)} async-done(((f32[32,1,128]{2,1,0:T(1,128)}), f32[32,1,128]{2,1,0:T(1,128)S(1)}, u32[]{:S(2)}, u32[]{:S(2)}) %all-to-all-start.5) | async-done | bytes 16416 | tf_op jit(solution)/shard_map/sum_norm_grad/all_to_all | solution.py:871
  278.1 12.0 %all_to_all.36 = f32[4,248,128]{2,1,0:T(8,128)S(1)} all-to-all(f32[4,248,128]{2,1,0:T(8,128)S(1)} %broadcast_in_dim.65), channel_id=1, replica_groups=mesh['dp'=32,'rep'=4] {'rep'}, dimensions={0} | all-to-all | bytes 1015808 | tf_op jit(solution)/shard_map/last_gather/all_to_all | solution.py:56
  (232 shorter events, 69.2 us)
Async XLA Ops:
  7.3 63.8 %all-gather.3.cloned.1.call-start = ((), (), s32[]{:S(2)}) async-start(), calls=%async_computation.8 | async-start | bytes 4257792 | tf_op jit(solution)/shard_map/gather_own_expand/all_gather | solution.py:613
  11.1 21.8 %collective-permute-start = (bf16[2,256,768]{2,1,0:T(8,128)(2,1)S(1)}, bf16[2,256,768]{2,1,0:T(8,128)(2,1)}, u32[]{:S(2)}, u32[]{:S(2)}) collective-permute-start(bf16[2,256,768]{2,1,0:T(8,128)(2,1)S(1)} %multiply_convert_fusion.1.b0), channel_id=1, source_target_pairs={{0,1},{1,2},{2,3},{3,0},{4,5},{5,6},{6,7},{7,4},{8,9},{9,10},{10,1... | collective-permute-start | bytes 2359304 | tf_op jit(solution)/shard_map/gather_branch_grad/ppermute | solution.py:36
  13.1 19.8 %collective-permute-start.1 = (bf16[2,256,768]{2,1,0:T(8,128)(2,1)S(1)}, bf16[2,256,768]{2,1,0:T(8,128)(2,1)}, u32[]{:S(2)}, u32[]{:S(2)}) collective-permute-start(bf16[2,256,768]{2,1,0:T(8,128)(2,1)S(1)} %multiply_convert_fusion.1.b0), channel_id=1, source_target_pairs={{0,3},{1,0},{2,1},{3,2},{4,7},{5,4},{6,5},{7,6},{8,11},{9,8},{10,9... | collective-permute-start | bytes 2359304 | tf_op jit(solution)/shard_map/gather_branch_grad/ppermute | solution.py:36
  16.0 14.7 %all-to-all-start = ((bf16[32,3,128]{2,1,0:T(4,128)(2,1)}), bf16[32,3,128]{2,1,0:T(4,128)(2,1)S(1)}, u32[]{:S(2)}, u32[]{:S(2)}) async-start(bf16[32,3,128]{2,1,0:T(4,128)(2,1)} %broadcast_in_dim.52), calls=%async_computation | async-start | bytes 65536 | tf_op jit(solution)/shard_map/gather_small/all_to_all | solution.py:625
  23.3 92.4 %all-gather.5.cloned.1.call-start = ((), (), s32[]{:S(2)}) async-start(), calls=%async_computation.9 | async-start | bytes 5677056 | tf_op jit(solution)/shard_map/gather_expand/all_gather | solution.py:651
  34.1 21.8 %collective-permute-start.3 = (bf16[2,256,768]{2,1,0:T(8,128)(2,1)S(1)}, bf16[2,256,768]{2,1,0:T(8,128)(2,1)S(1)}, u32[]{:S(2)}, u32[]{:S(2)}) collective-permute-start(bf16[2,256,768]{2,1,0:T(8,128)(2,1)S(1)} %multiply_convert_fusion.n0), channel_id=1, source_target_pairs={{0,1},{1,2},{2,3},{3,0},{4,5},{5,6},{6,7},{7,4},{8,9},{9,10},{10,1... | collective-permute-start | bytes 2359304 | tf_op jit(solution)/shard_map/gather_normed/ppermute | solution.py:36
  35.5 20.6 %collective-permute-start.2 = (bf16[2,256,768]{2,1,0:T(8,128)(2,1)S(1)}, bf16[2,256,768]{2,1,0:T(8,128)(2,1)}, u32[]{:S(2)}, u32[]{:S(2)}) collective-permute-start(bf16[2,256,768]{2,1,0:T(8,128)(2,1)S(1)} %multiply_convert_fusion.n0), channel_id=1, source_target_pairs={{0,3},{1,0},{2,1},{3,2},{4,7},{5,4},{6,5},{7,6},{8,11},{9,8},{10,9... | collective-permute-start | bytes 2359304 | tf_op jit(solution)/shard_map/gather_normed/ppermute | solution.py:36
  40.7 23.7 %collective-permute-start.6 = (bf16[1,256,768]{2,1,0:T(8,128)(2,1)S(1)}, bf16[1,256,768]{2,1,0:T(8,128)(2,1)S(1)}, u32[]{:S(2)}, u32[]{:S(2)}) collective-permute-start(bf16[1,256,768]{2,1,0:T(8,128)(2,1)S(1)} %slice.195), channel_id=1, source_target_pairs={{0,1},{1,2},{2,3},{3,0},{4,5},{5,6},{6,7},{7,4},{8,9},{9,10},{10,1... | collective-permute-start | bytes 1179656 | tf_op jit(solution)/shard_map/gather_branch_grad/ppermute | solution.py:36
  41.8 22.6 %collective-permute-start.7 = (bf16[1,256,768]{2,1,0:T(8,128)(2,1)S(1)}, bf16[1,256,768]{2,1,0:T(8,128)(2,1)S(1)}, u32[]{:S(2)}, u32[]{:S(2)}) collective-permute-start(bf16[1,256,768]{2,1,0:T(8,128)(2,1)S(1)} %slice.196), channel_id=1, source_target_pairs={{0,3},{1,0},{2,1},{3,2},{4,7},{5,4},{6,5},{7,6},{8,11},{9,8},{10,9... | collective-permute-start | bytes 1179656 | tf_op jit(solution)/shard_map/gather_branch_grad/ppermute | solution.py:36
  55.9 15.1 %collective-permute-start.4 = (bf16[1,256,768]{2,1,0:T(8,128)(2,1)S(1)}, bf16[1,256,768]{2,1,0:T(8,128)(2,1)S(1)}, u32[]{:S(2)}, u32[]{:S(2)}) collective-permute-start(bf16[1,256,768]{2,1,0:T(8,128)(2,1)S(1)} %slice.249), channel_id=1, source_target_pairs={{0,1},{1,2},{2,3},{3,0},{4,5},{5,6},{6,7},{7,4},{8,9},{9,10},{10,1... | collective-permute-start | bytes 1179656 | tf_op jit(solution)/shard_map/gather_normed/ppermute | solution.py:36
  57.2 13.8 %collective-permute-start.5 = (bf16[1,256,768]{2,1,0:T(8,128)(2,1)S(1)}, bf16[1,256,768]{2,1,0:T(8,128)(2,1)S(1)}, u32[]{:S(2)}, u32[]{:S(2)}) collective-permute-start(bf16[1,256,768]{2,1,0:T(8,128)(2,1)S(1)} %slice.250), channel_id=1, source_target_pairs={{0,3},{1,0},{2,1},{3,2},{4,7},{5,4},{6,5},{7,6},{8,11},{9,8},{10,9... | collective-permute-start | bytes 1179656 | tf_op jit(solution)/shard_map/gather_normed/ppermute | solution.py:36
  129.2 42.6 %all-to-all-start.2 = ((bf16[4,256,1536]{2,1,0:T(8,128)(2,1)}), bf16[4,256,1536]{2,1,0:T(8,128)(2,1)S(1)}, u32[]{:S(2)}, u32[]{:S(2)}) async-start(bf16[4,256,1536]{2,1,0:T(8,128)(2,1)} %get-tuple-element.75), calls=%async_computation.2 | async-start | bytes 6291456 | tf_op jit(solution)/shard_map/send_gate_parts/all_to_all | solution.py:56
  132.9 85.4 %reduce-scatter.2.cloned.1.call-start = ((), (), s32[]{:S(2)}) async-start(), calls=%async_computation.10 | async-start | bytes 2433024 | tf_op jit(solution)/shard_map/early_sums/reduce_scatter | solution.py:738
  173.5 28.8 %all-to-all-start.3 = ((f32[4,1024,128]{2,1,0:T(8,128)}), f32[4,1024,128]{2,1,0:T(8,128)}, u32[]{:S(2)}, u32[]{:S(2)}) async-start(f32[4,1024,128]{2,1,0:T(8,128)} %bitcast.120), calls=%async_computation.3 | async-start | bytes 4194304 | tf_op jit(solution)/shard_map/sum_writer_reader_grad/all_to_all | solution.py:56
  221.5 6.1 %collective-permute-start.8 = (f32[4,4,24,512]{3,2,1,0:T(8,128)}, f32[4,4,24,512]{3,2,1,0:T(8,128)}, u32[]{:S(2)}, u32[]{:S(2)}) collective-permute-start(f32[4,4,24,512]{3,2,1,0:T(8,128)} %fusion.1), channel_id=1, source_target_pairs={{0,4},{4,0},{8,12},{12,8},{16,20},{20,16},{24,28},{28,24},{32,36},... | collective-permute-start | bytes 2359304 | tf_op jit(solution)/shard_map/late_sums/ppermute | solution.py:42
  223.1 31.4 %all-to-all-start.4 = ((bf16[4,256,1024]{2,1,0:T(8,128)(2,1)}), bf16[4,256,1024]{2,1,0:T(8,128)(2,1)S(1)}, u32[]{:S(2)}, u32[]{:S(2)}) async-start(bf16[4,256,1024]{2,1,0:T(8,128)(2,1)} %pad_maximum_fusion), calls=%async_computation.5 | async-start | bytes 4194304 | tf_op jit(solution)/shard_map/send_values/all_to_all | solution.py:56
  229.8 9.3 %collective-permute-start.10 = (f32[4,24,512]{2,1,0:T(8,128)S(1)}, f32[4,24,512]{2,1,0:T(8,128)S(1)}, u32[]{:S(2)}, u32[]{:S(2)}) collective-permute-start(f32[4,24,512]{2,1,0:T(8,128)S(1)} %get-tuple-element.164), channel_id=1, source_target_pairs={{0,16},{4,20},{8,24},{12,28},{16,0},{20,4},{24,8},{28,12},{32,48},... | collective-permute-start | bytes 589832 | tf_op jit(solution)/shard_map/late_sums/ppermute | solution.py:42
  232.5 9.9 %collective-permute-start.11 = (f32[4,24,512]{2,1,0:T(8,128)S(1)}, f32[4,24,512]{2,1,0:T(8,128)S(1)}, u32[]{:S(2)}, u32[]{:S(2)}) collective-permute-start(f32[4,24,512]{2,1,0:T(8,128)S(1)} %get-tuple-element.163), channel_id=1, source_target_pairs={{0,24},{4,28},{8,0},{12,4},{16,8},{20,12},{24,16},{28,20},{32,56},... | collective-permute-start | bytes 589832 | tf_op jit(solution)/shard_map/late_sums/ppermute | solution.py:42
  233.7 8.9 %collective-permute-start.9 = (f32[4,24,512]{2,1,0:T(8,128)S(1)}, f32[4,24,512]{2,1,0:T(8,128)S(1)}, u32[]{:S(2)}, u32[]{:S(2)}) collective-permute-start(f32[4,24,512]{2,1,0:T(8,128)S(1)} %get-tuple-element.162), channel_id=1, source_target_pairs={{0,8},{4,12},{8,16},{12,20},{16,24},{20,28},{24,0},{28,4},{32,40},... | collective-permute-start | bytes 589832 | tf_op jit(solution)/shard_map/late_sums/ppermute | solution.py:42
  243.6 6.3 %collective-permute-start.12 = (f32[24,512]{1,0:T(8,128)S(1)}, f32[24,512]{1,0:T(8,128)S(1)}, u32[]{:S(2)}, u32[]{:S(2)}) collective-permute-start(f32[24,512]{1,0:T(8,128)S(1)} %get-tuple-element.183), channel_id=1, source_target_pairs={{0,32},{4,36},{8,40},{12,44},{16,48},{20,52},{24,56},{28,60},{32,6... | collective-permute-start | bytes 147464 | tf_op jit(solution)/shard_map/late_sums/ppermute | solution.py:42
  244.9 5.6 %collective-permute-start.13 = (f32[24,512]{1,0:T(8,128)S(1)}, f32[24,512]{1,0:T(8,128)S(1)}, u32[]{:S(2)}, u32[]{:S(2)}) collective-permute-start(f32[24,512]{1,0:T(8,128)S(1)} %get-tuple-element.185), channel_id=1, source_target_pairs={{0,64},{4,68},{8,72},{12,76},{16,80},{20,84},{24,88},{28,92},{32,9... | collective-permute-start | bytes 147464 | tf_op jit(solution)/shard_map/late_sums/ppermute | solution.py:42
  247.6 4.1 %collective-permute-start.14 = (f32[24,512]{1,0:T(8,128)S(1)}, f32[24,512]{1,0:T(8,128)S(1)}, u32[]{:S(2)}, u32[]{:S(2)}) collective-permute-start(f32[24,512]{1,0:T(8,128)S(1)} %get-tuple-element.184), channel_id=1, source_target_pairs={{0,96},{4,100},{8,104},{12,108},{16,112},{20,116},{24,120},{28,124... | collective-permute-start | bytes 147464 | tf_op jit(solution)/shard_map/late_sums/ppermute | solution.py:42
  249.0 21.7 %collective-permute-start.15 = (f32[24,384]{1,0:T(8,128)S(1)}, f32[24,384]{1,0:T(8,128)S(1)}, u32[]{:S(2)}, u32[]{:S(2)}) collective-permute-start(f32[24,384]{1,0:T(8,128)S(1)} %get-tuple-element.189), channel_id=1, source_target_pairs={{0,0},{1,32},{2,64},{3,96},{4,4},{5,36},{6,68},{7,100},{8,8},{9,40... | collective-permute-start | bytes 110600 | tf_op jit(solution)/shard_map/last_gather/ppermute | solution.py:858
  265.2 12.8 %all-to-all-start.5 = ((f32[32,1,128]{2,1,0:T(1,128)}), f32[32,1,128]{2,1,0:T(1,128)S(1)}, u32[]{:S(2)}, u32[]{:S(2)}) async-start(f32[32,1,128]{2,1,0:T(1,128)} %bitcast.39), calls=%async_computation.6 | async-start | bytes 32768 | tf_op jit(solution)/shard_map/sum_norm_grad/all_to_all | solution.py:871
  (33 other events, 195.7 us)
Sparse Core Ops, SparseCore 0:
  10.9 48.3 all-gather.2
  61.5 47.1 all-gather.4
  137.3 80.9 reduce-scatter.1

commit v4 on v3

--- a/solution.py
+++ b/solution.py
@@ -256,10 +256,8 @@
         ones = jnp.ones((8, ch), BF16)
         s1 = dot2(ones, gated * gated, NT)
         s2 = dot2(ones, outcome * cp[1:2, :] * gated, NT)
-        row = lax.broadcasted_iota(jnp.int32, s1.shape, 0)
-        both_sums = jnp.where(row == 0, s1, jnp.where(row == 1, s2, 0.0))
         for r in range(reps):
-            sums_o[r, m] = both_sums
+            sums_o[r, 2 * m : 2 * m + 2, :] = jnp.concatenate([s1[0:1], s2[0:1]], axis=0)
         gate_o[m] = gate
         sig_o[m] = signal[:, :ch]
         pre_o[m] = pre
@@ -293,7 +291,8 @@
         early_o[...] = jnp.zeros_like(early_o)
         acc_o[...] = jnp.zeros_like(acc_o)
 
-    s = jnp.sum(sums[:, 0], axis=0)
+    s = jnp.sum(sums[...], axis=0)
+    s = jnp.where(pl.program_id(0) < sums.shape[0], s[0:2], s[2:4])
     scale_row = lax.rsqrt(s[0:1] * (1.0 / width) + EPS)
     mean_row = scale_row * s[1:2] * (1.0 / width)
 
@@ -693,12 +692,12 @@
             pairs_of(width), pairs_of(width),
             pairs_of(ch), pairs_of(ch), pairs_of(cw), pairs_of(ch), pairs_of(ch), pairs_of(128),
             pl.BlockSpec((micro, 1, ch, ns), lambda b: (0, b, 0, 0)),
-            pl.BlockSpec((reps, micro, 8, q), lambda b: (0, 0, 0, b)), aside, aside,
+            pl.BlockSpec((reps, 2 * micro, q), lambda b: (0, 0, b)), aside, aside,
         ],
         out_shape=[
             pairs(width, BF16), pairs(width, BF16),
             pairs(ch), pairs(ch), pairs(cw), pairs(ch), pairs(ch), pairs(128),
-            sds((micro, reps, ch, ns), F32), sds((reps, micro, 8, total), F32),
+            sds((micro, reps, ch, ns), F32), sds((reps, 2 * micro, total), F32),
             sds((micro, total // 2, 2 * wr), F32), sds((micro, total // 2, 2 * wr), F32),
         ],
         scratch_shapes=[
@@ -714,7 +713,7 @@
     with jax.named_scope("sum_norm_terms"):
         sums, expand_full = lax.optimization_barrier((ax.exchange(sums), expand_full))
 
-    strip = pl.BlockSpec((reps, 1, 8, q), lambda b: (0, b // reps, 0, b % reps))
+    strip = pl.BlockSpec((reps, 2 * micro, q), lambda b: (0, 0, b % reps))
     ys = ax.size["y"]
     wide = width // 2
     early_rows = rows + 2 * (contract.shape[0] // ys)

time: 307 us -> 307 us (level)
  no operation moved by 1% of the time
where the time goes in v4:
time: 307 us; the launch traced here: 301 us
  Pallas kernels  112 us (36%)
  waiting for transfers between devices  54.8 us (18%)
  starting transfers between devices  51.8 us (17%)
  local copies, waits for them, and re-layouts  24.8 us (8%)
  blocking collectives  21.8 us (7%)
  between operations  14.8 us (5%)
  other arithmetic  13 us (4%)
  matrix products  7.99 us (3%)
    pallas_call x1, Pallas kernels, body(): pl.pallas_call(functools.partial(backward_kernel, heads, reps), grid=(rep...  38.1 us
    pallas_call x1, Pallas kernels, body(): pl.pallas_call(functools.partial(forward_kernel, heads, reps), grid=(reps...  33 us
    all_to_all x2, blocking collectives, exchange(): return lax.all_to_all(v, 'rep', 0, 0, tiled=True)  21.8 us
    ppermute x8, waiting for transfers between devices, shift(): return lax.ppermute(v, 'rep', [(i, (i + by) % n) for i in range(n)])  20.9 us
    ppermute x8, starting transfers between devices, shift(): return lax.ppermute(v, 'rep', [(i, (i + by) % n) for i in range(n)])  14.6 us
    pallas_call x1, Pallas kernels, body(): pl.pallas_call(functools.partial(gate_kernel, inner, ys), grid=(micro * r...  13.6 us
    all_to_all x3, starting transfers between devices, exchange(): return lax.all_to_all(v, 'rep', 0, 0, tiled=True)  13.1 us
    ppermute x7, starting transfers between devices, shift(): return lax.ppermute(v, 'dp', route)  10.1 us
  transfers between devices with their start and end apart: 24, of which 14 were waited for; matrix products, arithmetic and copies ran while one was open for 10% of the time, Pallas kernels for 33%

profile of v4, /device:TPU:0, one launch (start us, length us, event | category | flops | bytes accessed | tf_op | source)
XLA Modules:
  0.0 300.8 jit_solution(7236040269228675362)
XLA Ops:
  16.0 7.3 %all-to-all-start = ((bf16[32,3,128]{2,1,0:T(4,128)(2,1)}), bf16[32,3,128]{2,1,0:T(4,128)(2,1)S(1)}, u32[]{:S(2)}, u32[]{:S(2)}) async-start(bf16[32,3,128]{2,1,0:T(4,128)(2,1)} %broadcast_in_dim.52), calls=%async_computation | async-start | bytes 65536 | tf_op jit(solution)/shard_map/gather_small/all_to_all | solution.py:624
  23.6 7.2 %all-to-all-done = bf16[32,3,128]{2,1,0:T(4,128)(2,1)S(1)} async-done(((bf16[32,3,128]{2,1,0:T(4,128)(2,1)}), bf16[32,3,128]{2,1,0:T(4,128)(2,1)S(1)}, u32[]{:S(2)}, u32[]{:S(2)}) %all-to-all-start) | async-done | bytes 24608 | tf_op jit(solution)/shard_map/gather_small/all_to_all | solution.py:624
  41.8 3.3 %collective-permute-start.7 = (bf16[1,256,768]{2,1,0:T(8,128)(2,1)S(1)}, bf16[1,256,768]{2,1,0:T(8,128)(2,1)S(1)}, u32[]{:S(2)}, u32[]{:S(2)}) collective-permute-start(bf16[1,256,768]{2,1,0:T(8,128)(2,1)S(1)} %slice.196), channel_id=1, source_target_pairs={{0,3},{1,0},{2,1},{3,2},{4,7},{5,4},{6,5},{7,6},{8,11},{9,8},{10,9... | collective-permute-start | bytes 1179656 | tf_op jit(solution)/shard_map/gather_branch_grad/ppermute | solution.py:36
  45.1 10.8 %collective-permute-done.3.n3 = bf16[2,256,768]{2,1,0:T(8,128)(2,1)S(1)} collective-permute-done((bf16[2,256,768]{2,1,0:T(8,128)(2,1)S(1)}, bf16[2,256,768]{2,1,0:T(8,128)(2,1)S(1)}, u32[]{:S(2)}, u32[]{:S(2)}) %collective-permute-start.3) | collective-permute-done | bytes 786464 | tf_op jit(solution)/shard_map/gather_normed/ppermute | solution.py:36
  57.2 3.6 %collective-permute-start.5 = (bf16[1,256,768]{2,1,0:T(8,128)(2,1)S(1)}, bf16[1,256,768]{2,1,0:T(8,128)(2,1)S(1)}, u32[]{:S(2)}, u32[]{:S(2)}) collective-permute-start(bf16[1,256,768]{2,1,0:T(8,128)(2,1)S(1)} %slice.250), channel_id=1, source_target_pairs={{0,3},{1,0},{2,1},{3,2},{4,7},{5,4},{6,5},{7,6},{8,11},{9,8},{10,9... | collective-permute-start | bytes 1179656 | tf_op jit(solution)/shard_map/gather_normed/ppermute | solution.py:36
  64.4 6.6 %collective-permute-done.4.n2a = bf16[1,256,768]{2,1,0:T(8,128)(2,1)S(1)} collective-permute-done((bf16[1,256,768]{2,1,0:T(8,128)(2,1)S(1)}, bf16[1,256,768]{2,1,0:T(8,128)(2,1)S(1)}, u32[]{:S(2)}, u32[]{:S(2)}) %collective-permute-start.4) | collective-permute-done | bytes 393248 | tf_op jit(solution)/shard_map/gather_normed/ppermute | solution.py:36
  71.9 33.0 %scan_forward.1 = (bf16[2,1024,768]{2,1,0:T(8,128)(2,1)}, bf16[2,1024,768]{2,1,0:T(8,128)(2,1)}, f32[2,1024,384]{2,1,0:T(8,128)}, f32[2,1024,384]{2,1,0:T(8,128)...) custom-call(s32[1]{0:T(128)} %bitcast.place, ...), custom_call_target="tpu_custom_call" | custom-call | flops 40000000000 | bytes 40000000 | tf_op jit(solution)/shard_map/scan_forward/pallas_call | solution.py:684
  104.9 9.8 %all_to_all.35.sums = f32[4,4,1024]{2,1,0:T(4,128)} all-to-all(f32[4,4,1024]{2,1,0:T(4,128)} %get-tuple-element.70), channel_id=1, replica_groups=mesh['dp'=32,'rep'=4] {'rep'}, dimensions={0} | all-to-all | bytes 131072 | tf_op jit(solution)/shard_map/sum_norm_terms/all_to_all | solution.py:56
  114.7 13.6 %gate_backward.1 = (bf16[4,256,1536]{2,1,0:T(8,128)(2,1)}, f32[32,48,384]{2,1,0:T(8,128)}, f32[2048,384]{1,0:T(8,128)}, f32[8,384]{1,0:T(8,128)}) custom-call(f32[2048,384]{1,0:T(8,128)} %bitcast.147, f32[2048,384]{1,0:T(8,128)} %bitcast.144, f32[2048,384]{1,0:T(8,128)} %bitcast.148, f32[4,4,1024]{2,1,0:T(4,128)} %all_to_all.35.sums, ...), custom_call_target="tpu_custom_call" | custom-call | flops 8000000000 | bytes 20000000 | tf_op jit(solution)/shard_map/gate_backward/pallas_call | solution.py:720
  128.3 3.7 %all-to-all-start.2 = ((bf16[4,256,1536]{2,1,0:T(8,128)(2,1)}), bf16[4,256,1536]{2,1,0:T(8,128)(2,1)S(1)}, u32[]{:S(2)}, u32[]{:S(2)}) async-start(bf16[4,256,1536]{2,1,0:T(8,128)(2,1)} %get-tuple-element.75), calls=%async_computation.2 | async-start | bytes 6291456 | tf_op jit(solution)/shard_map/send_gate_parts/all_to_all | solution.py:56
  132.7 38.1 %scan_backward.1 = (bf16[2,1024,384]{2,1,0:T(8,128)(2,1)}, bf16[4,256,768]{2,1,0:T(8,128)(2,1)}, f32[4,2,512,128]{3,2,1,0:T(8,128)}, f32[2,1024,128]{2,1,0:T(8,1...) custom-call(f32[2,1024,384]{2,1,0:T(8,128)} %get-tuple-element.76.sig_r, f32[2,1024,640]{2,1,0:T(8,128)} %get-tuple-element.77.pre_r, ...), custom_call_target="tpu_custom_call" | custom-call | flops 80000000000 | bytes 40000000 | tf_op jit(solution)/shard_map/scan_backward/pallas_call | solution.py:744
  172.6 4.9 %all-to-all-start.3 = ((f32[4,1024,128]{2,1,0:T(8,128)}), f32[4,1024,128]{2,1,0:T(8,128)}, u32[]{:S(2)}, u32[]{:S(2)}) async-start(f32[4,1024,128]{2,1,0:T(8,128)} %bitcast.120), calls=%async_computation.3 | async-start | bytes 4194304 | tf_op jit(solution)/shard_map/sum_writer_reader_grad/all_to_all | solution.py:56
  181.1 5.2 %convolution_bitcast_fusion = f32[768,384]{1,0:T(8,128)} fusion(bf16[2,1024,768]{2,1,0:T(8,128)(2,1)} %get-tuple-element.74, bf16[2,1024,384]{2,1,0:T(8,128)(2,1)} %get-tuple-element.84), kind=kOutput, calls=%fused_computation.8 | convolution fusion | flops 1207959552 | bytes 5898240 | tf_op jit(solution)/shard_map/late_sums/dot_general | solution.py:790
  186.3 6.5 %normed_grad_gate.1.part = f32[2,256,768]{2,1,0:T(8,128)} custom-call(bf16[4,256,1536]{2,1,0:T(8,128)(2,1)} %copy-done, bf16[768,3584]{1,0:T(8,128)(2,1)} %all-gather.5.cloned.1.call-done.expand), custom_call_target="tpu_custom_call" | custom-call | flops 1200000000 | bytes 8000000 | tf_op jit(solution)/shard_map/normed_grad_gate/pallas_call | solution.py:781
  192.8 7.8 %mixed.1 = f32[2,256,768]{2,1,0:T(8,128)} custom-call(bf16[4,256,1536]{2,1,0:T(8,128)(2,1)} %copy-done, bf16[768,2688]{1,0:T(8,128)(2,1)} %all-gather.3.cloned.1.call-done.front, bf16[384,384]{1,0:T(8,128)(2,1)} %constant.165.clone.perm, f32[2,256,1]{2,1,0:T(8,128)} %compare_convert_fusion.mask, f32[2,256,768]{2,1,0:T(8,128)} %bitcast.111), custom_call_target="tpu_custom_call" | custom-call | flops 1200000000 | bytes 8000000 | tf_op jit(solution)/shard_map/mixed/pallas_call | solution.py:773
  201.3 4.8 %writer_reader_grad.1 = (bf16[2048,128]{1,0:T(8,128)(2,1)}, bf16[4,256,256]{2,1,0:T(8,128)(2,1)}, f32[8,64]{1,0:T(8,128)}) custom-call(f32[4,1024,128]{2,1,0:T(8,128)} %all-to-all-done.3.got, f32[1024,128]{1,0:T(8,128)} %bitcast.126, f32[1024,128]{1,0:T(8,128)} %bitcast.127, f32[8,64]{1,0:T(8,128)} %pad.35.fw, f32[2048,128]{1,0:T(8,128)} %bitcast.123), custom_call_target="tpu_custom_call" | custom-call | flops 100000000 | bytes 6000000 | tf_op jit(solution)/shard_map/writer_reader_grad/pallas_call | solution.py:794
  211.0 6.4 %reduce-scatter.2.cloned.1.call-done = f32[1,48,384]{2,1,0:T(8,128)} async-done(((f32[32,48,384]{2,1,0:T(8,128)}), f32[1,48,384]{2,1,0:T(8,128)}) %reduce-scatter.2.cloned.1.call-update) | async-done | bytes 73744 | tf_op jit(solution)/shard_map/early_sums/reduce_scatter | solution.py:737
  222.2 4.4 %all-to-all-start.4 = ((bf16[4,256,1024]{2,1,0:T(8,128)(2,1)}), bf16[4,256,1024]{2,1,0:T(8,128)(2,1)S(1)}, u32[]{:S(2)}, u32[]{:S(2)}) async-start(bf16[4,256,1024]{2,1,0:T(8,128)(2,1)} %pad_maximum_fusion), calls=%async_computation.5 | async-start | bytes 4194304 | tf_op jit(solution)/shard_map/send_values/all_to_all | solution.py:56
  234.3 3.9 %collective-permute-done.10 = f32[4,24,512]{2,1,0:T(8,128)S(1)} collective-permute-done((f32[4,24,512]{2,1,0:T(8,128)S(1)}, f32[4,24,512]{2,1,0:T(8,128)S(1)}, u32[]{:S(2)}, u32[]{:S(2)}) %collective-permute-start.10) | collective-permute-done | bytes 196640 | tf_op jit(solution)/shard_map/late_sums/ppermute | solution.py:42
  238.2 3.3 %collective-permute-done.11 = f32[4,24,512]{2,1,0:T(8,128)S(1)} collective-permute-done((f32[4,24,512]{2,1,0:T(8,128)S(1)}, f32[4,24,512]{2,1,0:T(8,128)S(1)}, u32[]{:S(2)}, u32[]{:S(2)}) %collective-permute-start.11) | collective-permute-done | bytes 196640 | tf_op jit(solution)/shard_map/late_sums/ppermute | solution.py:42
  255.0 7.9 %residual_grad.1 = (f32[2,256,768]{2,1,0:T(8,128)}, f32[8,768]{1,0:T(8,128)}) custom-call(f32[2,256,768]{2,1,0:T(8,128)} %normed_grad_gate.1.part, bf16[4,256,1024]{2,1,0:T(8,128)(2,1)} %copy-done.4, bf16[768,3584]{1,0:T(8,128)(2,1)} %all-gather.5.cloned.1.call-done.expand, f32[2,256,768]{2,1,0:T(8,128)} %bitcast.112, f32[2,256,768]{2,1,0:T(8,128)} %bitcast.117, ...), custom_call_target="tpu_custom_call" | custom-call | flops 2000000000 | bytes 15000000 | tf_op jit(solution)/shard_map/residual_grad/pallas_call | solution.py:859
  264.3 5.5 %all-to-all-start.5 = ((f32[32,1,128]{2,1,0:T(1,128)}), f32[32,1,128]{2,1,0:T(1,128)S(1)}, u32[]{:S(2)}, u32[]{:S(2)}) async-start(f32[32,1,128]{2,1,0:T(1,128)} %bitcast.39), calls=%async_computation.6 | async-start | bytes 32768 | tf_op jit(solution)/shard_map/sum_norm_grad/all_to_all | solution.py:870
  269.9 7.2 %all-to-all-done.5 = f32[32,1,128]{2,1,0:T(1,128)S(1)} async-done(((f32[32,1,128]{2,1,0:T(1,128)}), f32[32,1,128]{2,1,0:T(1,128)S(1)}, u32[]{:S(2)}, u32[]{:S(2)}) %all-to-all-start.5) | async-done | bytes 16416 | tf_op jit(solution)/shard_map/sum_norm_grad/all_to_all | solution.py:870
  277.2 12.0 %all_to_all.36 = f32[4,248,128]{2,1,0:T(8,128)S(1)} all-to-all(f32[4,248,128]{2,1,0:T(8,128)S(1)} %broadcast_in_dim.65), channel_id=1, replica_groups=mesh['dp'=32,'rep'=4] {'rep'}, dimensions={0} | all-to-all | bytes 1015808 | tf_op jit(solution)/shard_map/last_gather/all_to_all | solution.py:56
  (232 shorter events, 69.1 us)
Async XLA Ops:
  7.3 63.8 %all-gather.3.cloned.1.call-start = ((), (), s32[]{:S(2)}) async-start(), calls=%async_computation.8 | async-start | bytes 4257792 | tf_op jit(solution)/shard_map/gather_own_expand/all_gather | solution.py:612
  11.1 21.8 %collective-permute-start = (bf16[2,256,768]{2,1,0:T(8,128)(2,1)S(1)}, bf16[2,256,768]{2,1,0:T(8,128)(2,1)}, u32[]{:S(2)}, u32[]{:S(2)}) collective-permute-start(bf16[2,256,768]{2,1,0:T(8,128)(2,1)S(1)} %multiply_convert_fusion.1.b0), channel_id=1, source_target_pairs={{0,1},{1,2},{2,3},{3,0},{4,5},{5,6},{6,7},{7,4},{8,9},{9,10},{10,1... | collective-permute-start | bytes 2359304 | tf_op jit(solution)/shard_map/gather_branch_grad/ppermute | solution.py:36
  13.1 19.8 %collective-permute-start.1 = (bf16[2,256,768]{2,1,0:T(8,128)(2,1)S(1)}, bf16[2,256,768]{2,1,0:T(8,128)(2,1)}, u32[]{:S(2)}, u32[]{:S(2)}) collective-permute-start(bf16[2,256,768]{2,1,0:T(8,128)(2,1)S(1)} %multiply_convert_fusion.1.b0), channel_id=1, source_target_pairs={{0,3},{1,0},{2,1},{3,2},{4,7},{5,4},{6,5},{7,6},{8,11},{9,8},{10,9... | collective-permute-start | bytes 2359304 | tf_op jit(solution)/shard_map/gather_branch_grad/ppermute | solution.py:36
  16.0 14.7 %all-to-all-start = ((bf16[32,3,128]{2,1,0:T(4,128)(2,1)}), bf16[32,3,128]{2,1,0:T(4,128)(2,1)S(1)}, u32[]{:S(2)}, u32[]{:S(2)}) async-start(bf16[32,3,128]{2,1,0:T(4,128)(2,1)} %broadcast_in_dim.52), calls=%async_computation | async-start | bytes 65536 | tf_op jit(solution)/shard_map/gather_small/all_to_all | solution.py:624
  23.3 91.4 %all-gather.5.cloned.1.call-start = ((), (), s32[]{:S(2)}) async-start(), calls=%async_computation.9 | async-start | bytes 5677056 | tf_op jit(solution)/shard_map/gather_expand/all_gather | solution.py:650
  34.1 21.8 %collective-permute-start.3 = (bf16[2,256,768]{2,1,0:T(8,128)(2,1)S(1)}, bf16[2,256,768]{2,1,0:T(8,128)(2,1)S(1)}, u32[]{:S(2)}, u32[]{:S(2)}) collective-permute-start(bf16[2,256,768]{2,1,0:T(8,128)(2,1)S(1)} %multiply_convert_fusion.n0), channel_id=1, source_target_pairs={{0,1},{1,2},{2,3},{3,0},{4,5},{5,6},{6,7},{7,4},{8,9},{9,10},{10,1... | collective-permute-start | bytes 2359304 | tf_op jit(solution)/shard_map/gather_normed/ppermute | solution.py:36
  35.5 20.6 %collective-permute-start.2 = (bf16[2,256,768]{2,1,0:T(8,128)(2,1)S(1)}, bf16[2,256,768]{2,1,0:T(8,128)(2,1)}, u32[]{:S(2)}, u32[]{:S(2)}) collective-permute-start(bf16[2,256,768]{2,1,0:T(8,128)(2,1)S(1)} %multiply_convert_fusion.n0), channel_id=1, source_target_pairs={{0,3},{1,0},{2,1},{3,2},{4,7},{5,4},{6,5},{7,6},{8,11},{9,8},{10,9... | collective-permute-start | bytes 2359304 | tf_op jit(solution)/shard_map/gather_normed/ppermute | solution.py:36
  40.7 23.7 %collective-permute-start.6 = (bf16[1,256,768]{2,1,0:T(8,128)(2,1)S(1)}, bf16[1,256,768]{2,1,0:T(8,128)(2,1)S(1)}, u32[]{:S(2)}, u32[]{:S(2)}) collective-permute-start(bf16[1,256,768]{2,1,0:T(8,128)(2,1)S(1)} %slice.195), channel_id=1, source_target_pairs={{0,1},{1,2},{2,3},{3,0},{4,5},{5,6},{6,7},{7,4},{8,9},{9,10},{10,1... | collective-permute-start | bytes 1179656 | tf_op jit(solution)/shard_map/gather_branch_grad/ppermute | solution.py:36
  41.8 22.6 %collective-permute-start.7 = (bf16[1,256,768]{2,1,0:T(8,128)(2,1)S(1)}, bf16[1,256,768]{2,1,0:T(8,128)(2,1)S(1)}, u32[]{:S(2)}, u32[]{:S(2)}) collective-permute-start(bf16[1,256,768]{2,1,0:T(8,128)(2,1)S(1)} %slice.196), channel_id=1, source_target_pairs={{0,3},{1,0},{2,1},{3,2},{4,7},{5,4},{6,5},{7,6},{8,11},{9,8},{10,9... | collective-permute-start | bytes 1179656 | tf_op jit(solution)/shard_map/gather_branch_grad/ppermute | solution.py:36
  55.9 15.1 %collective-permute-start.4 = (bf16[1,256,768]{2,1,0:T(8,128)(2,1)S(1)}, bf16[1,256,768]{2,1,0:T(8,128)(2,1)S(1)}, u32[]{:S(2)}, u32[]{:S(2)}) collective-permute-start(bf16[1,256,768]{2,1,0:T(8,128)(2,1)S(1)} %slice.249), channel_id=1, source_target_pairs={{0,1},{1,2},{2,3},{3,0},{4,5},{5,6},{6,7},{7,4},{8,9},{9,10},{10,1... | collective-permute-start | bytes 1179656 | tf_op jit(solution)/shard_map/gather_normed/ppermute | solution.py:36
  57.2 13.8 %collective-permute-start.5 = (bf16[1,256,768]{2,1,0:T(8,128)(2,1)S(1)}, bf16[1,256,768]{2,1,0:T(8,128)(2,1)S(1)}, u32[]{:S(2)}, u32[]{:S(2)}) collective-permute-start(bf16[1,256,768]{2,1,0:T(8,128)(2,1)S(1)} %slice.250), channel_id=1, source_target_pairs={{0,3},{1,0},{2,1},{3,2},{4,7},{5,4},{6,5},{7,6},{8,11},{9,8},{10,9... | collective-permute-start | bytes 1179656 | tf_op jit(solution)/shard_map/gather_normed/ppermute | solution.py:36
  128.3 42.6 %all-to-all-start.2 = ((bf16[4,256,1536]{2,1,0:T(8,128)(2,1)}), bf16[4,256,1536]{2,1,0:T(8,128)(2,1)S(1)}, u32[]{:S(2)}, u32[]{:S(2)}) async-start(bf16[4,256,1536]{2,1,0:T(8,128)(2,1)} %get-tuple-element.75), calls=%async_computation.2 | async-start | bytes 6291456 | tf_op jit(solution)/shard_map/send_gate_parts/all_to_all | solution.py:56
  132.0 85.4 %reduce-scatter.2.cloned.1.call-start = ((), (), s32[]{:S(2)}) async-start(), calls=%async_computation.10 | async-start | bytes 2433024 | tf_op jit(solution)/shard_map/early_sums/reduce_scatter | solution.py:737
  172.6 28.7 %all-to-all-start.3 = ((f32[4,1024,128]{2,1,0:T(8,128)}), f32[4,1024,128]{2,1,0:T(8,128)}, u32[]{:S(2)}, u32[]{:S(2)}) async-start(f32[4,1024,128]{2,1,0:T(8,128)} %bitcast.120), calls=%async_computation.3 | async-start | bytes 4194304 | tf_op jit(solution)/shard_map/sum_writer_reader_grad/all_to_all | solution.py:56
  220.6 6.1 %collective-permute-start.8 = (f32[4,4,24,512]{3,2,1,0:T(8,128)}, f32[4,4,24,512]{3,2,1,0:T(8,128)}, u32[]{:S(2)}, u32[]{:S(2)}) collective-permute-start(f32[4,4,24,512]{3,2,1,0:T(8,128)} %fusion.1), channel_id=1, source_target_pairs={{0,4},{4,0},{8,12},{12,8},{16,20},{20,16},{24,28},{28,24},{32,36},... | collective-permute-start | bytes 2359304 | tf_op jit(solution)/shard_map/late_sums/ppermute | solution.py:42
  222.2 31.4 %all-to-all-start.4 = ((bf16[4,256,1024]{2,1,0:T(8,128)(2,1)}), bf16[4,256,1024]{2,1,0:T(8,128)(2,1)S(1)}, u32[]{:S(2)}, u32[]{:S(2)}) async-start(bf16[4,256,1024]{2,1,0:T(8,128)(2,1)} %pad_maximum_fusion), calls=%async_computation.5 | async-start | bytes 4194304 | tf_op jit(solution)/shard_map/send_values/all_to_all | solution.py:56
  228.9 9.3 %collective-permute-start.10 = (f32[4,24,512]{2,1,0:T(8,128)S(1)}, f32[4,24,512]{2,1,0:T(8,128)S(1)}, u32[]{:S(2)}, u32[]{:S(2)}) collective-permute-start(f32[4,24,512]{2,1,0:T(8,128)S(1)} %get-tuple-element.164), channel_id=1, source_target_pairs={{0,16},{4,20},{8,24},{12,28},{16,0},{20,4},{24,8},{28,12},{32,48},... | collective-permute-start | bytes 589832 | tf_op jit(solution)/shard_map/late_sums/ppermute | solution.py:42
  231.6 9.9 %collective-permute-start.11 = (f32[4,24,512]{2,1,0:T(8,128)S(1)}, f32[4,24,512]{2,1,0:T(8,128)S(1)}, u32[]{:S(2)}, u32[]{:S(2)}) collective-permute-start(f32[4,24,512]{2,1,0:T(8,128)S(1)} %get-tuple-element.163), channel_id=1, source_target_pairs={{0,24},{4,28},{8,0},{12,4},{16,8},{20,12},{24,16},{28,20},{32,56},... | collective-permute-start | bytes 589832 | tf_op jit(solution)/shard_map/late_sums/ppermute | solution.py:42
  232.8 8.9 %collective-permute-start.9 = (f32[4,24,512]{2,1,0:T(8,128)S(1)}, f32[4,24,512]{2,1,0:T(8,128)S(1)}, u32[]{:S(2)}, u32[]{:S(2)}) collective-permute-start(f32[4,24,512]{2,1,0:T(8,128)S(1)} %get-tuple-element.162), channel_id=1, source_target_pairs={{0,8},{4,12},{8,16},{12,20},{16,24},{20,28},{24,0},{28,4},{32,40},... | collective-permute-start | bytes 589832 | tf_op jit(solution)/shard_map/late_sums/ppermute | solution.py:42
  242.7 6.3 %collective-permute-start.12 = (f32[24,512]{1,0:T(8,128)S(1)}, f32[24,512]{1,0:T(8,128)S(1)}, u32[]{:S(2)}, u32[]{:S(2)}) collective-permute-start(f32[24,512]{1,0:T(8,128)S(1)} %get-tuple-element.183), channel_id=1, source_target_pairs={{0,32},{4,36},{8,40},{12,44},{16,48},{20,52},{24,56},{28,60},{32,6... | collective-permute-start | bytes 147464 | tf_op jit(solution)/shard_map/late_sums/ppermute | solution.py:42
  244.0 5.6 %collective-permute-start.13 = (f32[24,512]{1,0:T(8,128)S(1)}, f32[24,512]{1,0:T(8,128)S(1)}, u32[]{:S(2)}, u32[]{:S(2)}) collective-permute-start(f32[24,512]{1,0:T(8,128)S(1)} %get-tuple-element.185), channel_id=1, source_target_pairs={{0,64},{4,68},{8,72},{12,76},{16,80},{20,84},{24,88},{28,92},{32,9... | collective-permute-start | bytes 147464 | tf_op jit(solution)/shard_map/late_sums/ppermute | solution.py:42
  246.6 4.1 %collective-permute-start.14 = (f32[24,512]{1,0:T(8,128)S(1)}, f32[24,512]{1,0:T(8,128)S(1)}, u32[]{:S(2)}, u32[]{:S(2)}) collective-permute-start(f32[24,512]{1,0:T(8,128)S(1)} %get-tuple-element.184), channel_id=1, source_target_pairs={{0,96},{4,100},{8,104},{12,108},{16,112},{20,116},{24,120},{28,124... | collective-permute-start | bytes 147464 | tf_op jit(solution)/shard_map/late_sums/ppermute | solution.py:42
  248.1 21.7 %collective-permute-start.15 = (f32[24,384]{1,0:T(8,128)S(1)}, f32[24,384]{1,0:T(8,128)S(1)}, u32[]{:S(2)}, u32[]{:S(2)}) collective-permute-start(f32[24,384]{1,0:T(8,128)S(1)} %get-tuple-element.189), channel_id=1, source_target_pairs={{0,0},{1,32},{2,64},{3,96},{4,4},{5,36},{6,68},{7,100},{8,8},{9,40... | collective-permute-start | bytes 110600 | tf_op jit(solution)/shard_map/last_gather/ppermute | solution.py:857
  264.3 12.7 %all-to-all-start.5 = ((f32[32,1,128]{2,1,0:T(1,128)}), f32[32,1,128]{2,1,0:T(1,128)S(1)}, u32[]{:S(2)}, u32[]{:S(2)}) async-start(f32[32,1,128]{2,1,0:T(1,128)} %bitcast.39), calls=%async_computation.6 | async-start | bytes 32768 | tf_op jit(solution)/shard_map/sum_norm_grad/all_to_all | solution.py:870
  (33 other events, 195.8 us)
Sparse Core Ops, SparseCore 0:
  10.9 48.3 all-gather.2
  62.1 47.1 all-gather.4
  136.4 80.9 reduce-scatter.1
